TPU v7x, 128 devices: a whole 4x4x4 slice. The times are simulated.
128 devices in a mesh: fsdp: 4 (over z), ctx: 16 (over x, y_lo, core), tp: 2 (over y_hi).
Axes of the slice: x: 4, y: 4 (y_hi: 2, y_lo: 2; y = y_hi * 2 + y_lo), z: 4, core: 2. Of those that a mesh axis runs over, the one named last changes fastest.
Arguments:
- tokens: bfloat16 [4, 2048, 2048], P('fsdp', 'ctx'), may hold values from -6 to 6
- segments: int32 [4, 2048], P('fsdp'), may hold values from 0 to 30, as said below
- w_qkv: bfloat16 [2048, 3, 2048], P('fsdp', None, 'tp'), may hold values from -0.125 to 0.125
- b_qkv: bfloat16 [3, 32, 64], P(None, 'tp', 'fsdp'), may hold values from -3 to 3
- w_out: bfloat16 [2048, 2048], P('tp', 'fsdp'), may hold values from -1 to 1
- w_gate_up: bfloat16 [2048, 2, 5632], P('fsdp', None, 'tp'), may hold values from -0.125 to 0.125
- w_down: bfloat16 [5632, 2048], P('tp', 'fsdp'), may hold values from -0.078125 to 0.078125
- norm_gains: bfloat16 [2, 2048], P(None, 'fsdp'), may hold values from 0.25 to 1.75
- norm_shifts: bfloat16 [2, 2048], P(None, 'fsdp'), may hold values from -3 to 3
- cotangent: bfloat16 [4, 2048, 2048], P('fsdp', 'ctx'), may hold values from -6 to 6
Outputs:
- layer_out: bfloat16 [4, 2048, 2048], P('fsdp', 'ctx')
- grad_tokens: float32 [4, 2048, 2048], P('fsdp', 'ctx')
- grad_qkv: float32 [2048, 3, 2048], P('fsdp', None, 'tp')
- grad_bias: float32 [3, 32, 64], P(None, 'tp', 'fsdp')
- grad_out: float32 [2048, 2048], P('tp', 'fsdp')
- grad_gate_up: float32 [2048, 2, 5632], P('fsdp', None, 'tp')
- grad_down: float32 [5632, 2048], P('tp', 'fsdp')
- grad_gains: float32 [2, 2048], P(None, 'fsdp')
- grad_shifts: float32 [2, 2048], P(None, 'fsdp')
Inputs may be any that keep to these rules, and one draw needn't show every extreme that they name: `segments`: segment numbers start at 0 in every sequence and rise by one at each new document, never falling; in every sequence one document covers all positions from 127 to 1920, and every sequence ends at the same largest segment number.
All inputs are finite; a program needn't handle non-finite values.
Results may differ from a plain program's by a relative error of at most 0.022.
Values may be sent and summed in bfloat16 or wider, within the bound.
A program may use at most 256 MiB of HBM per device.

v0:
```python
import jax
import jax.numpy as jnp
from jax import lax
from jax.sharding import PartitionSpec as P

ROT = 16


EPS = 1e-05
NEG = -1e30


def layer_norm(values, gain_row, shift_row):
    row_mean = jnp.mean(values, axis=-1, keepdims=True)
    centred = values - row_mean
    variance = jnp.mean(centred * centred, axis=-1, keepdims=True)
    rstd_rows = lax.rsqrt(variance + EPS)
    normed = centred * rstd_rows
    return (normed * gain_row + shift_row, normed, rstd_rows)


def norm_back(gradient, normed, rstd_rows, gain_row):
    shaped = gradient * gain_row
    centre_term = (
        shaped
        - jnp.mean(shaped, axis=-1, keepdims=True)
        - normed * jnp.mean(shaped * normed, axis=-1, keepdims=True)
    )
    return (centre_term * rstd_rows, jnp.sum(gradient * normed, axis=0), jnp.sum(gradient, axis=0))


def rotation_tables(length, rot_dims):
    half_rot = rot_dims // 2
    positions = jnp.arange(length).astype(jnp.float32)
    inverse = 10000.0 ** (-(jnp.arange(half_rot).astype(jnp.float32) * 2.0 / rot_dims))
    angles = positions[:, None] * inverse[None, :]
    return (jnp.cos(angles)[:, None, :], jnp.sin(angles)[:, None, :])


def rotate(values, cosine_table, sine_table):
    half_rot = cosine_table.shape[-1]
    front_half = values[..., :half_rot]
    back_half = values[..., half_rot : 2 * half_rot]
    return jnp.concatenate(
        [
            front_half * cosine_table - back_half * sine_table,
            back_half * cosine_table + front_half * sine_table,
            values[..., 2 * half_rot :],
        ],
        axis=-1,
    )


def rotate_back(gradient, cosine_table, sine_table):
    half_rot = cosine_table.shape[-1]
    front_half = gradient[..., :half_rot]
    back_half = gradient[..., half_rot : 2 * half_rot]
    return jnp.concatenate(
        [
            front_half * cosine_table + back_half * sine_table,
            back_half * cosine_table - front_half * sine_table,
            gradient[..., 2 * half_rot :],
        ],
        axis=-1,
    )


def block_mask(segment, offset, block_rows, length):
    rows_seg = lax.dynamic_slice_in_dim(segment, offset, block_rows, 0)
    places = offset + jnp.arange(block_rows)
    columns = jnp.arange(length)
    return (rows_seg[:, None] == segment[None, :]) & (columns[None, :] <= places[:, None])


def attend_forward(queries, key_rows, value_rows, segment, block_rows):
    length, head_dim = queries.shape
    factor = head_dim ** (-0.5)

    def one_block(offset):
        rows_q = lax.dynamic_slice_in_dim(queries, offset, block_rows, 0)
        scores = (
            jnp.einsum("qd,kd->qk", rows_q, key_rows, preferred_element_type=jnp.float32) * factor
        )
        masked = jnp.where(block_mask(segment, offset, block_rows, length), scores, NEG)
        row_top = jnp.max(masked, axis=-1, keepdims=True)
        exp_terms = jnp.exp(masked - row_top)
        exp_total = jnp.sum(exp_terms, axis=-1, keepdims=True)
        prob_low = (exp_terms / exp_total).astype(jnp.bfloat16)
        output = jnp.dot(prob_low, value_rows, preferred_element_type=jnp.float32)
        return (output.astype(jnp.bfloat16), (row_top + jnp.log(exp_total))[:, 0])

    offsets = jnp.arange(length // block_rows) * block_rows
    outputs, logsum = lax.map(one_block, offsets)
    return (outputs.reshape(length, head_dim), logsum.reshape(length))


def attend_backward(queries, key_rows, value_rows, segment, logsum, grad_rows, block_rows):
    length, head_dim = queries.shape
    factor = head_dim ** (-0.5)

    def one_block(carried, offset):
        grad_keys, grad_values = carried
        rows_q = lax.dynamic_slice_in_dim(queries, offset, block_rows, 0)
        rows_do = lax.dynamic_slice_in_dim(grad_rows, offset, block_rows, 0)
        rows_lse = lax.dynamic_slice_in_dim(logsum, offset, block_rows, 0)
        scores = (
            jnp.einsum("qd,kd->qk", rows_q, key_rows, preferred_element_type=jnp.float32) * factor
        )
        masked = jnp.where(block_mask(segment, offset, block_rows, length), scores, NEG)
        probs = jnp.exp(masked - rows_lse[:, None])
        prob_low = probs.astype(jnp.bfloat16)
        grad_probs = jnp.einsum(
            "qd,kd->qk", rows_do, value_rows, preferred_element_type=jnp.float32
        )
        centre_term = jnp.sum(probs * grad_probs, axis=-1, keepdims=True)
        grad_scores = (probs * (grad_probs - centre_term)).astype(jnp.bfloat16)
        grad_q = jnp.dot(grad_scores, key_rows, preferred_element_type=jnp.float32) * factor
        grad_keys = (
            grad_keys
            + jnp.einsum("qk,qd->kd", grad_scores, rows_q, preferred_element_type=jnp.float32)
            * factor
        )
        grad_values = grad_values + jnp.einsum(
            "qk,qd->kd", prob_low, rows_do, preferred_element_type=jnp.float32
        )
        return ((grad_keys, grad_values), grad_q)

    offsets = jnp.arange(length // block_rows) * block_rows
    empty = jnp.zeros((length, head_dim), jnp.float32)
    (grad_keys, grad_values), grad_q = lax.scan(one_block, (empty, empty), offsets)
    return (grad_q.reshape(length, head_dim), grad_keys, grad_values)


def to_items(values):
    seq_count, length, heads_here, head_dim = values.shape
    return values.transpose(0, 2, 1, 3).reshape(seq_count * heads_here, length, head_dim)


def from_items(values, seq_count):
    item_count, length, head_dim = values.shape
    return values.reshape(seq_count, item_count // seq_count, length, head_dim).transpose(
        0, 2, 1, 3
    )


def local(
    tokens, segments, w_qkv, b_qkv, w_out, w_gate_up, w_down, norm_gains, norm_shifts, cotangent
):
    seq_count, tok_ctx, model_width = tokens.shape
    row_count = seq_count * tok_ctx
    full_qkv, qkv_bias, full_out, full_gate_up, full_down, gain_rows, shift_rows = (
        lax.all_gather(w_qkv, "fsdp", axis=0, tiled=True),
        lax.all_gather(b_qkv, "fsdp", axis=2, tiled=True),
        lax.all_gather(w_out, "fsdp", axis=1, tiled=True),
        lax.all_gather(w_gate_up, "fsdp", axis=0, tiled=True),
        lax.all_gather(w_down, "fsdp", axis=1, tiled=True),
        lax.all_gather(norm_gains, "fsdp", axis=1, tiled=True),
        lax.all_gather(norm_shifts, "fsdp", axis=1, tiled=True),
    )
    local_width = full_qkv.shape[2]
    heads_local, head_dim = (qkv_bias.shape[1], qkv_bias.shape[2])
    hidden_units = full_gate_up.shape[2]
    length = segments.shape[1]
    heads_here = heads_local // lax.axis_size("ctx")
    block_rows = min(512, length)
    gains_wide = gain_rows.astype(jnp.float32)
    shifts_wide = shift_rows.astype(jnp.float32)
    qkv_matrix = full_qkv.reshape(model_width, 3 * local_width)
    gate_matrix = full_gate_up.reshape(model_width, 2 * hidden_units)
    flat_tokens = tokens.reshape(row_count, model_width).astype(jnp.float32)
    normed_a_out, normed_a, rstd_a = layer_norm(flat_tokens, gains_wide[0], shifts_wide[0])
    inputs_a = normed_a_out.astype(jnp.bfloat16)
    projected = jnp.dot(inputs_a, qkv_matrix, preferred_element_type=jnp.float32)
    projected = projected.reshape(seq_count, tok_ctx, 3, heads_local, head_dim) + qkv_bias.astype(
        jnp.float32
    )
    spread_qkv = lax.all_to_all(
        projected.astype(jnp.bfloat16), "ctx", split_axis=3, concat_axis=1, tiled=True
    )
    cosine_table, sine_table = rotation_tables(length, ROT)
    queries = rotate(spread_qkv[:, :, 0].astype(jnp.float32), cosine_table, sine_table).astype(
        jnp.bfloat16
    )
    key_rows = rotate(spread_qkv[:, :, 1].astype(jnp.float32), cosine_table, sine_table).astype(
        jnp.bfloat16
    )
    q_items = to_items(queries)
    k_items = to_items(key_rows)
    v_items = to_items(spread_qkv[:, :, 2])
    seg_items = jnp.repeat(segments, heads_here, axis=0)
    o_items, lse_items = lax.map(
        lambda quad: attend_forward(quad[0], quad[1], quad[2], quad[3], block_rows),
        (q_items, k_items, v_items, seg_items),
    )
    attended = lax.all_to_all(
        from_items(o_items, seq_count), "ctx", split_axis=1, concat_axis=2, tiled=True
    )
    flat_attended = attended.reshape(row_count, local_width)
    attn_part = jnp.dot(flat_attended, full_out, preferred_element_type=jnp.float32)
    middle = flat_tokens + lax.psum(attn_part, "tp")
    normed_b_out, normed_b, rstd_b = layer_norm(middle, gains_wide[1], shifts_wide[1])
    inputs_b = normed_b_out.astype(jnp.bfloat16)
    gate_up = jnp.dot(inputs_b, gate_matrix, preferred_element_type=jnp.float32).reshape(
        row_count, 2, hidden_units
    )
    gate_part = gate_up[:, 0]
    up_part = gate_up[:, 1]
    sigmoid_gate = jax.nn.sigmoid(gate_part)
    silu_gate = gate_part * sigmoid_gate
    activated = (silu_gate * up_part).astype(jnp.bfloat16)
    mlp_part = jnp.dot(activated, full_down, preferred_element_type=jnp.float32)
    layer_out = (middle + lax.psum(mlp_part.astype(jnp.bfloat16), "tp").astype(jnp.float32)).astype(
        jnp.bfloat16
    )
    grad_low = cotangent.reshape(row_count, model_width)
    grad_middle = grad_low.astype(jnp.float32)
    grad_down = jnp.einsum("rf,rd->fd", activated, grad_low, preferred_element_type=jnp.float32)
    grad_act = jnp.einsum("rd,fd->rf", grad_low, full_down, preferred_element_type=jnp.float32)
    grad_gate = grad_act * up_part * sigmoid_gate * (1.0 + gate_part * (1.0 - sigmoid_gate))
    grad_up = grad_act * silu_gate
    grad_gu = jnp.stack([grad_gate, grad_up], axis=1).astype(jnp.bfloat16)
    grad_gate_up = jnp.einsum("rd,rch->dch", inputs_b, grad_gu, preferred_element_type=jnp.float32)
    part_b = jnp.einsum(
        "rk,dk->rd",
        grad_gu.reshape(row_count, 2 * hidden_units),
        gate_matrix,
        preferred_element_type=jnp.float32,
    )
    grad_normed_b = lax.psum(part_b.astype(jnp.bfloat16), "tp").astype(jnp.float32)
    back_b, gain_b, shift_b = norm_back(grad_normed_b, normed_b, rstd_b, gains_wide[1])
    grad_middle = grad_middle + back_b
    grad_mid_low = grad_middle.astype(jnp.bfloat16)
    grad_out = jnp.einsum(
        "rk,rd->kd", flat_attended, grad_mid_low, preferred_element_type=jnp.float32
    )
    grad_attended = jnp.einsum(
        "rd,kd->rk", grad_mid_low, full_out, preferred_element_type=jnp.float32
    )
    grad_attended = grad_attended.astype(jnp.bfloat16).reshape(
        seq_count, tok_ctx, heads_local, head_dim
    )
    grad_spread = lax.all_to_all(grad_attended, "ctx", split_axis=2, concat_axis=1, tiled=True)
    gq_items, gk_items, gv_items = lax.map(
        lambda sextet: attend_backward(
            sextet[0], sextet[1], sextet[2], sextet[3], sextet[4], sextet[5], block_rows
        ),
        (q_items, k_items, v_items, seg_items, lse_items, to_items(grad_spread)),
    )
    grad_queries = rotate_back(from_items(gq_items, seq_count), cosine_table, sine_table)
    grad_keys = rotate_back(from_items(gk_items, seq_count), cosine_table, sine_table)
    grad_values = from_items(gv_items, seq_count)
    stacked = jnp.stack([grad_queries, grad_keys, grad_values], axis=2).astype(jnp.bfloat16)
    grad_proj = lax.all_to_all(stacked, "ctx", split_axis=1, concat_axis=3, tiled=True)
    flat_grad_proj = grad_proj.reshape(row_count, 3 * local_width)
    grad_bias = jnp.sum(flat_grad_proj.astype(jnp.float32), axis=0).reshape(
        3, heads_local, head_dim
    )
    grad_qkv = jnp.einsum(
        "rd,rk->dk", inputs_a, flat_grad_proj, preferred_element_type=jnp.float32
    ).reshape(model_width, 3, local_width)
    part_a = jnp.einsum("rk,dk->rd", flat_grad_proj, qkv_matrix, preferred_element_type=jnp.float32)
    grad_normed_a = lax.psum(part_a.astype(jnp.bfloat16), "tp").astype(jnp.float32)
    back_a, gain_a, shift_a = norm_back(grad_normed_a, normed_a, rstd_a, gains_wide[0])
    grad_input = (grad_middle + back_a).reshape(tokens.shape)
    grad_gains = jnp.stack([gain_a, gain_b], axis=0)
    grad_shifts = jnp.stack([shift_a, shift_b], axis=0)
    summed = (
        lax.psum_scatter(
            grad_qkv.astype(jnp.bfloat16), "fsdp", scatter_dimension=0, tiled=True
        ).astype(jnp.float32),
        lax.psum_scatter(
            grad_out.astype(jnp.bfloat16), "fsdp", scatter_dimension=1, tiled=True
        ).astype(jnp.float32),
        lax.psum_scatter(
            grad_gate_up.astype(jnp.bfloat16), "fsdp", scatter_dimension=0, tiled=True
        ).astype(jnp.float32),
        lax.psum_scatter(
            grad_down.astype(jnp.bfloat16), "fsdp", scatter_dimension=1, tiled=True
        ).astype(jnp.float32),
        lax.psum_scatter(
            grad_bias.astype(jnp.bfloat16), "fsdp", scatter_dimension=2, tiled=True
        ).astype(jnp.float32),
        lax.psum_scatter(
            grad_gains.astype(jnp.bfloat16), "fsdp", scatter_dimension=1, tiled=True
        ).astype(jnp.float32),
        lax.psum_scatter(
            grad_shifts.astype(jnp.bfloat16), "fsdp", scatter_dimension=1, tiled=True
        ).astype(jnp.float32),
    )
    reduced = (
        lax.psum(summed[0].astype(jnp.bfloat16), "ctx").astype(jnp.float32),
        lax.psum(summed[1].astype(jnp.bfloat16), "ctx").astype(jnp.float32),
        lax.psum(summed[2].astype(jnp.bfloat16), "ctx").astype(jnp.float32),
        lax.psum(summed[3].astype(jnp.bfloat16), "ctx").astype(jnp.float32),
        lax.psum(summed[4].astype(jnp.bfloat16), "ctx").astype(jnp.float32),
        lax.psum(summed[5].astype(jnp.bfloat16), "ctx").astype(jnp.float32),
        lax.psum(summed[6].astype(jnp.bfloat16), "ctx").astype(jnp.float32),
    )
    red_qkv, red_out, red_gate_up, red_down = (reduced[0], reduced[1], reduced[2], reduced[3])
    red_bias, red_gains, red_shifts = (reduced[4], reduced[5], reduced[6])
    return (
        layer_out.reshape(tokens.shape),
        grad_input,
        red_qkv,
        red_bias,
        red_out,
        red_gate_up,
        red_down,
        red_gains,
        red_shifts,
    )


def solution(mesh):
    return jax.shard_map(
        local,
        mesh=mesh,
        in_specs=(
            P("fsdp", "ctx", None),
            P("fsdp", None),
            P("fsdp", None, "tp"),
            P(None, "tp", "fsdp"),
            P("tp", "fsdp"),
            P("fsdp", None, "tp"),
            P("tp", "fsdp"),
            P(None, "fsdp"),
            P(None, "fsdp"),
            P("fsdp", "ctx", None),
        ),
        out_specs=(
            P("fsdp", "ctx", None),
            P("fsdp", "ctx", None),
            P("fsdp", None, "tp"),
            P(None, "tp", "fsdp"),
            P("tp", "fsdp"),
            P("fsdp", None, "tp"),
            P("tp", "fsdp"),
            P(None, "fsdp"),
            P(None, "fsdp"),
        ),
        check_vma=False,
    )
```

profile of v0, /device:TPU:1, one launch (start us, length us, event | category | flops | bytes accessed | tf_op | source)
XLA Modules:
  0.0 1710.7 jit_solution(12967401174846856097)
XLA Ops:
  7.3 4.7 copy.160
  12.1 11.3 all_gather.24
  23.5 8.1 all_gather.22
  31.6 9.1 all_gather.21
  41.3 92.7 %all-gather.5.cloned.1.call-done = bf16[2048,3,1024]{0,2,1:T(8,128)(2,1)} async-done(((bf16[512,3,1024]{0,2,1:T(8,128)(2,1)}), bf16[2048,3,1024]{0,2,1:T(8,128)(2,1)}) %all-gather.5.cloned.1.call-update) | async-done | bytes 12582928 | tf_op jit(solution)/shard_map/all_gather | solution.py:152
  134.0 8.1 fusion.40
  143.1 5.9 all-to-all-start
  150.4 11.3 all-to-all-done
  165.4 34.2 %while.47 = (s32[]{:T(128)}, bf16[4,512,64]{1,2,0:T(8,128)(2,1)S(1)}, f32[4,512]{1,0:T(4,128)S(1)}, s32[4]{0:T(128)S(1)}, s32[2048]{0:T(1024)S(1)}, /*index=5*/b...) while((s32[]{:T(128)}, ...), condition=%wide.region_5.6_spmd, body=%wide.region_2.5_spmd.sunk | while | flops 280002560 | bytes 13605047 | solution.py:93
  200.7 11.5 reduce.6
  212.6 11.1 all_to_all.63
  225.1 3.9 fusion.127
  229.1 5.9 copy.173
  235.8 40.3 %all-reduce.8.cloned.1.call-done = f32[128,2048]{1,0:T(8,128)} async-done(((f32[128,2048]{1,0:T(8,128)}), f32[128,2048]{1,0:T(8,128)}) %all-reduce.8.cloned.1.call-update) | async-done | bytes 1048592 | tf_op jit(solution)/shard_map/psum | solution.py:200
  277.8 205.9 %all-gather.9.cloned.1.call-done = bf16[2048,2,2816]{2,0,1:T(8,128)(2,1)} async-done(((bf16[512,2,2816]{2,0,1:T(8,128)(2,1)}), bf16[2048,2,2816]{2,0,1:T(8,128)(2,1)}) %all-gather.9.cloned.1.call-update) | async-done | bytes 23068688 | tf_op jit(solution)/shard_map/all_gather | solution.py:155
  483.6 29.4 %copy.174 = bf16[2048,2,2816]{0,2,1:T(8,128)(2,1)} copy(bf16[2048,2,2816]{2,0,1:T(8,128)(2,1)} %all-gather.9.cloned.1.call-done) | data formatting | bytes 46137344 | tf_op jit(solution)/shard_map/all_gather | solution.py:155
  513.0 14.0 fusion.21
  527.0 69.0 %all-gather.11.cloned.1.call-done = bf16[2816,2048]{1,0:T(8,128)(2,1)} async-done(((bf16[2816,512]{1,0:T(8,128)(2,1)}), bf16[2816,2048]{1,0:T(8,128)(2,1)}) %all-gather.11.cloned.1.call-update) | async-done | bytes 11534352 | tf_op jit(solution)/shard_map/all_gather | solution.py:156
  596.0 9.2 fusion.63
  605.2 13.3 fusion.23
  618.5 37.8 %all-reduce.10.cloned.1.call-done = bf16[128,2048]{1,0:T(8,128)(2,1)} async-done(((bf16[128,2048]{1,0:T(8,128)(2,1)}), bf16[128,2048]{1,0:T(8,128)(2,1)}) %all-reduce.10.cloned.1.call-update) | async-done | bytes 524304 | tf_op jit(solution)/shard_map/psum | solution.py:229
  663.0 5.3 all-to-all-start.2
  668.3 7.3 all-to-all-done.2
  676.5 87.3 %while.48 = (s32[]{:T(128)}, f32[2048,64]{0,1:T(8,128)}, f32[2048,64]{0,1:T(8,128)}, f32[4,512,64]{1,0,2:T(4,128)}, s32[4]{0:T(128)S(1)}, /*index=5*/s32[2048]{0...) while((s32[]{:T(128)}, f32[2048,64]{0,1:T(8,128)}, ...), condition=%wide.region_15.16_spmd.clone, body=%wide.region_13.15_spmd.clone.sunk | while | flops 684359680 | bytes 52850944 | solution.py:130
  681.7 3.0 multiply_reduce_fusion.3
  689.0 3.5 convolution_add_fusion.2
  694.4 3.6 dynamic_update_slice.32
  703.3 3.0 multiply_reduce_fusion.3
  708.3 2.4 fusion.179
  710.7 3.7 convolution_add_fusion.2
  716.3 3.6 dynamic_update_slice.32
  725.2 3.0 multiply_reduce_fusion.3
  730.2 2.4 fusion.179
  732.6 3.7 convolution_add_fusion.2
  738.3 3.6 dynamic_update_slice.32
  747.1 3.0 multiply_reduce_fusion.3
  752.1 2.4 fusion.179
  754.5 3.7 convolution_add_fusion.2
  760.2 3.6 dynamic_update_slice.32
  769.6 2.8 copy.183
  772.4 2.5 reshape.458
  774.9 4.4 all-to-all-start.3
  779.4 7.7 convolution_convert_fusion.5
  787.1 5.1 all-to-all-done.3
  792.2 2.9 reshape.459
  795.1 2.5 copy.196
  797.6 7.5 convolution_convert_fusion.4
  805.2 4.5 convolution_convert_fusion.3
  810.2 8.0 convolution_convert_fusion.1
  819.5 8.2 convolution_convert_fusion.2
  829.0 11.4 convolution_convert_fusion
  845.3 7.1 all-reduce.14.cloned.1.call-done
  857.5 44.5 %reduce-scatter.16.cloned.1.call-done = bf16[1024,512]{1,0:T(8,128)(2,1)} async-done(((bf16[1024,2048]{1,0:T(8,128)(2,1)}), bf16[1024,512]{1,0:T(8,128)(2,1)}) %reduce-scatter.16.cloned.1.call-update) | async-done | bytes 1048592 | tf_op jit(solution)/shard_map/reduce_scatter | solution.py:271
  902.0 108.9 %reduce-scatter.20.cloned.1.call-done = bf16[2816,512]{1,0:T(8,128)(2,1)} async-done(((bf16[2816,2048]{1,0:T(8,128)(2,1)}), bf16[2816,512]{1,0:T(8,128)(2,1)}) %reduce-scatter.20.cloned.1.call-update) | async-done | bytes 2883600 | tf_op jit(solution)/shard_map/reduce_scatter | solution.py:277
  1010.9 116.6 %reduce-scatter.14.cloned.1.call-done = bf16[512,3,1024]{2,0,1:T(8,128)(2,1)} async-done(((bf16[2048,3,1024]{2,0,1:T(8,128)(2,1)}), bf16[512,3,1024]{2,0,1:T(8,128)(2,1)}) %reduce-scatter.14.cloned.1.call-update) | async-done | bytes 3145744 | tf_op jit(solution)/shard_map/reduce_scatter | solution.py:268
  1127.5 201.0 %reduce-scatter.18.cloned.1.call-done = bf16[512,2,2816]{2,0,1:T(8,128)(2,1)} async-done(((bf16[2048,2,2816]{2,0,1:T(8,128)(2,1)}), bf16[512,2,2816]{2,0,1:T(8,128)(2,1)}) %reduce-scatter.18.cloned.1.call-update) | async-done | bytes 5767184 | tf_op jit(solution)/shard_map/reduce_scatter | solution.py:274
  1328.5 20.6 %reduce-scatter.22.cloned.1.call-done = bf16[16,48]{1,0:T(8,128)(2,1)} async-done(((bf16[64,48]{1,0:T(8,128)(2,1)}), bf16[16,48]{1,0:T(8,128)(2,1)}) %reduce-scatter.22.cloned.1.call-update) | async-done | bytes 1552
  1353.4 20.5 %reduce-scatter.24.cloned.1.call-done = bf16[512,2]{1,0:T(8,128)(2,1)} async-done(((bf16[2048,2]{1,0:T(8,128)(2,1)}), bf16[512,2]{1,0:T(8,128)(2,1)}) %reduce-scatter.24.cloned.1.call-update) | async-done | bytes 2064
  1374.9 23.0 %reduce-scatter.26.cloned.1.call-done = bf16[512,2]{1,0:T(8,128)(2,1)} async-done(((bf16[2048,2]{1,0:T(8,128)(2,1)}), bf16[512,2]{1,0:T(8,128)(2,1)}) %reduce-scatter.26.cloned.1.call-update) | async-done | bytes 2064
  1399.0 58.5 %all-reduce = (bf16[3,16,16]{2,1,0:T(8,128)(2,1)S(1)}, bf16[2,512]{1,0:T(2,128)(2,1)S(1)}, bf16[2,512]{1,0:T(2,128)(2,1)S(1)}) all-reduce(bf16[3,16,16]{2,1,0:T(8,128)(2,1)S(1)} %copy.200, bf16[2,512]{1,0:T(2,128)(2,1)S(1)} %copy.202, bf16[2,512]{1,0:T(2,128)(2,1)S(1)} %copy.204), channel_id=1, replica_groups=mesh['fsdp'=4,'ctx'=16,'tp'=2] {'ctx'}, use_global_device_ids=true, to_apply=%region_23.24 | all-reduce | flops 2816 | bytes 11264 | tf_op jit(solution)/shard_map/psum | solution.py:295
  1459.3 228.6 %all-reduce.12.cloned.1.call-done = (bf16[512,2,2816]{2,0,1:T(8,128)(2,1)}, bf16[512,3,1024]{2,0,1:T(8,128)(2,1)}, bf16[1024,512]{1,0:T(8,128)(2,1)}, bf16[2816,512]{1,0:T(8,128)(2,1)}) async-done(((bf16[512,2,2816]{2,0,1:T(8,128)(2,1)}, bf16[512,3,1024]{2,0,1:T(8,128)(2,1)}, bf16[1024,512]{1,0:T(8,128)(2,1)}, bf16[2816,512]{1,0:T(8,128)(2,1)}), (bf16[512,2,2816]{2,0,1:T(8,128)(2,1)}, ...) | async-done | bytes 12845072 | tf_op jit(solution)/shard_map/psum | solution.py:293
  1687.9 5.5 convert_element_type.283
  1695.0 5.7 copy.189
  1700.7 3.4 convert_element_type.292
  (258 shorter events, 105.5 us)
Async XLA Ops:
  7.2 4.8 copy-start.27
  7.2 16.3 copy-start.32
  7.2 24.4 %copy-start.33 = (bf16[2,512]{1,0:T(2,128)(2,1)S(1)}, bf16[2,512]{1,0:T(2,128)(2,1)}, u32[]{:S(2)}) copy-start(bf16[2,512]{1,0:T(2,128)(2,1)} %param.21) | copy-start | bytes 6148
  7.2 33.5 %copy-start.1 = (bf16[1,128,2048]{2,1,0:T(8,128)(2,1)S(1)}, bf16[1,128,2048]{2,1,0:T(8,128)(2,1)}, u32[]{:S(2)}) copy-start(bf16[1,128,2048]{2,1,0:T(8,128)(2,1)} %param.14) | copy-start | bytes 1572868
  7.2 126.8 %all-gather.5.cloned.1.call-start = ((), (), s32[]{:S(2)}) async-start(), calls=%async_computation.11 | async-start | bytes 15728640 | tf_op jit(solution)/shard_map/all_gather | solution.py:152
  40.9 101.2 %copy-start.25 = (f32[128]{0:T(128)}, f32[128]{0:T(128)S(1)}, u32[]{:S(2)}) copy-start(f32[128]{0:T(128)S(1)} %broadcast_multiply_fusion.5) | copy-start | bytes 1540
  41.2 100.9 %copy-start.28 = (f32[128]{0:T(128)}, f32[128]{0:T(128)S(1)}, u32[]{:S(2)}) copy-start(f32[128]{0:T(128)S(1)} %add_rsqrt_fusion.1) | copy-start | bytes 1540
  41.2 100.9 %copy-start.20 = (f32[1,2048]{1,0:T(1,128)}, f32[1,2048]{1,0:T(1,128)S(1)}, u32[]{:S(2)}) copy-start(f32[1,2048]{1,0:T(1,128)S(1)} %get-tuple-element.482) | copy-start | bytes 24580
  41.3 100.9 %copy-start.18 = (f32[1,2048]{1,0:T(1,128)}, f32[1,2048]{1,0:T(1,128)S(1)}, u32[]{:S(2)}) copy-start(f32[1,2048]{1,0:T(1,128)S(1)} %get-tuple-element.480) | copy-start | bytes 24580
  143.1 18.5 %all-to-all-start = ((bf16[1,128,3,16,64]{1,4,2,0,3:T(8,128)(2,1)}), bf16[1,128,3,16,64]{1,4,2,0,3:T(8,128)(2,1)S(1)}, u32[]{:S(2)}, u32[]{:S(2)}) async-start(bf16[1,128,3,16,64]{1,4,2,0,3:T(8,128)(2,1)} %copy.163), calls=%async_computation | async-start | bytes 1572864 | tf_op jit(solution)/shard_map/all_to_all | solution.py:177
  149.0 76.1 %all-gather.7.cloned.1.call-start = ((), (), s32[]{:S(2)}) async-start(), calls=%async_computation.12 | async-start | bytes 5242880 | tf_op jit(solution)/shard_map/all_gather | solution.py:154
  149.7 126.4 %all-reduce.8.cloned.1.call-start = ((), (), s32[]{:S(2)}) async-start(), calls=%async_computation.13 | async-start | bytes 2097152 | tf_op jit(solution)/shard_map/psum | solution.py:200
  150.3 14.1 copy-start.30
  150.3 14.1 copy-start.22
  161.8 3.6 copy-start.24
  229.0 254.6 %all-gather.9.cloned.1.call-start = ((), (), s32[]{:S(2)}) async-start(), calls=%async_computation.14 | async-start | bytes 28835840 | tf_op jit(solution)/shard_map/all_gather | solution.py:155
  234.9 361.1 %all-gather.11.cloned.1.call-start = ((), (), s32[]{:S(2)}) async-start(), calls=%async_computation.15 | async-start | bytes 14417920 | tf_op jit(solution)/shard_map/all_gather | solution.py:156
  235.5 420.8 %all-reduce.10.cloned.1.call-start = ((), (), s32[]{:S(2)}) async-start(), calls=%async_computation.16 | async-start | bytes 1048576 | tf_op jit(solution)/shard_map/psum | solution.py:229
  513.0 83.0 %copy-start.11 = (bf16[1,128,2048]{2,1,0:T(8,128)(2,1)S(1)}, bf16[1,128,2048]{2,1,0:T(8,128)(2,1)}, u32[]{:S(2)}) copy-start(bf16[1,128,2048]{2,1,0:T(8,128)(2,1)} %param.23) | copy-start | bytes 1572868
  605.2 13.3 copy-start.14
  605.2 13.3 copy-start.16
  656.3 4.3 copy-start.4
  659.6 1.0 copy-start.5
  663.0 12.6 all-to-all-start.2
  676.5 89.7 %copy-start.23 = (f32[2048]{0:T(1024)S(1)}, f32[2048]{0:T(1024)}, u32[]{:S(2)}) copy-start(f32[2048]{0:T(1024)} %copy-done.22) | copy-start | bytes 24580
  676.5 89.7 %copy-start.31 = (f32[8]{0:T(128)S(1)}, f32[8]{0:T(128)}, u32[]{:S(2)}) copy-start(f32[8]{0:T(128)} %copy-done.30) | copy-start | bytes 100
  684.7 2.0 copy-start
  706.3 2.0 copy-start
  728.2 2.0 copy-start
  750.1 2.0 copy-start
  774.9 17.3 %all-to-all-start.3 = ((bf16[16,2,12288]{2,1,0:T(2,128)(2,1)}), bf16[16,2,12288]{2,1,0:T(2,128)(2,1)}, u32[]{:S(2)}, u32[]{:S(2)}) async-start(bf16[16,2,12288]{2,1,0:T(2,128)(2,1)} %reshape.458), calls=%async_computation.3 | async-start | bytes 1572864 | tf_op jit(solution)/shard_map/all_to_all | solution.py:253
  779.3 73.0 %all-reduce.14.cloned.1.call-start = ((), (), s32[]{:S(2)}) async-start(), calls=%async_computation.25 | async-start | bytes 2097152 | tf_op jit(solution)/shard_map/psum | solution.py:212
  795.1 10.0 copy-start.3
  805.1 5.1 copy-start.12
  805.1 96.9 %reduce-scatter.16.cloned.1.call-start = ((), (), s32[]{:S(2)}) async-start(), calls=%async_computation.18 | async-start | bytes 5242880 | tf_op jit(solution)/shard_map/reduce_scatter | solution.py:271
  809.7 201.2 %reduce-scatter.20.cloned.1.call-start = ((), (), s32[]{:S(2)}) async-start(), calls=%async_computation.20 | async-start | bytes 14417920 | tf_op jit(solution)/shard_map/reduce_scatter | solution.py:277
  818.2 1.0 copy-start.2
  818.2 1.3 copy-start.7
  818.2 1.3 copy-start.19
  818.2 1.3 copy-start.21
  818.2 1.3 copy-start.26
  818.2 1.3 copy-start.29
  818.2 309.3 %reduce-scatter.14.cloned.1.call-start = ((), (), s32[]{:S(2)}) async-start(), calls=%async_computation.17 | async-start | bytes 15728640 | tf_op jit(solution)/shard_map/reduce_scatter | solution.py:268
  827.6 1.1 copy-start.15
  827.6 1.4 copy-start.17
  827.7 500.8 %reduce-scatter.18.cloned.1.call-start = ((), (), s32[]{:S(2)}) async-start(), calls=%async_computation.19 | async-start | bytes 28835840 | tf_op jit(solution)/shard_map/reduce_scatter | solution.py:274
  840.4 1.0 copy-start.8
  840.4 508.8 %reduce-scatter.22.cloned.1.call-start = ((), (), s32[]{:S(2)}) async-start(), calls=%async_computation.21 | async-start | bytes 20480
  845.2 528.7 %reduce-scatter.24.cloned.1.call-start = ((), (), s32[]{:S(2)}) async-start(), calls=%async_computation.22 | async-start | bytes 655360
  856.2 541.8 %reduce-scatter.26.cloned.1.call-start = ((), (), s32[]{:S(2)}) async-start(), calls=%async_computation.23 | async-start | bytes 655360
  857.3 830.6 %all-reduce.12.cloned.1.call-start = ((), (), s32[]{:S(2)}) async-start(), calls=%async_computation.24 | async-start | bytes 25690112 | tf_op jit(solution)/shard_map/psum | solution.py:293
  1328.5 23.5 %copy-start.6 = (f32[128,2048]{1,0:T(8,128)S(1)}, f32[128,2048]{1,0:T(8,128)}, u32[]{:S(2)}) copy-start(f32[128,2048]{1,0:T(8,128)} %copy-done.5) | copy-start | bytes 3145732
  1328.5 23.5 %copy-start.9 = (bf16[128,2048]{1,0:T(8,128)(2,1)S(1)}, bf16[128,2048]{1,0:T(8,128)(2,1)}, u32[]{:S(2)}) copy-start(bf16[128,2048]{1,0:T(8,128)(2,1)} %get-tuple-element.451) | copy-start | bytes 1572868
  1687.9 7.1 slice-start
  1687.9 5.5 copy-start.13
  1687.9 7.1 slice-start.1
  1695.0 5.7 copy-start.10
Sparse Core Ops, SparseCore 0:
  12.1 121.8 all-gather.4
  151.5 49.0 all-gather.6
  229.1 46.8 all-reduce.7
  278.3 205.2 all-gather.8
  485.2 110.7 all-gather.10
  618.6 37.6 all-reduce.9
  805.2 47.0 all-reduce.13
  855.5 46.4 reduce-scatter.15
  905.0 105.7 reduce-scatter.19
  1013.2 114.2 reduce-scatter.13
  1130.0 198.4 reduce-scatter.17
  1331.4 17.7 reduce-scatter.21
  1352.1 21.7 reduce-scatter.23
  1376.8 21.1 reduce-scatter.25
  1400.6 287.2 all-reduce.11
where the time goes:
time: 1720 us; the launch traced here: 1710 us
  waiting for transfers between devices  1240 us (72%)
  matrix products  166 us (10%)
  local copies, waits for them, and re-layouts  108 us (6%)
  blocking collectives  98.1 us (6%)
  other arithmetic  49.5 us (3%)
  starting transfers between devices  17.4 us (1%)
    psum x1, waiting for transfers between devices, local(): lax.psum(summed[2].astype(jnp.bfloat16), 'ctx').astype(jnp.float32)  229 us
    all_gather x1, waiting for transfers between devices, local(): lax.all_gather(w_gate_up, 'fsdp', axis=0, tiled=True)  206 us
    reduce_scatter x1, waiting for transfers between devices, local(): lax.psum_scatter(grad_gate_up.astype(jnp.bfloat16), 'fsdp', scatter_dimen...  201 us
    reduce_scatter x1, waiting for transfers between devices, local(): lax.psum_scatter(grad_qkv.astype(jnp.bfloat16), 'fsdp', scatter_dimension...  117 us
    reduce_scatter x1, waiting for transfers between devices, local(): lax.psum_scatter(grad_down.astype(jnp.bfloat16), 'fsdp', scatter_dimensio...  109 us
    all_gather x1, waiting for transfers between devices, local(): lax.all_gather(w_qkv, 'fsdp', axis=0, tiled=True)  92.7 us
    all_gather x1, waiting for transfers between devices, local(): lax.all_gather(w_down, 'fsdp', axis=1, tiled=True)  69 us
    unnamed x18, waiting for transfers between devices  65.6 us
  transfers between devices with their start and end apart: 18, of which 17 were waited for; matrix products, arithmetic and copies ran while one was open for 9% of the time, Pallas kernels for 0%

commit v1 on v0

v1 whole, which is shorter than its diff:
```python
import functools

import jax
import jax.numpy as jnp
from jax import lax
from jax.experimental import pallas as pl
from jax.experimental.pallas import tpu as pltpu
from jax.sharding import Mesh
from jax.sharding import PartitionSpec as P

EPS = 1e-05
NEG = -1e30
ROT = 16
HEAD = 64
SEQ = 2048
WIDTH = 2048
OWN = 64
ROWS = 512
QB = 256
F32 = jnp.float32
BF16 = jnp.bfloat16
MESH_ID = pl.DeviceIdType.MESH
ANY = pl.BlockSpec(memory_space=pl.ANY)
VMEM = pl.BlockSpec(memory_space=pltpu.VMEM)


def place():
    return tuple(lax.axis_index(a) for a in ("z", "x", "yl", "core", "yh"))


def lanes(index, size=128):
    return pl.ds(pl.multiple_of(index * size, size), size)


def rows_at(index, size):
    return pl.ds(pl.multiple_of(index * size, size), size)


def z_peer(d):
    z = lax.axis_index("z")
    return {"z": lax.rem(z + d, 4)}


def x_peer(d):
    x = lax.axis_index("x")
    return {"x": lax.rem(x + d, 4)}


def y_peer(d):
    y = lax.rem(lax.axis_index("yh") * 2 + lax.axis_index("yl") + d, 4)
    return {"yh": y // 2, "yl": lax.rem(y, 2)}


def xy_peer(dx, dy):
    return {**x_peer(dx), **y_peer(dy)}


def sibling():
    return {"core": 1 - lax.axis_index("core")}


Z_PEERS = [functools.partial(z_peer, d) for d in (1, 2, 3)]
X_PEERS = [functools.partial(x_peer, d) for d in (1, 2, 3)]
Y_PEERS = [functools.partial(y_peer, d) for d in (1, 2, 3)]
XY_ALL = [(dx, dy) for dx in range(4) for dy in range(4) if dx or dy]
XY_PEERS = [functools.partial(xy_peer, dx, dy) for dx, dy in XY_ALL]


class Engine:
    def __init__(self, send_sem, recv_sem, local_sem):
        self.sems = (send_sem, recv_sem, local_sem)
        self.remote = 0
        self.locals = 0

    def send(self, src, dst, device):
        i = self.remote
        self.remote += 1
        copy = pltpu.make_async_remote_copy(
            src, dst, self.sems[0].at[i], self.sems[1].at[i], device_id=device, device_id_type=MESH_ID
        )
        copy.start()
        return copy

    def local(self, src, dst):
        i = self.locals
        self.locals += 1
        copy = pltpu.make_async_copy(src, dst, self.sems[2].at[i])
        copy.start()
        return copy


class Op:
    def __init__(self, ins, outs, peers, body, scratch=()):
        self.ins, self.outs, self.peers, self.body, self.scratch = ins, outs, peers, body, scratch


def exchange(name, number, ops, n_remote, n_local):
    peers = []
    for op in ops:
        for peer in op.peers:
            if peer not in peers:
                peers.append(peer)

    def kernel(*refs):
        refs = list(refs)

        def take(count):
            taken = refs[:count]
            del refs[:count]
            return taken

        ins = [take(len(op.ins)) for op in ops]
        outs = [take(len(op.outs)) for op in ops]
        scratch = [take(len(op.scratch)) for op in ops]
        engine = Engine(*refs)
        barrier = pltpu.get_barrier_semaphore()
        for peer in peers:
            pl.semaphore_signal(barrier, 1, device_id=peer(), device_id_type=MESH_ID)
        pl.semaphore_wait(barrier, len(peers))
        running = [op.body(engine, *i, *o, *s) for op, i, o, s in zip(ops, ins, outs, scratch)]
        while running:
            left = []
            for item in running:
                try:
                    next(item)
                    left.append(item)
                except StopIteration:
                    pass
            running = left

    results = pl.pallas_call(
        kernel,
        out_shape=[jax.ShapeDtypeStruct(o[0], o[1]) for op in ops for o in op.outs],
        in_specs=[ANY for op in ops for _ in op.ins],
        out_specs=[o[2] if len(o) > 2 else ANY for op in ops for o in op.outs],
        scratch_shapes=[s for op in ops for s in op.scratch]
        + [
            pltpu.SemaphoreType.DMA((n_remote,)),
            pltpu.SemaphoreType.DMA((n_remote,)),
            pltpu.SemaphoreType.DMA((n_local,)),
        ],
        compiler_params=pltpu.CompilerParams(
            collective_id=number, has_side_effects=True, vmem_limit_bytes=32 * 2**20
        ),
        name=name,
    )(*[i for op in ops for i in op.ins])
    split = []
    for op in ops:
        split.append(tuple(results[: len(op.outs)]))
        results = results[len(op.outs) :]
    return split


def swap_op(values):
    def body(engine, src, dst):
        core = lax.axis_index("core")
        copy = engine.send(src.at[rows_at(1 - core, OWN)], dst, sibling())
        yield
        copy.wait()

    return Op([values], [((OWN, WIDTH), values.dtype)], [sibling], body)


def weight_z_op(piece):
    n = piece.shape[1]

    def body(engine, src, dst):
        z = lax.axis_index("z")
        copies = [engine.local(src.at[z], dst.at[z])]
        for d in (1, 2, 3):
            to = z_peer(d)
            copies.append(engine.send(src.at[to["z"]], dst.at[z], to))
        yield
        for copy in copies:
            copy.wait()

    return Op([piece], [((4, n, 128), piece.dtype)], Z_PEERS, body)


def small_op(packed):
    def body(engine, src, dst):
        z, yh = lax.axis_index("z"), lax.axis_index("yh")
        copies = [engine.local(src, dst.at[z, yh])]
        for d in range(4):
            for e in range(2):
                if d or e:
                    to = {"z": lax.rem(z + d, 4), "yh": lax.rem(yh + e, 2)}
                    copies.append(engine.send(src, dst.at[z, yh], to))
        yield
        for copy in copies:
            copy.wait()

    def partner(d, e):
        return {
            "z": lax.rem(lax.axis_index("z") + d, 4),
            "yh": lax.rem(lax.axis_index("yh") + e, 2),
        }

    peers = [functools.partial(partner, d, e) for d in range(4) for e in range(2) if d or e]
    return Op([packed], [((4, 2) + packed.shape, packed.dtype)], peers, body)


def z_gather_op(block):
    def body(engine, src, dst):
        z = lax.axis_index("z")
        copies = [engine.local(src, dst.at[z])]
        for d in (1, 2, 3):
            copies.append(engine.send(src, dst.at[z], z_peer(d)))
        yield
        for copy in copies:
            copy.wait()

    return Op([block], [((4,) + block.shape, block.dtype)], Z_PEERS, body)


def token_gather_op(block):
    def body(engine, src, dst):
        z, core = lax.axis_index("z"), lax.axis_index("core")
        mine = dst.at[rows_at(z * 2 + core, OWN)]
        first = [engine.send(src, mine, z_peer(d)) for d in (1, 2, 3)]
        rest = [engine.send(src, mine, sibling()), engine.local(src, mine)]
        yield
        for d in (1, 2, 3):
            first[d - 1].wait_recv()
            here = dst.at[rows_at(lax.rem(z + 4 - d, 4) * 2 + core, OWN)]
            rest.append(engine.send(here, here, sibling()))
        yield
        for copy in first:
            copy.wait_send()
        for copy in rest:
            copy.wait()

    return Op([block], [((ROWS, WIDTH), block.dtype)], Z_PEERS + [sibling], body)


def token_scatter_op(partial):
    def body(engine, src, dst, own, other, arrived):
        z, core = lax.axis_index("z"), lax.axis_index("core")
        pairs = []
        for i in range(4):
            base = lax.rem(z + 1 + i, 4) * 2
            there = engine.send(src.at[rows_at(base + 1 - core, OWN)], other.at[i], sibling())
            here = engine.local(src.at[rows_at(base + core, OWN)], own.at[i])
            pairs.append((there, here))
        yield
        sent = []
        for i in range(3):
            pairs[i][0].wait_recv()
            pairs[i][1].wait()
            own[i] = (own[i].astype(F32) + other[i].astype(F32)).astype(BF16)
            sent.append(engine.send(own.at[i], arrived.at[i], z_peer(i + 1)))
        yield
        pairs[3][0].wait_recv()
        pairs[3][1].wait()
        dst[...] = own[3].astype(F32) + other[3].astype(F32)
        for i in range(3):
            sent[i].wait_recv()
            dst[...] += arrived[i].astype(F32)
        for i in range(3):
            sent[i].wait_send()
        for there, _ in pairs:
            there.wait_send()

    scratch = (
        pltpu.VMEM((4, OWN, WIDTH), BF16),
        pltpu.VMEM((4, OWN, WIDTH), BF16),
        pltpu.VMEM((3, OWN, WIDTH), BF16),
    )
    return Op([partial], [((OWN, WIDTH), F32, VMEM)], Z_PEERS + [sibling], body, scratch)


def first_part(n):
    return (n // 2 + 15) // 16 * 16


def weight_xy_op(piece):
    n = piece.shape[1]
    cut = first_part(n)
    head, tail = pl.ds(0, cut), pl.ds(cut, n - cut)

    def body(engine, src, dst):
        x = lax.axis_index("x")
        y = lax.axis_index("yh") * 2 + lax.axis_index("yl")
        local = [engine.local(src.at[zz], dst.at[y, :, lanes(zz * 4 + x)]) for zz in range(4)]
        along_x, along_y = [], []
        for d in (1, 2, 3):
            for zz in range(4):
                along_x.append(engine.send(src.at[zz, head], dst.at[y, head, lanes(zz * 4 + x)], x_peer(d)))
                along_y.append(engine.send(src.at[zz, tail], dst.at[y, tail, lanes(zz * 4 + x)], y_peer(d)))
        yield
        for copy in local:
            copy.wait()
        for copy in along_x:
            copy.wait_recv()
        second = [engine.send(dst.at[y, head], dst.at[y, head], y_peer(d)) for d in (1, 2, 3)]
        for copy in along_y:
            copy.wait_recv()
        for d in (1, 2, 3):
            for zz in range(4):
                block = dst.at[:, tail, lanes(zz * 4 + x)]
                second.append(engine.send(block, block, x_peer(d)))
        yield
        for copy in along_x + along_y:
            copy.wait_send()
        for copy in second:
            copy.wait()

    return Op([piece], [((4, n, WIDTH), piece.dtype)], X_PEERS + Y_PEERS, body)


def items_out_op(values, n):
    def body(engine, src, dst):
        x, yl, yh = lax.axis_index("x"), lax.axis_index("yl"), lax.axis_index("yh")
        y = yh * 2 + yl
        mine = dst.at[:, lanes(x * 4 + yl * 2 + yh)]
        copies = []
        for dx, dy in XY_ALL:
            tx, ty = lax.rem(x + dx, 4), lax.rem(y + dy, 4)
            copies.append(engine.send(src.at[rows_at(ty, n), lanes(tx)], mine, xy_peer(dx, dy)))
        copies.append(engine.local(src.at[rows_at(y, n), lanes(x)], mine))
        yield
        for copy in copies:
            copy.wait()

    return Op([values], [((n, SEQ), values.dtype)], XY_PEERS, body)


def items_back_op(values):
    n = values.shape[0]

    def body(engine, src, dst):
        x, yl, yh = lax.axis_index("x"), lax.axis_index("yl"), lax.axis_index("yh")
        y = yh * 2 + yl
        mine = dst.at[rows_at(y, n), lanes(x)]
        copies = []
        for dx, dy in XY_ALL:
            to = xy_peer(dx, dy)
            copies.append(engine.send(src.at[:, lanes(to["x"] * 4 + to["yl"] * 2 + to["yh"])], mine, to))
        copies.append(engine.local(src.at[:, lanes(x * 4 + yl * 2 + yh)], mine))
        yield
        for copy in copies:
            copy.wait()

    return Op([values], [((4 * n, ROWS), values.dtype)], XY_PEERS, body)


def grad_first_op(grad):
    n = grad.shape[1]
    cut = first_part(n)
    head, tail = pl.ds(0, cut), pl.ds(cut, n - cut)

    def body(engine, src, by_y, by_x):
        copies = []
        for d in (1, 2, 3):
            ty, tx = y_peer(d), x_peer(d)
            copies.append(engine.send(src.at[ty["yh"] * 2 + ty["yl"], head], by_y.at[d - 1], ty))
            for zz in range(4):
                block = src.at[:, tail, lanes(zz * 4 + tx["x"])]
                copies.append(engine.send(block, by_x.at[d - 1, :, :, lanes(zz)], tx))
        yield
        for copy in copies:
            copy.wait()

    outs = [((3, cut, WIDTH), grad.dtype), ((3, 4, n - cut, 512), grad.dtype)]
    return Op([grad], outs, X_PEERS + Y_PEERS, body)


def sum_first(grad, by_y, by_x):
    n = grad.shape[1]
    cut = first_part(n)
    x = lax.axis_index("x")
    y = lax.axis_index("yh") * 2 + lax.axis_index("yl")
    own_y = lax.dynamic_index_in_dim(grad[:, :cut], y, 0, keepdims=False).astype(F32)
    tail = grad[:, cut:].reshape(4, n - cut, 4, 4, 128)
    own_x = lax.dynamic_index_in_dim(tail, x, 3, keepdims=False).reshape(4, n - cut, 512).astype(F32)
    summed_y = own_y + jnp.sum(by_y.astype(F32), axis=0)
    summed_x = own_x + jnp.sum(by_x.astype(F32), axis=0)
    return summed_y.astype(BF16), summed_x.astype(BF16)


def grad_second_op(head_sum, tail_sum):
    cut, rest = head_sum.shape[0], tail_sum.shape[1]

    def body(engine, heads, tails, by_x, by_y):
        copies = []
        for d in (1, 2, 3):
            ty, tx = y_peer(d), x_peer(d)
            copies.append(engine.send(tails.at[ty["yh"] * 2 + ty["yl"]], by_y.at[d - 1], ty))
            for zz in range(4):
                block = heads.at[:, lanes(zz * 4 + tx["x"])]
                copies.append(engine.send(block, by_x.at[d - 1, :, lanes(zz)], tx))
        yield
        for copy in copies:
            copy.wait()

    outs = [((3, cut, 512), BF16), ((3, rest, 512), BF16)]
    return Op([head_sum, tail_sum], outs, X_PEERS + Y_PEERS, body)


def sum_second(head_sum, tail_sum, by_x, by_y):
    cut = head_sum.shape[0]
    x = lax.axis_index("x")
    y = lax.axis_index("yh") * 2 + lax.axis_index("yl")
    own_x = lax.dynamic_index_in_dim(head_sum.reshape(cut, 4, 4, 128), x, 2, keepdims=False)
    own_y = lax.dynamic_index_in_dim(tail_sum, y, 0, keepdims=False)
    heads = own_x.reshape(cut, 512).astype(F32) + jnp.sum(by_x.astype(F32), axis=0)
    tails = own_y.astype(F32) + jnp.sum(by_y.astype(F32), axis=0)
    return jnp.concatenate([heads, tails], axis=0).astype(BF16)


def grad_z_op(summed):
    n = summed.shape[0]

    def body(engine, src, dst):
        z = lax.axis_index("z")
        copies = [engine.local(src.at[:, lanes(z)], dst.at[z])]
        for d in (1, 2, 3):
            to = z_peer(d)
            copies.append(engine.send(src.at[:, lanes(to["z"])], dst.at[z], to))
        yield
        for copy in copies:
            copy.wait()

    return Op([summed], [((4, n, 128), summed.dtype)], Z_PEERS, body)


def hand_back_op(block):
    def body(engine, src, dst):
        core, yh = lax.axis_index("core"), lax.axis_index("yh")
        far = {"core": yh, "yh": 1 - yh}
        near = {"core": yh}
        stays = core == yh
        mine = dst.at[rows_at(core, OWN)]
        i, j = engine.remote, engine.locals
        engine.remote += 4
        engine.locals += 1
        send_sem, recv_sem, local_sem = engine.sems

        def make(to, slot):
            return pltpu.make_async_remote_copy(
                src,
                mine,
                send_sem.at[i + slot],
                recv_sem.at[i + 2 + core],
                device_id=to,
                device_id_type=MESH_ID,
            )

        def arrival(half):
            part = dst.at[rows_at(half, OWN)]
            return pltpu.make_async_remote_copy(
                part, part, send_sem.at[i], recv_sem.at[i + 2 + half], device_id=far, device_id_type=MESH_ID
            )

        make(far, 0).start()

        @pl.when(stays)
        def _():
            pltpu.make_async_copy(src, mine, local_sem.at[j]).start()

        @pl.when(jnp.logical_not(stays))
        def _():
            make(near, 1).start()

        yield
        make(far, 0).wait_send()

        @pl.when(stays)
        def _():
            pltpu.make_async_copy(src, mine, local_sem.at[j]).wait()
            arrival(1 - core).wait_recv()

        @pl.when(jnp.logical_not(stays))
        def _():
            make(near, 1).wait_send()
            arrival(core).wait_recv()
            arrival(1 - core).wait_recv()

    def partner(dc, dh):
        return {
            "core": lax.rem(lax.axis_index("core") + dc, 2),
            "yh": lax.rem(lax.axis_index("yh") + dh, 2),
        }

    peers = [functools.partial(partner, dc, dh) for dc, dh in ((0, 1), (1, 0), (1, 1))]
    return Op([block], [((2 * OWN, WIDTH), block.dtype)], peers, body)


def dot(a, b, dims):
    return lax.dot_general(a, b, ((dims[:1], dims[1:]), ((), ())), preferred_element_type=F32)


def rope(block, cosine, sine):
    front, back = block[:8], block[8:16]
    return jnp.concatenate(
        [front * cosine - back * sine, back * cosine + front * sine, block[16:]], axis=0
    )


def rope_back(block, cosine, sine):
    front, back = block[:8], block[8:16]
    return jnp.concatenate(
        [front * cosine + back * sine, back * cosine - front * sine, block[16:]], axis=0
    )


def masked_scores(scores, start, seg_row, seg_col):
    stop = start + QB

    def hide(first, last, by_segment, causal):
        part = scores[first:last]
        keep = None
        if by_segment:
            keep = seg_col[first:last] == seg_row[:, start:stop]
        if causal:
            key_at = first + lax.broadcasted_iota(jnp.int32, part.shape, 0)
            query_at = start + lax.broadcasted_iota(jnp.int32, part.shape, 1)
            order = key_at <= query_at
            keep = order if keep is None else keep & order
        return jnp.where(keep, part, NEG)

    if start == 0:
        return hide(0, stop, True, True)
    if stop + 127 <= SEQ:
        parts = [hide(0, 128, True, False)]
        if start > 128:
            parts.append(scores[128:start])
        parts.append(hide(start, stop, False, True))
        return jnp.concatenate(parts, axis=0)
    return jnp.concatenate([hide(0, start, True, False), hide(start, stop, True, True)], axis=0)


def attend_kernel(qkv_ref, row_ref, col_ref, cos_ref, sin_ref, o_ref, wide_ref, lse_ref, qk_ref):
    cosine, sine = cos_ref[...], sin_ref[...]
    q_t = rope(qkv_ref[:HEAD].astype(F32), cosine, sine).astype(BF16) * jnp.asarray(0.125, BF16)
    k_t = rope(qkv_ref[HEAD : 2 * HEAD].astype(F32), cosine, sine).astype(BF16)
    v_t = qkv_ref[2 * HEAD :]
    qk_ref[:HEAD] = q_t
    qk_ref[HEAD:] = k_t
    keys = k_t.astype(F32).T.astype(BF16)
    seg_row, seg_col = row_ref[...], col_ref[...]
    for start in range(0, SEQ, QB):
        stop = start + QB
        scores = dot(keys[:stop], q_t[:, start:stop], (1, 0))
        scores = masked_scores(scores, start, seg_row, seg_col)
        top = jnp.max(scores, axis=0, keepdims=True)
        terms = jnp.exp(scores - top)
        total = jnp.sum(terms, axis=0, keepdims=True)
        out = dot(v_t[:, :stop], terms.astype(BF16), (1, 0)) / total
        wide_ref[:, start:stop] = out
        o_ref[:, start:stop] = out.astype(BF16)
        lse_ref[:, start:stop] = top + jnp.log(total)


def attend_back_kernel(
    qk_ref, qkv_ref, do_ref, wide_ref, lse_ref, row_ref, col_ref, cos_ref, sin_ref, out_ref, dk_ref, dv_ref
):
    cosine, sine = cos_ref[...], sin_ref[...]
    q_t, k_t, do_t = qk_ref[:HEAD], qk_ref[HEAD:], do_ref[...]
    queries = q_t.astype(F32).T.astype(BF16)
    keys = k_t.astype(F32).T.astype(BF16)
    values = qkv_ref[2 * HEAD :].astype(F32).T.astype(BF16)
    grads = do_t.astype(F32).T.astype(BF16)
    centre = jnp.sum(do_t.astype(F32) * wide_ref[...], axis=0, keepdims=True)
    lse = lse_ref[...]
    seg_row, seg_col = row_ref[...], col_ref[...]
    dk_ref[...] = jnp.zeros_like(dk_ref)
    dv_ref[...] = jnp.zeros_like(dv_ref)
    dq_parts = []
    for start in range(0, SEQ, QB):
        stop = start + QB
        scores = dot(keys[:stop], q_t[:, start:stop], (1, 0))
        scores = masked_scores(scores, start, seg_row, seg_col)
        probs = jnp.exp(scores - lse[:, start:stop])
        d_probs = dot(values[:stop], do_t[:, start:stop], (1, 0))
        d_scores = (probs * (d_probs - centre[:, start:stop])).astype(BF16)
        dv_ref[:stop] += dot(probs.astype(BF16), grads[start:stop], (1, 0))
        dk_ref[:stop] += dot(d_scores, queries[start:stop], (1, 0))
        dq_parts.append(dot(k_t[:, :stop], d_scores, (1, 0)) * 0.125)
    out_ref[:HEAD] = rope_back(jnp.concatenate(dq_parts, axis=1), cosine, sine).astype(BF16)
    out_ref[HEAD : 2 * HEAD] = rope_back(dk_ref[...].T, cosine, sine).astype(BF16)
    out_ref[2 * HEAD :] = dv_ref[...].T.astype(BF16)


def kernel_here(kernel, name, out_shape, scratch=()):
    return pl.pallas_call(
        kernel,
        out_shape=out_shape,
        scratch_shapes=scratch,
        compiler_params=pltpu.CompilerParams(vmem_limit_bytes=48 * 2**20),
        name=name,
    )


def rotation_tables():
    half = ROT // 2
    positions = jnp.arange(SEQ).astype(F32)
    inverse = 10000.0 ** (-(jnp.arange(half).astype(F32) * 2.0 / ROT))
    angles = inverse[:, None] * positions[None, :]
    return jnp.cos(angles), jnp.sin(angles)


def layer_norm(values, gain_row, shift_row):
    row_mean = jnp.mean(values, axis=-1, keepdims=True)
    centred = values - row_mean
    variance = jnp.mean(centred * centred, axis=-1, keepdims=True)
    rstd = lax.rsqrt(variance + EPS)
    normed = centred * rstd
    return normed * gain_row + shift_row, normed, rstd


def norm_back(gradient, normed, rstd, gain_row):
    shaped = gradient * gain_row
    centre = (
        shaped
        - jnp.mean(shaped, axis=-1, keepdims=True)
        - normed * jnp.mean(shaped * normed, axis=-1, keepdims=True)
    )
    return centre * rstd, jnp.sum(gradient * normed, axis=0), jnp.sum(gradient, axis=0)


def local(tokens, segments, w_qkv, b_qkv, w_out, w_gate_up, w_down, norm_gains, norm_shifts, cotangent):
    z, x, yl, core, yh = place()

    def pick(values, axis, index):
        return lax.dynamic_index_in_dim(values, index, axis, keepdims=False)

    piece = lax.dynamic_slice_in_dim(w_qkv, x * 128, 128, 0).reshape(128, 3, 4, 2, 2, HEAD)
    piece = pick(pick(piece, 3, core), 3, yl)
    piece_qkv = piece.transpose(2, 1, 3, 0).reshape(4, 192, 128)
    piece = w_out.reshape(4, 2, 2, 64, 4, 128)
    piece_out = pick(pick(pick(piece, 1, core), 1, yl), 2, x)
    piece = lax.dynamic_slice_in_dim(w_gate_up, x * 128, 128, 0).reshape(128, 2, 4, 2, 2, 176)
    piece = pick(pick(piece, 3, core), 3, yl)
    piece_gu = piece.transpose(2, 1, 3, 0).reshape(4, 352, 128)
    piece = w_down.reshape(4, 2, 2, 176, 4, 128)
    piece_down = pick(pick(pick(piece, 1, core), 1, yl), 2, x)

    packed = jnp.concatenate(
        [
            norm_gains,
            norm_shifts,
            jnp.pad(b_qkv.reshape(-1), (0, 256)).reshape(2, 512),
            jnp.zeros((10, 512), BF16),
        ],
        axis=0,
    )
    token_block, grad_block = tokens[0], cotangent[0]
    got = exchange(
        "start",
        1,
        [
            swap_op(token_block),
            swap_op(grad_block),
            small_op(packed),
            z_gather_op(segments.reshape(16, 128)),
            weight_z_op(piece_qkv),
            weight_z_op(piece_out),
            weight_z_op(piece_gu),
            weight_z_op(piece_down),
        ],
        32,
        8,
    )
    (swapped_x,), (swapped_dy,), (small,), (all_segments,) = got[:4]
    (z_qkv,), (z_out,), (z_gu,), (z_down,) = got[4:]

    stays = core == yh
    x_own = jnp.where(stays, lax.dynamic_slice_in_dim(token_block, core * OWN, OWN, 0), swapped_x).astype(F32)
    dy_own = jnp.where(stays, lax.dynamic_slice_in_dim(grad_block, core * OWN, OWN, 0), swapped_dy)
    wide = small[:, 0, :4].transpose(1, 0, 2).reshape(4, WIDTH).astype(F32)
    gains, shifts = wide[:2], wide[2:]
    bias = small[:, :, 4:6].reshape(4, 2, 1024)[:, :, :768].reshape(4, 2, 3, 4, 2, 2, 16)
    bias = pick(pick(bias, 3, z), 3, core)
    bias = bias.transpose(1, 3, 2, 0, 4).reshape(768, 1).astype(F32)
    item_segments = pick(all_segments, 0, x).reshape(1, SEQ)
    segment_column = item_segments.reshape(SEQ, 1)
    cosine, sine = rotation_tables()

    h1_full, normed_a, rstd_a = layer_norm(x_own, gains[:1], shifts[:1])
    (h1,), (m_qkv,) = exchange(
        "gather_h1", 2, [token_gather_op(h1_full.astype(BF16)), weight_xy_op(z_qkv)], 64, 8
    )
    m_qkv = m_qkv.reshape(768, WIDTH)
    qkv_t = (dot(m_qkv, h1, (1, 1)) + bias).astype(BF16)

    (item_qkv,), (dy,), (m_out,) = exchange(
        "to_items", 3, [items_out_op(qkv_t, 192), token_gather_op(dy_own), weight_xy_op(z_out)], 72, 8
    )
    m_out = m_out.reshape(256, WIDTH)
    o_item, o_wide, lse, qk_item = kernel_here(
        attend_kernel,
        "attend",
        [
            jax.ShapeDtypeStruct((HEAD, SEQ), BF16),
            jax.ShapeDtypeStruct((HEAD, SEQ), F32),
            jax.ShapeDtypeStruct((1, SEQ), F32),
            jax.ShapeDtypeStruct((2 * HEAD, SEQ), BF16),
        ],
    )(item_qkv, item_segments, segment_column, cosine, sine)
    ((o_t,),) = exchange("from_items", 4, [items_back_op(o_item)], 16, 2)

    part = dot(o_t, m_out, (0, 0)).astype(BF16)
    (attn_own,), (m_down,) = exchange(
        "sum_out", 5, [token_scatter_op(part), weight_xy_op(z_down)], 64, 12
    )
    middle = x_own + attn_own
    h2_full, normed_b, rstd_b = layer_norm(middle, gains[1:], shifts[1:])
    (h2,), (m_gu,) = exchange(
        "gather_h2", 6, [token_gather_op(h2_full.astype(BF16)), weight_xy_op(z_gu)], 64, 8
    )
    m_gu = m_gu.reshape(1408, WIDTH)
    m_down = m_down.reshape(704, WIDTH)

    gate_up = dot(m_gu, h2, (1, 1)).reshape(4, 2, 176, ROWS)
    gate, up = gate_up[:, 0], gate_up[:, 1]
    sigmoid = jax.nn.sigmoid(gate)
    silu = gate * sigmoid
    act = (silu * up).astype(BF16).reshape(704, ROWS)
    d_act = dot(m_down, dy, (1, 1)).reshape(4, 176, ROWS)
    d_gate = d_act * up * sigmoid * (1.0 + gate * (1.0 - sigmoid))
    d_gu = jnp.stack([d_gate, d_act * silu], axis=1).astype(BF16).reshape(1408, ROWS)
    mlp_part = dot(act, m_down, (0, 0)).astype(BF16)
    back_part = dot(d_gu, m_gu, (0, 0)).astype(BF16)
    (mlp_own,), (dh2_own,) = exchange(
        "sum_mlp", 7, [token_scatter_op(back_part), token_scatter_op(mlp_part)][::-1], 16, 8
    )
    g_gu = dot(d_gu, h2, (1, 0)).astype(BF16).reshape(4, 352, WIDTH)
    g_down = dot(act, dy, (1, 0)).astype(BF16).reshape(4, 176, WIDTH)

    out_own = (middle + mlp_own).astype(BF16)
    back_b, gain_b, shift_b = norm_back(dh2_own, normed_b, rstd_b, gains[1:])
    d_middle = dy_own.astype(F32) + back_b
    (dz,), first_gu, first_down = exchange(
        "gather_dz",
        8,
        [token_gather_op(d_middle.astype(BF16)), grad_first_op(g_gu), grad_first_op(g_down)],
        48,
        2,
    )
    d_o = dot(m_out, dz, (1, 1)).astype(BF16)
    g_out = dot(o_t, dz, (1, 0)).astype(BF16).reshape(4, 64, WIDTH)
    sums_gu = sum_first(g_gu, *first_gu)
    sums_down = sum_first(g_down, *first_down)
    (do_item,), second_gu, second_down = exchange(
        "do_items",
        9,
        [items_out_op(d_o, HEAD), grad_second_op(*sums_gu), grad_second_op(*sums_down)],
        64,
        2,
    )
    d_item = kernel_here(
        attend_back_kernel,
        "attend_back",
        jax.ShapeDtypeStruct((192, SEQ), BF16),
        [pltpu.VMEM((SEQ, HEAD), F32), pltpu.VMEM((SEQ, HEAD), F32)],
    )(qk_item, item_qkv, do_item, o_wide, lse, item_segments, segment_column, cosine, sine)
    mlp_sum = jnp.concatenate([sum_second(*sums_gu, *second_gu), sum_second(*sums_down, *second_down)], axis=0)
    (d_qkv,), (mlp_z,) = exchange("d_items", 10, [items_back_op(d_item), grad_z_op(mlp_sum)], 24, 2)
    mlp_all = lax.all_gather(mlp_z, ("x", "yl", "core"), axis=0)

    back_part = dot(d_qkv, m_qkv, (0, 0)).astype(BF16)
    g_qkv = dot(d_qkv, h1, (1, 0)).astype(BF16).reshape(4, 192, WIDTH)
    g_bias = jnp.sum(d_qkv.astype(F32), axis=1)
    (dh1_own,), first_qkv, first_out = exchange(
        "sum_dh1", 11, [token_scatter_op(back_part), grad_first_op(g_qkv), grad_first_op(g_out)], 48, 8
    )
    back_a, gain_a, shift_a = norm_back(dh1_own, normed_a, rstd_a, gains[:1])
    grad_own = (d_middle + back_a).astype(BF16)
    sums_qkv = sum_first(g_qkv, *first_qkv)
    sums_out = sum_first(g_out, *first_out)
    (layer_out,), (grad_tokens,), second_qkv, second_out = exchange(
        "hand_back",
        12,
        [hand_back_op(out_own), hand_back_op(grad_own), grad_second_op(*sums_qkv), grad_second_op(*sums_out)],
        48,
        2,
    )
    attn_sum = jnp.concatenate([sum_second(*sums_qkv, *second_qkv), sum_second(*sums_out, *second_out)], axis=0)
    ((attn_z,),) = exchange("grad_z", 13, [grad_z_op(attn_sum)], 4, 2)
    attn_all = lax.all_gather(attn_z, ("x", "yl", "core"), axis=0)

    bias_slots = jnp.arange(8)[:, None] == z * 2 + core
    norms = jnp.stack([gain_a, gain_b, shift_a, shift_b])
    vector = jnp.concatenate([norms.reshape(-1), jnp.where(bias_slots, g_bias[None], 0.0).reshape(-1)])
    vector = lax.psum(vector, ("z", "x", "yl", "core", "yh"))
    norms = lax.dynamic_slice_in_dim(vector[: 4 * WIDTH].reshape(4, WIDTH), z * 512, 512, 1)
    bias_all = vector[4 * WIDTH :].reshape(4, 2, 2, 2, 3, 4, 16)
    bias_all = pick(pick(bias_all, 2, yh), 4, z)
    grad_bias = bias_all.transpose(3, 0, 1, 2, 4).reshape(3, 16, 16)

    mlp_all = mlp_all.reshape(4, 2, 2, 4, 528, 128).astype(F32)
    attn_all = attn_all.reshape(4, 2, 2, 4, 256, 128).astype(F32)
    out_qkv = attn_all[..., :192, :].reshape(4, 2, 2, 4, 3, 64, 128)
    out_qkv = out_qkv.transpose(0, 6, 4, 3, 2, 1, 5).reshape(512, 3, 1024)
    out_out = attn_all[..., 192:, :].transpose(3, 2, 1, 4, 0, 5).reshape(1024, 512)
    out_gu = mlp_all[..., :352, :].reshape(4, 2, 2, 4, 2, 176, 128)
    out_gu = out_gu.transpose(0, 6, 4, 3, 2, 1, 5).reshape(512, 2, 2816)
    out_down = mlp_all[..., 352:, :].transpose(3, 2, 1, 4, 0, 5).reshape(2816, 512)
    return (
        layer_out[None],
        grad_tokens.astype(F32)[None],
        out_qkv,
        grad_bias,
        out_out,
        out_gu,
        out_down,
        norms[:2],
        norms[2:],
    )


def solution(mesh):
    fine = Mesh(mesh.devices.reshape(4, 4, 2, 2, 2), ("z", "x", "yl", "core", "yh"))
    ctx = ("x", "yl", "core")
    return jax.shard_map(
        local,
        mesh=fine,
        in_specs=(
            P("z", ctx, None),
            P("z", None),
            P("z", None, "yh"),
            P(None, "yh", "z"),
            P("yh", "z"),
            P("z", None, "yh"),
            P("yh", "z"),
            P(None, "z"),
            P(None, "z"),
            P("z", ctx, None),
        ),
        out_specs=(
            P("z", ctx, None),
            P("z", ctx, None),
            P("z", None, "yh"),
            P(None, "yh", "z"),
            P("yh", "z"),
            P("z", None, "yh"),
            P("yh", "z"),
            P(None, "z"),
            P(None, "z"),
        ),
        check_vma=False,
    )
```

time: 1720 us -> 748 us (0.43)
  waiting for transfers between devices: 1240 us -> 0.71 us
  Pallas kernels: 0 us -> 351 us
  matrix products: 166 us -> 26.1 us
  local copies, waits for them, and re-layouts: 108 us -> 227 us
  blocking collectives: 98.1 us -> 65.3 us
  starting transfers between devices: 17.4 us -> 0.08 us
    reduce_scatter x4 -> x0, waiting for transfers between devices: 471 us -> none  [the longest x1 201 us: local(): lax.psum_scatter(grad_gate_up.astype(jnp.bfloat16), 'fsdp', scatter_dimen...]
    all_gather x4 -> x2, waiting for transfers between devices: 368 us -> 0.01 us  [the longest x1 0.01 us: local(): attn_all = lax.all_gather(attn_z, ('x', 'yl', 'core'), axis=0)]
    pallas_call x0 -> x15, Pallas kernels: none -> 351 us  [the longest x13 338 us: exchange(): pl.pallas_call(kernel, out_shape=[jax.ShapeDtypeStruct(o[0], o[1]) for op...]
    psum x4 -> x0, waiting for transfers between devices: 314 us -> none  [the longest x1 229 us: local(): lax.psum(summed[2].astype(jnp.bfloat16), 'ctx').astype(jnp.float32)]
    dot_general x40 -> x12, matrix products: 166 us -> 26.1 us  [dot(): lax.dot_general(a, b, ((dims[:1], dims[1:]), ((), ())), preferred_element...]
    unnamed x90 -> x166, local copies, waits for them, and re-layouts: 34.4 us -> 111 us
    unnamed x18 -> x2, waiting for transfers between devices: 65.6 us -> 0.71 us
    all_gather x2 -> x0, local copies, waits for them, and re-layouts: 29.5 us -> none  [the longest x1 29.4 us: local(): lax.all_gather(w_gate_up, 'fsdp', axis=0, tiled=True)]
  transfers between devices with their start and end apart: 18 -> 2, of which waited for: 17 -> 0; matrix products, arithmetic and copies ran while one was open for 9% -> 7% of each run, Pallas kernels for 0% -> 0%
where the time goes in v1:
time: 748 us; the launch traced here: 739 us
  Pallas kernels  351 us (47%)
  local copies, waits for them, and re-layouts  227 us (30%)
  blocking collectives  65.3 us (9%)
  other arithmetic  52.5 us (7%)
  matrix products  26.1 us (3%)
  between operations  16 us (2%)
    pallas_call x13, Pallas kernels, exchange(): pl.pallas_call(kernel, out_shape=[jax.ShapeDtypeStruct(o[0], o[1]) for op...  338 us
    unnamed x166, local copies, waits for them, and re-layouts  111 us
    psum x1, blocking collectives, local(): vector = lax.psum(vector, ('z', 'x', 'yl', 'core', 'yh'))  65.3 us
    dot_general x12, matrix products, dot(): lax.dot_general(a, b, ((dims[:1], dims[1:]), ((), ())), preferred_element...  26.1 us
    reshape x4, local copies, waits for them, and re-layouts, sum_first(): tail = grad[:, cut:].reshape(4, n - cut, 4, 4, 128)  16.1 us
  transfers between devices with their start and end apart: 2, of which 0 were waited for; matrix products, arithmetic and copies ran while one was open for 7% of the time, Pallas kernels for 0%

profile of v1, /device:TPU:1, one launch (start us, length us, event | category | flops | bytes accessed | tf_op | source)
XLA Modules:
  0.0 738.7 jit_solution(1032451656308721757)
XLA Ops:
  7.3 6.1 reshape.331
  15.5 2.1 reshape.328
  19.4 3.4 constant_dynamic-slice_fusion.16
  22.8 4.8 copy.194
  31.7 19.7 %start.1 = (bf16[64,2048]{1,0:T(8,128)(2,1)S(1)}, bf16[64,2048]{1,0:T(8,128)(2,1)S(1)}, bf16[4,2,16,512]{3,2,1,0:T(8,128)(2,1)S(1)}, s32[4,16,128]{2,1,0:T(8,128...) custom-call(bf16[128,2048]{1,0:T(8,128)(2,1)S(1)} %bitcast.264, ...), custom_call_target="tpu_custom_call" | custom-call | tf_op jit(solution)/shard_map/start/pallas_call | solution.py:131
  53.7 33.9 %gather_h1.1 = (bf16[512,2048]{1,0:T(8,128)(2,1)S(1)}, bf16[4,192,2048]{2,1,0:T(8,128)(2,1)S(1)}) custom-call(bf16[64,2048]{1,0:T(8,128)(2,1)S(1)} %fusion.28.refs_0_, bf16[4,192,128]{2,1,0:T(8,128)(2,1)S(1)} %get-tuple-element.57.refs_1_), custom_call_target="tpu_custom_call" | custom-call | tf_op jit(solution)/shard_map/gather_h1/pallas_call | solution.py:131
  88.0 1.8 add_convert_fusion.refs_0_
  90.0 25.9 %to_items.1 = (bf16[192,2048]{1,0:T(8,128)(2,1)S(1)}, bf16[512,2048]{1,0:T(8,128)(2,1)S(1)}, bf16[4,64,2048]{2,1,0:T(8,128)(2,1)S(1)}) custom-call(bf16[768,512]{1,0:T(8,128)(2,1)S(1)} %add_convert_fusion.refs_0_, bf16[64,2048]{1,0:T(8,128)(2,1)S(1)} %bitcast_select_fusion.refs_1_, bf16[4,64,128]{2,1,0:T(8,128)(2,1)S(1)} %copy-done.42), custom_call_target="tpu_custom_call" | custom-call | tf_op jit(solution)/shard_map/to_items/pallas_call | solution.py:131
  115.9 6.0 attend.1
  122.7 9.4 %from_items.1 = bf16[256,512]{1,0:T(8,128)(2,1)S(1)} custom-call(bf16[64,2048]{1,0:T(8,128)(2,1)S(1)} %get-tuple-element.64.refs_0_), custom_call_target="tpu_custom_call" | custom-call | tf_op jit(solution)/shard_map/from_items/pallas_call | solution.py:131
  133.1 25.4 %sum_out.1 = (f32[64,2048]{1,0:T(8,128)S(1)}, bf16[4,176,2048]{2,1,0:T(8,128)(2,1)S(1)}) custom-call(bf16[512,2048]{1,0:T(8,128)(2,1)S(1)} %convolution_convert_fusion.3.refs_0_, bf16[4,176,128]{2,1,0:T(8,128)(2,1)S(1)} %copy-done.39), custom_call_target="tpu_custom_call" | custom-call | tf_op jit(solution)/shard_map/sum_out/pallas_call | solution.py:131
  159.1 50.3 %gather_h2.1 = (bf16[512,2048]{1,0:T(8,128)(2,1)S(1)}, bf16[4,352,2048]{2,1,0:T(8,128)(2,1)S(1)}) custom-call(bf16[64,2048]{1,0:T(8,128)(2,1)S(1)} %add_convert_fusion.5.refs_0_, bf16[4,352,128]{2,1,0:T(8,128)(2,1)S(1)} %copy-done.31), custom_call_target="tpu_custom_call" | custom-call | tf_op jit(solution)/shard_map/gather_h2/pallas_call | solution.py:131
  209.4 3.2 fusion
  213.1 1.9 bitcast_convert_fusion.refs_0_
  215.0 2.1 fusion.13
  222.0 3.4 convolution_convert_fusion
  225.4 3.9 convolution_convert_fusion.5.refs_1_
  229.3 30.0 %sum_mlp.1 = (f32[64,2048]{1,0:T(8,128)S(1)}, f32[64,2048]{1,0:T(8,128)S(1)}) custom-call(bf16[512,2048]{1,0:T(8,128)(2,1)S(1)} %bitcast_convert_fusion.refs_0_, bf16[512,2048]{1,0:T(8,128)(2,1)S(1)} %convolution_convert_fusion.5.refs_1_), custom_call_target="tpu_custom_call" | custom-call | tf_op jit(solution)/shard_map/sum_mlp/pallas_call | solution.py:131
  260.1 3.5 fusion.58
  264.8 52.4 %gather_dz.1 = (bf16[512,2048]{1,0:T(8,128)(2,1)S(1)}, bf16[3,176,2048]{2,1,0:T(8,128)(2,1)S(1)}, bf16[3,4,176,512]{3,2,1,0:T(8,128)(2,1)S(1)}, bf16[3,96,2048]{...) custom-call(bf16[64,2048]{1,0:T(8,128)(2,1)S(1)} %get-tuple-element.154.refs_0_, bf16[4,352,2048]{2,1,0:T(8,128)(2,1)S(1)} %bitcast.253, ...), custom_call_target="tpu_custom_call" | custom-call | tf_op jit(solution)/shard_map/gather_dz/pallas_call | solution.py:131
  323.5 3.1 reduce_sum.279
  326.6 2.6 dynamic-slice_convert_fusion
  331.6 2.6 reduce_sum.282
  335.5 2.0 dynamic-slice_convert_fusion.2
  337.5 2.4 constant_dynamic-slice_fusion.11
  340.0 3.0 reshape.360
  343.0 1.8 constant_dynamic-slice_fusion.4
  347.7 4.1 reshape.341
  351.8 2.0 constant_dynamic-slice_fusion.12
  354.8 2.2 reshape.359
  357.0 3.3 convert_reduce_fusion
  360.2 7.1 reshape.340
  367.3 3.3 constant_dynamic-slice_fusion.13
  372.0 3.1 reshape.357
  375.1 2.8 convolution_convert_fusion.7.refs_0_
  378.6 20.6 %do_items.1 = (bf16[64,2048]{1,0:T(8,128)(2,1)S(1)}, bf16[3,176,512]{2,1,0:T(8,128)(2,1)S(1)}, bf16[3,176,512]{2,1,0:T(8,128)(2,1)S(1)}, bf16[3,96,512]{2,1,0:T(8,128)(2,1)S(1)}, bf16[3,80,512]{2,1,0:T(8,128)(2,1)S(1)}) custom-call(bf16[256,512]{1,0:T(8,128)(2,1)S(1)} %convolution_convert_fusion.7.refs_0_, bf16[176,2048]{1,0:T(8,128)(2,1)S(1)} %fusion.14.refs_1_, ...), custom_call_target="tpu_custom_call" | custom-call | tf_op jit(solution)/shard_map/do_items/pallas_call | solution.py:131
  402.3 2.6 reshape.363
  408.0 6.4 attend_back.1.refs_0_
  414.4 13.1 %d_items.1 = (bf16[768,512]{1,0:T(8,128)(2,1)S(1)}, bf16[4,528,128]{2,1,0:T(8,128)(2,1)}) custom-call(bf16[192,2048]{1,0:T(8,128)(2,1)S(1)} %attend_back.1.refs_0_, bf16[528,512]{1,0:T(8,128)(2,1)S(1)} %pad_maximum_fusion.refs_1_), custom_call_target="tpu_custom_call" | custom-call | tf_op jit(solution)/shard_map/d_items/pallas_call | solution.py:131
  427.6 2.0 convolution_convert_fusion.1
  429.6 1.9 convolution_convert_fusion.4.refs_0_
  432.2 2.1 fusion.59
  435.4 27.6 %sum_dh1.1 = (f32[64,2048]{1,0:T(8,128)S(1)}, bf16[3,96,2048]{2,1,0:T(8,128)(2,1)S(1)}, bf16[3,4,96,512]{3,2,1,0:T(8,128)(2,1)S(1)}, bf16[3,32,2048]{2,1,0:T(8,128)(2,1)S(1)}, bf16[3,4,32,512]{3,2,1,0:T(8,128)(2,1)S(1)}) custom-call(bf16[512,2048]{1,0:T(8,128)(2,1)S(1)} %convolution_convert_fusion.4.refs_0_, bf16[4,192,2048]{2,1,0:T(8,128)(2,1)S(1)} %bitcast.255, ...), custom_call_target="tpu_custom_call" | custom-call | tf_op jit(solution)/shard_map/sum_dh1/pallas_call | solution.py:131
  466.4 1.9 dynamic-slice_convert_fusion.1
  473.6 2.6 reshape.371
  476.2 1.8 constant_dynamic-slice_fusion.2
  482.9 3.8 reshape.344
  486.7 2.3 constant_dynamic-slice_fusion.9
  490.0 2.3 reshape.367
  494.4 24.0 %hand_back.1 = (bf16[128,2048]{1,0:T(8,128)(2,1)S(1)}, bf16[128,2048]{1,0:T(8,128)(2,1)S(1)}, bf16[3,96,512]{2,1,0:T(8,128)(2,1)S(1)}, bf16[3,96,512]{2,1,0:T(8,...) custom-call(bf16[64,2048]{1,0:T(8,128)(2,1)S(1)} %copy-done.13, ...), custom_call_target="tpu_custom_call" | custom-call | tf_op jit(solution)/shard_map/hand_back/pallas_call | solution.py:131
  522.5 5.9 grad_z.1
  529.5 65.3 %psum.7 = f32[14336]{0:T(1024)S(1)} all-reduce(f32[14336]{0:T(1024)S(1)} %pad_maximum_fusion.2), channel_id=1, replica_groups=mesh['z'=4,'x'=4,'yl'=2,'core'=2,'yh'=2] {'z','x','yl','core','yh'}, use_global_device_ids=true, to_apply=%region_29.30 | all-reduce | flops 14336 | bytes 114688 | tf_op jit(solution)/shard_map/psum | solution.py:786
  597.5 5.6 slice.138
  603.1 4.5 convert.61
  607.6 17.8 %copy.188 = f32[4,128,3,4,2,2,64]{6,5,4,3,1,0,2:T(2,128)} copy(f32[4,128,3,4,2,2,64]{1,6,2,3,4,5,0:T(8,128)} %bitcast.283) | data formatting | bytes 12582912
  625.4 15.1 %reshape.390 = f32[512,3,1024]{2,0,1:T(8,128)} reshape(f32[4,128,3,4,2,2,64]{6,5,4,3,1,0,2:T(2,128)} %copy.188) | data formatting | bytes 12582912
  640.5 1.8 slice_bitcast_fusion.1
  645.2 8.6 %slice.141 = f32[4,2,2,4,352,128]{5,4,3,2,1,0:T(8,128)} slice(bf16[4,2,2,4,528,128]{5,4,3,2,1,0:T(8,128)(2,1)} %bitcast.278), slice={[0:4], [0:2], [0:2], [0:4], [0:352], [0:128]} | slice | bytes 23068672 | tf_op jit(solution)/shard_map/slice | solution.py:797
  653.8 11.3 %convert.62 = f32[4,2,2,4,528,128]{5,4,3,2,1,0:T(8,128)} convert(bf16[4,2,2,4,528,128]{5,4,3,2,1,0:T(8,128)(2,1)} %bitcast.279) | non-fusion elementwise | flops 4325376 | bytes 25952256 | tf_op jit(solution)/shard_map/convert_element_type | solution.py:792
  665.1 23.8 %copy.189 = f32[4,128,2,4,2,2,176]{6,5,4,3,2,1,0:T(2,128)} copy(f32[4,128,2,4,2,2,176]{1,6,2,3,4,5,0:T(8,128)} %bitcast.280) | data formatting | bytes 23068672
  688.9 31.7 %reshape.391 = f32[512,2,2816]{2,1,0:T(2,128)} reshape(f32[4,128,2,4,2,2,176]{6,5,4,3,2,1,0:T(2,128)} %copy.189) | data formatting | bytes 23068672
  720.6 3.1 slice_bitcast_fusion
  723.6 3.7 copy.184
  727.4 3.2 copy.261
  (292 shorter events, 71.6 us)
Async XLA Ops:
  7.2 21.5 %copy-start = (bf16[512,3,1024]{2,0,1:T(8,128)(2,1)S(1)}, bf16[512,3,1024]{2,0,1:T(8,128)(2,1)}, u32[]{:S(2)}) copy-start(bf16[512,3,1024]{2,0,1:T(8,128)(2,1)} %param.12) | copy-start | bytes 9437188
  7.2 590.3 %all-gather.5.cloned.1.call-start = ((), (), s32[]{:S(2)}) async-start(), calls=%async_computation | async-start | bytes 4456448 | tf_op jit(solution)/shard_map/all_gather | solution.py:781
  28.7 2.7 copy-start.70
  28.7 2.9 copy-start.75
  28.7 2.9 copy-start.76
  28.7 2.9 copy-start.43
  29.7 2.0 copy-start.7
  29.7 2.0 copy-start.8
  29.7 2.0 copy-start.17
  29.7 2.0 copy-start.36
  51.5 1.7 copy-start.30
  51.5 36.2 %copy-start.38 = (bf16[4,176,128]{2,1,0:T(8,128)(2,1)}, bf16[4,176,128]{2,1,0:T(8,128)(2,1)S(1)}, u32[]{:S(2)}) copy-start(bf16[4,176,128]{2,1,0:T(8,128)(2,1)S(1)} %get-tuple-element.66.refs_1_) | copy-start | bytes 540676
  51.7 106.7 %copy-start.49 = (bf16[64,2048]{1,0:T(8,128)(2,1)}, bf16[64,2048]{1,0:T(8,128)(2,1)S(1)}, u32[]{:S(2)}) copy-start(bf16[64,2048]{1,0:T(8,128)(2,1)S(1)} %get-tuple-element.159) | copy-start | bytes 786436
  51.8 38.1 %copy-start.71 = (f32[64]{0:T(128)}, f32[64]{0:T(128)S(1)}, u32[]{:S(2)}) copy-start(f32[64]{0:T(128)S(1)} %broadcast_multiply_fusion.5) | copy-start | bytes 772
  52.0 37.8 %copy-start.73 = (f32[64]{0:T(128)}, f32[64]{0:T(128)S(1)}, u32[]{:S(2)}) copy-start(f32[64]{0:T(128)S(1)} %add_rsqrt_fusion.1) | copy-start | bytes 772
  52.1 37.8 %copy-start.66 = (f32[1,4,512]{2,0,1:T(1,128)}, f32[1,4,512]{2,0,1:T(1,128)S(1)}, u32[]{:S(2)}) copy-start(f32[1,4,512]{2,0,1:T(1,128)S(1)} %get-tuple-element.176) | copy-start | bytes 24580
  87.6 2.2 copy-start.2
  87.7 2.3 copy-start.45
  88.0 27.9 %copy-start.18 = (f32[8,2048]{1,0:T(8,128)}, f32[8,2048]{1,0:T(8,128)S(1)}, u32[]{:S(2)}) copy-start(f32[8,2048]{1,0:T(8,128)S(1)} %get-tuple-element.177.sin_ref) | copy-start | bytes 196612
  88.0 27.9 %copy-start.20 = (f32[8,2048]{1,0:T(8,128)}, f32[8,2048]{1,0:T(8,128)S(1)}, u32[]{:S(2)}) copy-start(f32[8,2048]{1,0:T(8,128)S(1)} %get-tuple-element.178.cos_ref) | copy-start | bytes 196612
  88.0 2.0 copy-start.42
  115.9 17.0 %copy-start.14 = (bf16[4,64,2048]{2,1,0:T(8,128)(2,1)}, bf16[4,64,2048]{2,1,0:T(8,128)(2,1)S(1)}, u32[]{:S(2)}) copy-start(bf16[4,64,2048]{2,1,0:T(8,128)(2,1)S(1)} %get-tuple-element.65) | copy-start | bytes 3145732
  122.7 10.2 %copy-start.26 = (bf16[128,2048]{1,0:T(8,128)(2,1)}, bf16[128,2048]{1,0:T(8,128)(2,1)S(1)}, u32[]{:S(2)}) copy-start(bf16[128,2048]{1,0:T(8,128)(2,1)S(1)} %get-tuple-element.75.qk_ref) | copy-start | bytes 1572868
  133.1 26.0 %copy-start.31 = (bf16[4,352,128]{2,1,0:T(8,128)(2,1)S(1)}, bf16[4,352,128]{2,1,0:T(8,128)(2,1)}, u32[]{:S(2)}) copy-start(bf16[4,352,128]{2,1,0:T(8,128)(2,1)} %copy-done.30) | copy-start | bytes 1081348
  326.6 2.6 copy-start.48
  326.6 3.9 copy-start.12
  343.0 3.7 copy-start.16
  375.1 2.9 copy-start.56
  375.1 2.9 copy-start.57
  375.1 3.0 copy-start.53
  375.1 3.1 copy-start.54
  399.2 1.8 copy-start.32
  399.3 1.8 copy-start.34
  399.3 1.7 copy-start.37
  402.3 4.2 copy-start.33
  404.9 2.8 copy-start.60
  404.9 2.9 copy-start.61
  404.9 3.0 copy-start.65
  406.3 1.6 copy-start.19
  406.4 1.6 copy-start.21
  406.4 1.6 copy-start.25
  406.4 1.6 copy-start.27
  406.4 1.6 copy-start.35
  408.0 19.6 %copy-start.46 = (bf16[512,2048]{1,0:T(8,128)(2,1)S(1)}, bf16[512,2048]{1,0:T(8,128)(2,1)}, u32[]{:S(2)}) copy-start(bf16[512,2048]{1,0:T(8,128)(2,1)} %copy-done.45) | copy-start | bytes 6291460
  427.6 2.0 copy-start.3
  429.6 1.9 copy-start.6
  465.0 1.4 copy-start.52
  468.4 4.9 copy-start.50
  468.4 4.9 copy-start.67
  468.4 4.9 copy-start.72
  468.4 4.9 copy-start.74
  473.3 5.5 copy-start.29
  473.6 6.0 copy-start.59
  486.7 5.7 copy-start.10
  492.3 1.5 copy-start.51
  492.3 1.5 copy-start.58
  518.4 4.0 copy-start.22
  518.4 3.9 copy-start.64
  519.1 10.1 %copy-start.68 = (f32[2048]{0:T(1024)S(1)}, f32[2048]{0:T(1024)}, u32[]{:S(2)}) copy-start(f32[2048]{0:T(1024)} %get-tuple-element.146) | copy-start | bytes 24580
  519.1 10.0 %copy-start.69 = (f32[2048]{0:T(1024)S(1)}, f32[2048]{0:T(1024)}, u32[]{:S(2)}) copy-start(f32[2048]{0:T(1024)} %get-tuple-element.153) | copy-start | bytes 24580
  528.4 116.9 %all-gather.7.cloned.1.call-start = ((), (), s32[]{:S(2)}) async-start(), calls=%async_computation.1 | async-start | bytes 9191424 | tf_op jit(solution)/shard_map/all_gather | solution.py:760
  597.5 5.7 copy-start.47
  727.4 3.2 copy-start.23
  727.4 4.0 copy-start.1
  (15 other events, 15.1 us)
Sparse Core Ops, SparseCore 0:
  528.5 36.9 all-gather.4
  567.2 53.9 all-gather.6

commit v2 on v1

--- a/solution.py
+++ b/solution.py
@@ -128,10 +128,11 @@
                     pass
             running = left
 
+    given = [i if isinstance(i, tuple) else (i, ANY) for op in ops for i in op.ins]
     results = pl.pallas_call(
         kernel,
         out_shape=[jax.ShapeDtypeStruct(o[0], o[1]) for op in ops for o in op.outs],
-        in_specs=[ANY for op in ops for _ in op.ins],
+        in_specs=[spec for _, spec in given],
         out_specs=[o[2] if len(o) > 2 else ANY for op in ops for o in op.outs],
         scratch_shapes=[s for op in ops for s in op.scratch]
         + [
@@ -140,10 +141,10 @@
             pltpu.SemaphoreType.DMA((n_local,)),
         ],
         compiler_params=pltpu.CompilerParams(
-            collective_id=number, has_side_effects=True, vmem_limit_bytes=32 * 2**20
+            collective_id=number, has_side_effects=True, vmem_limit_bytes=48 * 2**20
         ),
         name=name,
-    )(*[i for op in ops for i in op.ins])
+    )(*[value for value, _ in given])
     split = []
     for op in ops:
         split.append(tuple(results[: len(op.outs)]))
@@ -161,20 +162,63 @@
     return Op([values], [((OWN, WIDTH), values.dtype)], [sibling], body)
 
 
-def weight_z_op(piece):
-    n = piece.shape[1]
-
+def send_pieces(engine, pieces, dst):
+    z = lax.axis_index("z")
+    copies = [engine.local(pieces(z), dst.at[z])]
+    for d in (1, 2, 3):
+        to = z_peer(d)
+        copies.append(engine.send(pieces(to["z"]), dst.at[z], to))
+    return copies
+
+
+def weight_rows_op(weight, n):
     def body(engine, src, dst):
-        z = lax.axis_index("z")
-        copies = [engine.local(src.at[z], dst.at[z])]
-        for d in (1, 2, 3):
-            to = z_peer(d)
-            copies.append(engine.send(src.at[to["z"]], dst.at[z], to))
+        x, yl, core = (lax.axis_index(a) for a in ("x", "yl", "core"))
+
+        def pieces(z):
+            return src.at[rows_at((z * 2 + core) * 2 + yl, n), lanes(x)]
+
+        copies = send_pieces(engine, pieces, dst)
         yield
         for copy in copies:
             copy.wait()
 
-    return Op([piece], [((4, n, 128), piece.dtype)], Z_PEERS, body)
+    return Op([weight], [((4, n, 128), weight.dtype)], Z_PEERS, body)
+
+
+def weight_columns_op(weight, n, middle):
+    groups = weight.shape[1] if middle else weight.shape[0]
+    features = weight.shape[2]
+    joined = not middle
+    block = (128, groups, features) if middle else (groups, 128, features)
+
+    def body(engine, src, *refs):
+        dsts = refs[: 1 if joined else groups]
+        held, turned, cut = refs[len(dsts) :]
+        x, yl, core = (lax.axis_index(a) for a in ("x", "yl", "core"))
+        rows = rows_at(x, 128)
+        load = engine.local(src.at[rows] if middle else src.at[:, rows], held)
+        yield
+        load.wait()
+        copies = []
+        for g in range(groups):
+            turned[...] = (held[:, g, :] if middle else held[g]).astype(F32).T
+            for z in range(4):
+                rows = rows_at((z * 2 + core) * 2 + yl, n)
+                cut[g, z] = turned[rows, :].astype(BF16)
+        for g in range(groups):
+            dst = dsts[0].at[:, pl.ds(g * n, n)] if joined else dsts[g]
+            copies += send_pieces(engine, lambda z: cut.at[g, z], dst)
+        yield
+        for copy in copies:
+            copy.wait()
+
+    if joined:
+        outs = [((4, groups * n, 128), BF16)]
+    else:
+        outs = [((4, n, 128), BF16)] * groups
+    scratch = (pltpu.VMEM(block, BF16), pltpu.VMEM((features, 128), F32), pltpu.VMEM((groups, 4, n, 128), BF16))
+    return Op([weight], outs, Z_PEERS, body, scratch)
 
 
 def small_op(packed):
@@ -292,65 +336,143 @@
             copy.wait()
         for copy in along_x:
             copy.wait_recv()
-        second = [engine.send(dst.at[y, head], dst.at[y, head], y_peer(d)) for d in (1, 2, 3)]
+        left_y, left_x = lax.rem(y + 3, 4), lax.rem(x + 3, 4)
+        right_y, right_x = lax.rem(y + 1, 4), lax.rem(x + 1, 4)
+        ring_y = [engine.send(dst.at[y, head], dst.at[y, head], y_peer(d)) for d in (1, 3)]
         for copy in along_y:
             copy.wait_recv()
-        for d in (1, 2, 3):
-            for zz in range(4):
-                block = dst.at[:, tail, lanes(zz * 4 + x)]
-                second.append(engine.send(block, block, x_peer(d)))
-        yield
-        for copy in along_x + along_y:
+
+        def column(zz, xx):
+            return dst.at[:, tail, lanes(zz * 4 + xx)]
+
+        ring_x = [[engine.send(column(zz, x), column(zz, x), x_peer(d)) for zz in range(4)] for d in (1, 3)]
+        yield
+        rest = []
+        half = first_part(cut)
+        early, late = pl.ds(0, half), pl.ds(half, cut - half)
+        ring_y[0].wait_recv()
+        rest.append(engine.send(dst.at[left_y, early], dst.at[left_y, early], y_peer(1)))
+        ring_y[1].wait_recv()
+        rest.append(engine.send(dst.at[right_y, late], dst.at[right_y, late], y_peer(3)))
+        for zz in range(2):
+            ring_x[0][zz].wait_recv()
+            rest.append(engine.send(column(zz, left_x), column(zz, left_x), x_peer(1)))
+            ring_x[1][zz + 2].wait_recv()
+            rest.append(engine.send(column(zz + 2, right_x), column(zz + 2, right_x), x_peer(3)))
+        yield
+        for zz in range(2):
+            ring_x[0][zz + 2].wait_recv()
+            ring_x[1][zz].wait_recv()
+        for copy in along_x + along_y + ring_y + ring_x[0] + ring_x[1]:
             copy.wait_send()
-        for copy in second:
+        for copy in rest:
             copy.wait()
 
     return Op([piece], [((4, n, WIDTH), piece.dtype)], X_PEERS + Y_PEERS, body)
 
 
-def items_out_op(values, n):
-    def body(engine, src, dst):
-        x, yl, yh = lax.axis_index("x"), lax.axis_index("yl"), lax.axis_index("yh")
-        y = yh * 2 + yl
-        mine = dst.at[:, lanes(x * 4 + yl * 2 + yh)]
-        copies = []
-        for dx, dy in XY_ALL:
-            tx, ty = lax.rem(x + dx, 4), lax.rem(y + dy, 4)
-            copies.append(engine.send(src.at[rows_at(ty, n), lanes(tx)], mine, xy_peer(dx, dy)))
-        copies.append(engine.local(src.at[rows_at(y, n), lanes(x)], mine))
-        yield
-        for copy in copies:
-            copy.wait()
-
-    return Op([values], [((n, SEQ), values.dtype)], XY_PEERS, body)
-
-
-def items_back_op(values):
-    n = values.shape[0]
-
-    def body(engine, src, dst):
-        x, yl, yh = lax.axis_index("x"), lax.axis_index("yl"), lax.axis_index("yh")
-        y = yh * 2 + yl
-        mine = dst.at[rows_at(y, n), lanes(x)]
-        copies = []
-        for dx, dy in XY_ALL:
-            to = xy_peer(dx, dy)
-            copies.append(engine.send(src.at[:, lanes(to["x"] * 4 + to["yl"] * 2 + to["yh"])], mine, to))
-        copies.append(engine.local(src.at[:, lanes(x * 4 + yl * 2 + yh)], mine))
-        yield
-        for copy in copies:
-            copy.wait()
-
-    return Op([values], [((4 * n, ROWS), values.dtype)], XY_PEERS, body)
+def send_items(engine, src, dst, n):
+    x, yl, yh = (lax.axis_index(a) for a in ("x", "yl", "yh"))
+    y = yh * 2 + yl
+    mine = dst.at[:, lanes(x * 4 + yl * 2 + yh)]
+    copies = []
+    for dx, dy in XY_ALL:
+        tx, ty = lax.rem(x + dx, 4), lax.rem(y + dy, 4)
+        copies.append(engine.send(src.at[rows_at(ty, n), lanes(tx)], mine, xy_peer(dx, dy)))
+    copies.append(engine.local(src.at[rows_at(y, n), lanes(x)], mine))
+    return copies
+
+
+def return_items(engine, src, dst, n):
+    x, yl, yh = (lax.axis_index(a) for a in ("x", "yl", "yh"))
+    mine = dst.at[rows_at(yh * 2 + yl, n), lanes(x)]
+    copies = []
+    for dx, dy in XY_ALL:
+        to = xy_peer(dx, dy)
+        copies.append(engine.send(src.at[:, lanes(to["x"] * 4 + to["yl"] * 2 + to["yh"])], mine, to))
+    copies.append(engine.local(src.at[:, lanes(x * 4 + yl * 2 + yh)], mine))
+    return copies
+
+
+def attention_op(qkv_t, seg_row, seg_col, cosine, sine):
+    def body(engine, src, row, col, cos, sin, dst, kept, wide, lse, item, out):
+        copies = send_items(engine, src, item, 3 * HEAD)
+        yield
+        for copy in copies[:-1]:
+            copy.wait_recv()
+        copies[-1].wait()
+        yield
+        attend(item, row, col, cos, sin, out, wide, lse, kept)
+        for copy in copies[:-1]:
+            copy.wait_send()
+        back = return_items(engine, out, dst, HEAD)
+        yield
+        yield
+        for copy in back:
+            copy.wait()
+
+    outs = [
+        ((4 * HEAD, ROWS), BF16),
+        ((3 * HEAD, SEQ), BF16, VMEM),
+        ((HEAD, SEQ), F32, VMEM),
+        ((1, SEQ), F32, VMEM),
+    ]
+    scratch = (pltpu.VMEM((3 * HEAD, SEQ), BF16), pltpu.VMEM((HEAD, SEQ), BF16))
+    ins = [qkv_t] + [(value, VMEM) for value in (seg_row, seg_col, cosine, sine)]
+    return Op(ins, outs, XY_PEERS, body, scratch)
+
+
+def attention_back_op(d_o, kept, wide, lse, seg_row, seg_col, cosine, sine):
+    def body(engine, src, kept, wide, lse, row, col, cos, sin, dst, item, out, dk, dv):
+        copies = send_items(engine, src, item, HEAD)
+        yield
+        for copy in copies[:-1]:
+            copy.wait_recv()
+        copies[-1].wait()
+        yield
+        attend_back(kept, item, wide, lse, row, col, cos, sin, out, dk, dv)
+        for copy in copies[:-1]:
+            copy.wait_send()
+        back = return_items(engine, out, dst, 3 * HEAD)
+        yield
+        yield
+        for copy in back:
+            copy.wait()
+
+    scratch = (
+        pltpu.VMEM((HEAD, SEQ), BF16),
+        pltpu.VMEM((3 * HEAD, SEQ), BF16),
+        pltpu.VMEM((SEQ, HEAD), F32),
+        pltpu.VMEM((SEQ, HEAD), F32),
+    )
+    ins = [d_o] + [(value, VMEM) for value in (kept, wide, lse, seg_row, seg_col, cosine, sine)]
+    return Op(ins, [((12 * HEAD, ROWS), BF16)], XY_PEERS, body, scratch)
+
+
+def add_up(total, own, others, index, rows, width):
+    def step(i, carry):
+        here = (*index, rows_at(i, 16), slice(0, width))
+        value = own[here].astype(F32)
+        for k in range(3):
+            value += others[(k, *here)].astype(F32)
+        total[here] = value.astype(total.dtype)
+        return carry
+
+    lax.fori_loop(0, rows // 16, step, 0)
 
 
 def grad_first_op(grad):
     n = grad.shape[1]
     cut = first_part(n)
-    head, tail = pl.ds(0, cut), pl.ds(cut, n - cut)
-
-    def body(engine, src, by_y, by_x):
-        copies = []
+    rest = n - cut
+    head, tail = pl.ds(0, cut), pl.ds(cut, rest)
+
+    def body(engine, src, sum_y, sum_x, by_y, by_x, own_y, own_x):
+        x = lax.axis_index("x")
+        y = lax.axis_index("yh") * 2 + lax.axis_index("yl")
+        copies, local = [], [engine.local(src.at[y, head], own_y)]
+        for zz in range(4):
+            local.append(engine.local(src.at[:, tail, lanes(zz * 4 + x)], own_x.at[:, :, lanes(zz)]))
         for d in (1, 2, 3):
             ty, tx = y_peer(d), x_peer(d)
             copies.append(engine.send(src.at[ty["yh"] * 2 + ty["yl"], head], by_y.at[d - 1], ty))
@@ -358,31 +480,37 @@
                 block = src.at[:, tail, lanes(zz * 4 + tx["x"])]
                 copies.append(engine.send(block, by_x.at[d - 1, :, :, lanes(zz)], tx))
         yield
+        for copy in local:
+            copy.wait()
+        yield
         for copy in copies:
-            copy.wait()
-
-    outs = [((3, cut, WIDTH), grad.dtype), ((3, 4, n - cut, 512), grad.dtype)]
-    return Op([grad], outs, X_PEERS + Y_PEERS, body)
-
-
-def sum_first(grad, by_y, by_x):
-    n = grad.shape[1]
-    cut = first_part(n)
-    x = lax.axis_index("x")
-    y = lax.axis_index("yh") * 2 + lax.axis_index("yl")
-    own_y = lax.dynamic_index_in_dim(grad[:, :cut], y, 0, keepdims=False).astype(F32)
-    tail = grad[:, cut:].reshape(4, n - cut, 4, 4, 128)
-    own_x = lax.dynamic_index_in_dim(tail, x, 3, keepdims=False).reshape(4, n - cut, 512).astype(F32)
-    summed_y = own_y + jnp.sum(by_y.astype(F32), axis=0)
-    summed_x = own_x + jnp.sum(by_x.astype(F32), axis=0)
-    return summed_y.astype(BF16), summed_x.astype(BF16)
-
-
-def grad_second_op(head_sum, tail_sum):
-    cut, rest = head_sum.shape[0], tail_sum.shape[1]
-
-    def body(engine, heads, tails, by_x, by_y):
-        copies = []
+            copy.wait_recv()
+        add_up(sum_y, own_y, by_y, (), cut, WIDTH)
+        for q in range(4):
+            add_up(sum_x, own_x, by_x, (q,), rest, 512)
+        for copy in copies:
+            copy.wait_send()
+
+    outs = [((cut, WIDTH), BF16, VMEM), ((4, rest, 512), BF16, VMEM)]
+    scratch = (
+        pltpu.VMEM((3, cut, WIDTH), BF16),
+        pltpu.VMEM((3, 4, rest, 512), BF16),
+        pltpu.VMEM((cut, WIDTH), BF16),
+        pltpu.VMEM((4, rest, 512), BF16),
+    )
+    return Op([grad], outs, X_PEERS + Y_PEERS, body, scratch)
+
+
+def grad_rest_op(sum_y, sum_x, gather=False):
+    cut, rest = sum_y.shape[0], sum_x.shape[1]
+    n = cut + rest
+
+    def body(engine, heads, tails, dst, by_x, by_y, own, total, *held):
+        x, yl, core = (lax.axis_index(a) for a in ("x", "yl", "core"))
+        y = lax.axis_index("yh") * 2 + yl
+        copies, local = [], [engine.local(tails.at[y], own.at[pl.ds(cut, rest)])]
+        for zz in range(4):
+            local.append(engine.local(heads.at[:, lanes(zz * 4 + x)], own.at[pl.ds(0, cut), lanes(zz)]))
         for d in (1, 2, 3):
             ty, tx = y_peer(d), x_peer(d)
             copies.append(engine.send(tails.at[ty["yh"] * 2 + ty["yl"]], by_y.at[d - 1], ty))
@@ -390,38 +518,137 @@
                 block = heads.at[:, lanes(zz * 4 + tx["x"])]
                 copies.append(engine.send(block, by_x.at[d - 1, :, lanes(zz)], tx))
         yield
+        for copy in local:
+            copy.wait()
         for copy in copies:
-            copy.wait()
-
-    outs = [((3, cut, 512), BF16), ((3, rest, 512), BF16)]
-    return Op([head_sum, tail_sum], outs, X_PEERS + Y_PEERS, body)
-
-
-def sum_second(head_sum, tail_sum, by_x, by_y):
-    cut = head_sum.shape[0]
-    x = lax.axis_index("x")
-    y = lax.axis_index("yh") * 2 + lax.axis_index("yl")
-    own_x = lax.dynamic_index_in_dim(head_sum.reshape(cut, 4, 4, 128), x, 2, keepdims=False)
-    own_y = lax.dynamic_index_in_dim(tail_sum, y, 0, keepdims=False)
-    heads = own_x.reshape(cut, 512).astype(F32) + jnp.sum(by_x.astype(F32), axis=0)
-    tails = own_y.astype(F32) + jnp.sum(by_y.astype(F32), axis=0)
-    return jnp.concatenate([heads, tails], axis=0).astype(BF16)
-
-
-def grad_z_op(summed):
-    n = summed.shape[0]
-
-    def body(engine, src, dst):
-        z = lax.axis_index("z")
-        copies = [engine.local(src.at[:, lanes(z)], dst.at[z])]
+            copy.wait_recv()
+        add_up(total.at[pl.ds(0, cut)], own.at[pl.ds(0, cut)], by_x, (), cut, 512)
+        add_up(total.at[pl.ds(cut, rest)], own.at[pl.ds(cut, rest)], by_y, (), rest, 512)
+        landing = held[0] if gather else dst
+        moved = send_pieces(engine, lambda z: total.at[:, lanes(z)], landing)
+        for copy in copies:
+            copy.wait_send()
+        yield
+        for copy in moved:
+            copy.wait()
+        if not gather:
+            return
+
+        def slot(xx, ll, cc):
+            return (xx * 2 + ll) * 2 + cc
+
+        first, second = pl.ds(0, 2), pl.ds(2, 2)
+        me = slot(x, yl, core)
+        partner = {"yl": 1 - yl}
+        there = sibling()
+        done = [engine.local(landing, dst.at[me]), engine.send(landing, dst.at[me], there)]
+        to_y = engine.send(landing.at[first], dst.at[me, first], partner)
+        to_x = [engine.send(landing.at[second], dst.at[me, second], x_peer(d)) for d in (1, 2, 3)]
+        yield
+        done[0].wait()
+        final = []
+
+        def pass_on(index, part):
+            block = dst.at[index, part]
+            done.append(engine.send(block, block, there))
+
         for d in (1, 2, 3):
-            to = z_peer(d)
-            copies.append(engine.send(src.at[:, lanes(to["z"])], dst.at[z], to))
-        yield
-        for copy in copies:
-            copy.wait()
-
-    return Op([summed], [((4, n, 128), summed.dtype)], Z_PEERS, body)
+            block = dst.at[me, first]
+            final.append((slot(lax.rem(x + 4 - d, 4), yl, core), first, engine.send(block, block, x_peer(d))))
+        block = dst.at[me, second]
+        final.append((slot(x, 1 - yl, core), second, engine.send(block, block, partner)))
+        to_y.wait_recv()
+        other = slot(x, 1 - yl, core)
+        for d in (1, 2, 3):
+            block = dst.at[other, first]
+            final.append((slot(lax.rem(x + 4 - d, 4), 1 - yl, core), first, engine.send(block, block, x_peer(d))))
+        pass_on(other, first)
+        for d in (1, 2, 3):
+            to_x[d - 1].wait_recv()
+            source = lax.rem(x + 4 - d, 4)
+            block = dst.at[slot(source, yl, core), second]
+            final.append((slot(source, 1 - yl, core), second, engine.send(block, block, partner)))
+            pass_on(slot(source, yl, core), second)
+        yield
+        for index, part, copy in final:
+            copy.wait_recv()
+            pass_on(index, part)
+        yield
+        for copy in [to_y] + to_x + [c for _, _, c in final]:
+            copy.wait_send()
+        for copy in done[1:]:
+            copy.wait()
+
+    shape = (4, n, 128)
+    scratch = [
+        pltpu.VMEM((3, cut, 512), BF16),
+        pltpu.VMEM((3, rest, 512), BF16),
+        pltpu.VMEM((n, 512), BF16),
+        pltpu.VMEM((n, 512), BF16),
+    ]
+    peers = X_PEERS + Y_PEERS + Z_PEERS
+    if gather:
+        scratch.append(pltpu.VMEM(shape, BF16))
+        shape = (16,) + shape
+        peers = peers + [sibling, other_yl]
+    return Op([sum_y, sum_x], [(shape, BF16)], peers, body, tuple(scratch))
+
+
+def other_yl():
+    return {"yl": 1 - lax.axis_index("yl")}
+
+
+def group_peer(dz, dc):
+    return {
+        "z": lax.rem(lax.axis_index("z") + dz, 4),
+        "core": lax.rem(lax.axis_index("core") + dc, 2),
+    }
+
+
+GROUP_ALL = [(dz, dc) for dz in range(4) for dc in range(2) if dz or dc]
+GROUP_PEERS = [functools.partial(group_peer, dz, dc) for dz, dc in GROUP_ALL]
+
+
+def small_sum_op(norms, bias):
+    def body(engine, norms, bias, norm_sum, bias_all, by_group, by_x, by_y):
+        z, x, yl, core, yh = place()
+        y = yh * 2 + yl
+        me = z * 2 + core
+        first = []
+        for dz, dc in GROUP_ALL:
+            to = group_peer(dz, dc)
+            first.append(engine.send(norms.at[:, lanes(to["z"], 512)], by_group.at[me], to))
+        mine = engine.local(norms.at[:, lanes(z, 512)], by_group.at[me])
+        yield
+        mine.wait()
+        for copy in first:
+            copy.wait()
+        by_x[x, :, :512] = sum(by_group[k] for k in range(8))
+        by_x[x, :, 512:] = bias[...]
+        second = [engine.send(by_x.at[x], by_x.at[x], x_peer(d)) for d in (1, 2, 3)]
+        yield
+        for copy in second:
+            copy.wait()
+        by_y[y] = sum(by_x[k] for k in range(4))
+        third = [engine.send(by_y.at[y], by_y.at[y], y_peer(d)) for d in (1, 2, 3)]
+        yield
+        for copy in third:
+            copy.wait()
+        total = sum(by_y[k] for k in range(4))
+        norm_sum[...] = total[:, :512]
+        bias_all[me] = total[:, 512:]
+        last = [engine.send(bias_all.at[me], bias_all.at[me], group_peer(dz, dc)) for dz, dc in GROUP_ALL]
+        yield
+        for copy in last:
+            copy.wait()
+
+    outs = [((8, 512), F32, VMEM), ((8, 8, 128), F32, VMEM)]
+    scratch = (
+        pltpu.VMEM((8, 8, 512), F32),
+        pltpu.VMEM((4, 8, 640), F32),
+        pltpu.VMEM((4, 8, 640), F32),
+    )
+    return Op([(norms, VMEM), (bias, VMEM)], outs, GROUP_PEERS + X_PEERS + Y_PEERS, body, scratch)
 
 
 def hand_back_op(block):
@@ -530,13 +757,14 @@
     return jnp.concatenate([hide(0, start, True, False), hide(start, stop, True, True)], axis=0)
 
 
-def attend_kernel(qkv_ref, row_ref, col_ref, cos_ref, sin_ref, o_ref, wide_ref, lse_ref, qk_ref):
+def attend(qkv_ref, row_ref, col_ref, cos_ref, sin_ref, o_ref, wide_ref, lse_ref, kept_ref):
     cosine, sine = cos_ref[...], sin_ref[...]
     q_t = rope(qkv_ref[:HEAD].astype(F32), cosine, sine).astype(BF16) * jnp.asarray(0.125, BF16)
     k_t = rope(qkv_ref[HEAD : 2 * HEAD].astype(F32), cosine, sine).astype(BF16)
     v_t = qkv_ref[2 * HEAD :]
-    qk_ref[:HEAD] = q_t
-    qk_ref[HEAD:] = k_t
+    kept_ref[:HEAD] = q_t
+    kept_ref[HEAD : 2 * HEAD] = k_t
+    kept_ref[2 * HEAD :] = v_t
     keys = k_t.astype(F32).T.astype(BF16)
     seg_row, seg_col = row_ref[...], col_ref[...]
     for start in range(0, SEQ, QB):
@@ -552,14 +780,12 @@
         lse_ref[:, start:stop] = top + jnp.log(total)
 
 
-def attend_back_kernel(
-    qk_ref, qkv_ref, do_ref, wide_ref, lse_ref, row_ref, col_ref, cos_ref, sin_ref, out_ref, dk_ref, dv_ref
-):
+def attend_back(kept_ref, do_ref, wide_ref, lse_ref, row_ref, col_ref, cos_ref, sin_ref, out_ref, dk_ref, dv_ref):
     cosine, sine = cos_ref[...], sin_ref[...]
-    q_t, k_t, do_t = qk_ref[:HEAD], qk_ref[HEAD:], do_ref[...]
+    q_t, k_t, do_t = kept_ref[:HEAD], kept_ref[HEAD : 2 * HEAD], do_ref[...]
     queries = q_t.astype(F32).T.astype(BF16)
     keys = k_t.astype(F32).T.astype(BF16)
-    values = qkv_ref[2 * HEAD :].astype(F32).T.astype(BF16)
+    values = kept_ref[2 * HEAD :].astype(F32).T.astype(BF16)
     grads = do_t.astype(F32).T.astype(BF16)
     centre = jnp.sum(do_t.astype(F32) * wide_ref[...], axis=0, keepdims=True)
     lse = lse_ref[...]
@@ -582,14 +808,61 @@
     out_ref[2 * HEAD :] = dv_ref[...].T.astype(BF16)
 
 
-def kernel_here(kernel, name, out_shape, scratch=()):
+def assemble_kernel(mlp_ref, attn_ref, gu_ref, down_ref, qkv_ref, out_ref, turned):
+    for g in range(2):
+        for zz in range(4):
+            for core in range(2):
+                for yl in range(2):
+                    row = zz * 704 + core * 352 + yl * 176
+                    block = mlp_ref[0, yl * 2 + core, zz, g * 176 : (g + 1) * 176]
+                    turned[row : row + 176, :] = block.astype(F32)
+        for t in range(22):
+            gu_ref[:, g, t * 128 : (t + 1) * 128] = turned[t * 128 : (t + 1) * 128, :].T
+    for zz in range(4):
+        for core in range(2):
+            for yl in range(2):
+                row = zz * 704 + core * 352 + yl * 176
+                down_ref[row : row + 176, :] = mlp_ref[0, yl * 2 + core, zz, 352:].astype(F32)
+                row = zz * 256 + core * 128 + yl * 64
+                out_ref[row : row + 32, :] = attn_ref[0, yl * 2 + core, zz, 96:128].astype(F32)
+                out_ref[row + 32 : row + 64, :] = attn_ref[0, yl * 2 + core, zz, 224:].astype(F32)
+            for part in range(3):
+                pieces = []
+                for yl in range(2):
+                    for row in (part * 64, part * 64 + 32):
+                        row = row if row < 96 else row + 32
+                        pieces.append(attn_ref[0, yl * 2 + core, zz, row : row + 32])
+                block = jnp.concatenate(pieces, axis=0)
+                column = zz * 256 + core * 128
+                qkv_ref[part, :, column : column + 128] = block.astype(F32).T
+
+
+def assemble(mlp_all, attn_all):
+    mlp_all = mlp_all.reshape(4, 4, 4, 528, 128)
+    attn_all = attn_all.reshape(4, 4, 4, 256, 128)
     return pl.pallas_call(
-        kernel,
-        out_shape=out_shape,
-        scratch_shapes=scratch,
+        assemble_kernel,
+        grid=(4,),
+        in_specs=[
+            pl.BlockSpec((1, 4, 4, 528, 128), lambda i: (i, 0, 0, 0, 0)),
+            pl.BlockSpec((1, 4, 4, 256, 128), lambda i: (i, 0, 0, 0, 0)),
+        ],
+        out_specs=[
+            pl.BlockSpec((128, 2, 2816), lambda i: (i, 0, 0)),
+            pl.BlockSpec((2816, 128), lambda i: (0, i)),
+            pl.BlockSpec((3, 128, 1024), lambda i: (0, i, 0)),
+            pl.BlockSpec((1024, 128), lambda i: (0, i)),
+        ],
+        out_shape=[
+            jax.ShapeDtypeStruct((512, 2, 2816), F32),
+            jax.ShapeDtypeStruct((2816, 512), F32),
+            jax.ShapeDtypeStruct((3, 512, 1024), F32),
+            jax.ShapeDtypeStruct((1024, 512), F32),
+        ],
+        scratch_shapes=[pltpu.VMEM((2816, 128), F32)],
         compiler_params=pltpu.CompilerParams(vmem_limit_bytes=48 * 2**20),
-        name=name,
-    )
+        name="assemble",
+    )(mlp_all, attn_all)
 
 
 def rotation_tables():
@@ -624,17 +897,6 @@
 
     def pick(values, axis, index):
         return lax.dynamic_index_in_dim(values, index, axis, keepdims=False)
-
-    piece = lax.dynamic_slice_in_dim(w_qkv, x * 128, 128, 0).reshape(128, 3, 4, 2, 2, HEAD)
-    piece = pick(pick(piece, 3, core), 3, yl)
-    piece_qkv = piece.transpose(2, 1, 3, 0).reshape(4, 192, 128)
-    piece = w_out.reshape(4, 2, 2, 64, 4, 128)
-    piece_out = pick(pick(pick(piece, 1, core), 1, yl), 2, x)
-    piece = lax.dynamic_slice_in_dim(w_gate_up, x * 128, 128, 0).reshape(128, 2, 4, 2, 2, 176)
-    piece = pick(pick(piece, 3, core), 3, yl)
-    piece_gu = piece.transpose(2, 1, 3, 0).reshape(4, 352, 128)
-    piece = w_down.reshape(4, 2, 2, 176, 4, 128)
-    piece_down = pick(pick(pick(piece, 1, core), 1, yl), 2, x)
 
     packed = jnp.concatenate(
         [
@@ -654,16 +916,16 @@
             swap_op(grad_block),
             small_op(packed),
             z_gather_op(segments.reshape(16, 128)),
-            weight_z_op(piece_qkv),
-            weight_z_op(piece_out),
-            weight_z_op(piece_gu),
-            weight_z_op(piece_down),
+            weight_columns_op(w_qkv.transpose(1, 0, 2), HEAD, False),
+            weight_rows_op(w_out, 64),
+            weight_rows_op(w_down, 176),
+            weight_columns_op(w_gate_up, 176, True),
         ],
-        32,
-        8,
+        48,
+        16,
     )
     (swapped_x,), (swapped_dy,), (small,), (all_segments,) = got[:4]
-    (z_qkv,), (z_out,), (z_gu,), (z_down,) = got[4:]
+    (z_qkv,), (z_out,), (z_down,), (z_gate, z_up) = got[4:]
 
     stays = core == yh
     x_own = jnp.where(stays, lax.dynamic_slice_in_dim(token_block, core * OWN, OWN, 0), swapped_x).astype(F32)
@@ -678,135 +940,123 @@
     cosine, sine = rotation_tables()
 
     h1_full, normed_a, rstd_a = layer_norm(x_own, gains[:1], shifts[:1])
-    (h1,), (m_qkv,) = exchange(
-        "gather_h1", 2, [token_gather_op(h1_full.astype(BF16)), weight_xy_op(z_qkv)], 64, 8
+    (m_qkv,), (h1,) = exchange(
+        "gather_h1", 2, [weight_xy_op(z_qkv), token_gather_op(h1_full.astype(BF16))], 64, 8
     )
     m_qkv = m_qkv.reshape(768, WIDTH)
     qkv_t = (dot(m_qkv, h1, (1, 1)) + bias).astype(BF16)
 
-    (item_qkv,), (dy,), (m_out,) = exchange(
-        "to_items", 3, [items_out_op(qkv_t, 192), token_gather_op(dy_own), weight_xy_op(z_out)], 72, 8
-    )
+    attention, (dy,), (m_out,), (m_down,) = exchange(
+        "attention",
+        3,
+        [
+            attention_op(qkv_t, item_segments, segment_column, cosine, sine),
+            token_gather_op(dy_own),
+            weight_xy_op(z_out),
+            weight_xy_op(z_down),
+        ],
+        144,
+        16,
+    )
+    o_t, kept, o_wide, lse = attention
     m_out = m_out.reshape(256, WIDTH)
-    o_item, o_wide, lse, qk_item = kernel_here(
-        attend_kernel,
-        "attend",
-        [
-            jax.ShapeDtypeStruct((HEAD, SEQ), BF16),
-            jax.ShapeDtypeStruct((HEAD, SEQ), F32),
-            jax.ShapeDtypeStruct((1, SEQ), F32),
-            jax.ShapeDtypeStruct((2 * HEAD, SEQ), BF16),
-        ],
-    )(item_qkv, item_segments, segment_column, cosine, sine)
-    ((o_t,),) = exchange("from_items", 4, [items_back_op(o_item)], 16, 2)
+    m_down = m_down.reshape(704, WIDTH)
 
     part = dot(o_t, m_out, (0, 0)).astype(BF16)
-    (attn_own,), (m_down,) = exchange(
-        "sum_out", 5, [token_scatter_op(part), weight_xy_op(z_down)], 64, 12
-    )
+    (m_gate,), (attn_own,) = exchange("sum_out", 4, [weight_xy_op(z_gate), token_scatter_op(part)], 64, 12)
     middle = x_own + attn_own
     h2_full, normed_b, rstd_b = layer_norm(middle, gains[1:], shifts[1:])
-    (h2,), (m_gu,) = exchange(
-        "gather_h2", 6, [token_gather_op(h2_full.astype(BF16)), weight_xy_op(z_gu)], 64, 8
-    )
-    m_gu = m_gu.reshape(1408, WIDTH)
-    m_down = m_down.reshape(704, WIDTH)
-
-    gate_up = dot(m_gu, h2, (1, 1)).reshape(4, 2, 176, ROWS)
-    gate, up = gate_up[:, 0], gate_up[:, 1]
+    (m_up,), (h2,) = exchange(
+        "gather_h2", 5, [weight_xy_op(z_up), token_gather_op(h2_full.astype(BF16))], 64, 8
+    )
+    m_gate = m_gate.reshape(704, WIDTH)
+    m_up = m_up.reshape(704, WIDTH)
+
+    gate, up = dot(m_gate, h2, (1, 1)), dot(m_up, h2, (1, 1))
     sigmoid = jax.nn.sigmoid(gate)
     silu = gate * sigmoid
-    act = (silu * up).astype(BF16).reshape(704, ROWS)
-    d_act = dot(m_down, dy, (1, 1)).reshape(4, 176, ROWS)
-    d_gate = d_act * up * sigmoid * (1.0 + gate * (1.0 - sigmoid))
-    d_gu = jnp.stack([d_gate, d_act * silu], axis=1).astype(BF16).reshape(1408, ROWS)
+    act = (silu * up).astype(BF16)
+    d_act = dot(m_down, dy, (1, 1))
+    d_gate = (d_act * up * sigmoid * (1.0 + gate * (1.0 - sigmoid))).astype(BF16)
+    d_up = (d_act * silu).astype(BF16)
     mlp_part = dot(act, m_down, (0, 0)).astype(BF16)
-    back_part = dot(d_gu, m_gu, (0, 0)).astype(BF16)
-    (mlp_own,), (dh2_own,) = exchange(
-        "sum_mlp", 7, [token_scatter_op(back_part), token_scatter_op(mlp_part)][::-1], 16, 8
-    )
-    g_gu = dot(d_gu, h2, (1, 0)).astype(BF16).reshape(4, 352, WIDTH)
-    g_down = dot(act, dy, (1, 0)).astype(BF16).reshape(4, 176, WIDTH)
+    back_part = (dot(d_gate, m_gate, (0, 0)) + dot(d_up, m_up, (0, 0))).astype(BF16)
+
+    def weight_grad(a, b):
+        return dot(a, b, (1, 0)).astype(BF16).reshape(4, a.shape[0] // 4, WIDTH)
+
+    g_gate, g_up, g_down = weight_grad(d_gate, h2), weight_grad(d_up, h2), weight_grad(act, dy)
+    (dh2_own,), (mlp_own,), first_gate, first_down = exchange(
+        "sum_mlp",
+        6,
+        [token_scatter_op(back_part), token_scatter_op(mlp_part), grad_first_op(g_gate), grad_first_op(g_down)],
+        48,
+        24,
+    )
 
     out_own = (middle + mlp_own).astype(BF16)
     back_b, gain_b, shift_b = norm_back(dh2_own, normed_b, rstd_b, gains[1:])
     d_middle = dy_own.astype(F32) + back_b
-    (dz,), first_gu, first_down = exchange(
+    (dz,), first_up, (z_down,) = exchange(
         "gather_dz",
+        7,
+        [token_gather_op(d_middle.astype(BF16)), grad_first_op(g_up), grad_rest_op(*first_down)],
+        48,
+        24,
+    )
+    d_o = dot(m_out, dz, (1, 1)).astype(BF16)
+    g_out = weight_grad(o_t, dz)
+    (d_qkv,), (z_gate,), (z_up,), (layer_out,) = exchange(
+        "attention_back",
         8,
-        [token_gather_op(d_middle.astype(BF16)), grad_first_op(g_gu), grad_first_op(g_down)],
-        48,
-        2,
-    )
-    d_o = dot(m_out, dz, (1, 1)).astype(BF16)
-    g_out = dot(o_t, dz, (1, 0)).astype(BF16).reshape(4, 64, WIDTH)
-    sums_gu = sum_first(g_gu, *first_gu)
-    sums_down = sum_first(g_down, *first_down)
-    (do_item,), second_gu, second_down = exchange(
-        "do_items",
-        9,
-        [items_out_op(d_o, HEAD), grad_second_op(*sums_gu), grad_second_op(*sums_down)],
-        64,
-        2,
-    )
-    d_item = kernel_here(
-        attend_back_kernel,
-        "attend_back",
-        jax.ShapeDtypeStruct((192, SEQ), BF16),
-        [pltpu.VMEM((SEQ, HEAD), F32), pltpu.VMEM((SEQ, HEAD), F32)],
-    )(qk_item, item_qkv, do_item, o_wide, lse, item_segments, segment_column, cosine, sine)
-    mlp_sum = jnp.concatenate([sum_second(*sums_gu, *second_gu), sum_second(*sums_down, *second_down)], axis=0)
-    (d_qkv,), (mlp_z,) = exchange("d_items", 10, [items_back_op(d_item), grad_z_op(mlp_sum)], 24, 2)
+        [
+            attention_back_op(d_o, kept, o_wide, lse, item_segments, segment_column, cosine, sine),
+            grad_rest_op(*first_gate),
+            grad_rest_op(*first_up),
+            hand_back_op(out_own),
+        ],
+        96,
+        24,
+    )
+    mlp_z = jnp.concatenate([z_gate, z_up, z_down], axis=1)
     mlp_all = lax.all_gather(mlp_z, ("x", "yl", "core"), axis=0)
 
     back_part = dot(d_qkv, m_qkv, (0, 0)).astype(BF16)
-    g_qkv = dot(d_qkv, h1, (1, 0)).astype(BF16).reshape(4, 192, WIDTH)
+    g_qkv = weight_grad(d_qkv, h1)
     g_bias = jnp.sum(d_qkv.astype(F32), axis=1)
     (dh1_own,), first_qkv, first_out = exchange(
-        "sum_dh1", 11, [token_scatter_op(back_part), grad_first_op(g_qkv), grad_first_op(g_out)], 48, 8
+        "sum_dh1", 9, [token_scatter_op(back_part), grad_first_op(g_qkv), grad_first_op(g_out)], 48, 24
     )
     back_a, gain_a, shift_a = norm_back(dh1_own, normed_a, rstd_a, gains[:1])
     grad_own = (d_middle + back_a).astype(BF16)
-    sums_qkv = sum_first(g_qkv, *first_qkv)
-    sums_out = sum_first(g_out, *first_out)
-    (layer_out,), (grad_tokens,), second_qkv, second_out = exchange(
-        "hand_back",
-        12,
-        [hand_back_op(out_own), hand_back_op(grad_own), grad_second_op(*sums_qkv), grad_second_op(*sums_out)],
-        48,
-        2,
-    )
-    attn_sum = jnp.concatenate([sum_second(*sums_qkv, *second_qkv), sum_second(*sums_out, *second_out)], axis=0)
-    ((attn_z,),) = exchange("grad_z", 13, [grad_z_op(attn_sum)], 4, 2)
-    attn_all = lax.all_gather(attn_z, ("x", "yl", "core"), axis=0)
-
-    bias_slots = jnp.arange(8)[:, None] == z * 2 + core
-    norms = jnp.stack([gain_a, gain_b, shift_a, shift_b])
-    vector = jnp.concatenate([norms.reshape(-1), jnp.where(bias_slots, g_bias[None], 0.0).reshape(-1)])
-    vector = lax.psum(vector, ("z", "x", "yl", "core", "yh"))
-    norms = lax.dynamic_slice_in_dim(vector[: 4 * WIDTH].reshape(4, WIDTH), z * 512, 512, 1)
-    bias_all = vector[4 * WIDTH :].reshape(4, 2, 2, 2, 3, 4, 16)
+    norms = jnp.pad(jnp.stack([gain_a, gain_b, shift_a, shift_b]), ((0, 4), (0, 0)))
+    first_attn = [jnp.concatenate([a, b], axis=-2) for a, b in zip(first_qkv, first_out)]
+    (attn_all,), (norm_sum, bias_all), (grad_tokens,) = exchange(
+        "finish",
+        10,
+        [
+            grad_rest_op(*first_attn, gather=True),
+            small_sum_op(norms, jnp.pad(g_bias, (0, 256)).reshape(8, 128)),
+            hand_back_op(grad_own),
+        ],
+        80,
+        24,
+    )
+    attn_all = attn_all.reshape(16, 4, 256, 128)
+    bias_all = bias_all.reshape(8, 1024)[:, :768].reshape(4, 2, 2, 2, 3, 4, 16)
     bias_all = pick(pick(bias_all, 2, yh), 4, z)
     grad_bias = bias_all.transpose(3, 0, 1, 2, 4).reshape(3, 16, 16)
-
-    mlp_all = mlp_all.reshape(4, 2, 2, 4, 528, 128).astype(F32)
-    attn_all = attn_all.reshape(4, 2, 2, 4, 256, 128).astype(F32)
-    out_qkv = attn_all[..., :192, :].reshape(4, 2, 2, 4, 3, 64, 128)
-    out_qkv = out_qkv.transpose(0, 6, 4, 3, 2, 1, 5).reshape(512, 3, 1024)
-    out_out = attn_all[..., 192:, :].transpose(3, 2, 1, 4, 0, 5).reshape(1024, 512)
-    out_gu = mlp_all[..., :352, :].reshape(4, 2, 2, 4, 2, 176, 128)
-    out_gu = out_gu.transpose(0, 6, 4, 3, 2, 1, 5).reshape(512, 2, 2816)
-    out_down = mlp_all[..., 352:, :].transpose(3, 2, 1, 4, 0, 5).reshape(2816, 512)
+    out_gu, out_down, out_qkv, out_out = assemble(mlp_all, attn_all)
     return (
         layer_out[None],
         grad_tokens.astype(F32)[None],
-        out_qkv,
+        out_qkv.transpose(1, 0, 2),
         grad_bias,
         out_out,
         out_gu,
         out_down,
-        norms[:2],
-        norms[2:],
+        norm_sum[:2],
+        norm_sum[2:4],
     )
 
 

time: 748 us -> 431 us (0.58)
  local copies, waits for them, and re-layouts: 227 us -> 12.9 us
  blocking collectives: 65.3 us -> 0 us
  other arithmetic: 52.5 us -> 5.84 us
  matrix products: 26.1 us -> 36.5 us
    unnamed x166 -> x36, local copies, waits for them, and re-layouts: 111 us -> 9.87 us
    psum x1 -> x0, blocking collectives: 65.3 us -> none  [local(): vector = lax.psum(vector, ('z', 'x', 'yl', 'core', 'yh'))]
    convert_element_type x24 -> x0, other arithmetic: 34.6 us -> none  [the longest x1 11.3 us: local(): mlp_all = mlp_all.reshape(4, 2, 2, 4, 528, 128).astype(F32)]
    reshape x7 -> x2, local copies, waits for them, and re-layouts: 24.5 us -> 0.18 us  [the longest x1 0.18 us: local(): bias_all = bias_all.reshape(8, 1024)[:, :768].reshape(4, 2, 2, 2, 3, 4, 16)]
    slice x12 -> x2, local copies, waits for them, and re-layouts: 24.7 us -> 0.6 us  [the longest x1 0.6 us: local(): norm_sum[2:4]]
    dynamic_slice x12 -> x0, local copies, waits for them, and re-layouts: 23.1 us -> none  [the longest x6 9.75 us: sum_second(): lax.dynamic_index_in_dim(head_sum.reshape(cut, 4, 4, 128), x, 2, keepdims...]
    convert_element_type x13 -> x0, local copies, waits for them, and re-layouts: 19.8 us -> none  [the longest x4 9.37 us: sum_first(): lax.dynamic_index_in_dim(grad[:, :cut], y, 0, keepdims=False).astype(F32)]
    transpose x9 -> x0, local copies, waits for them, and re-layouts: 11.7 us -> none  [the longest x2 6.76 us: local(): mlp_all[..., 352:, :].transpose(3, 2, 1, 4, 0, 5).reshape(2816, 512)]
  transfers between devices with their start and end apart: 2 -> 1, of which waited for: 0 -> 0; matrix products, arithmetic and copies ran while one was open for 7% -> 3% of each run, Pallas kernels for 0% -> 23%
where the time goes in v2:
time: 431 us; the launch traced here: 427 us
  Pallas kernels  357 us (83%)
  matrix products  36.5 us (8%)
  between operations  14.8 us (3%)
  local copies, waits for them, and re-layouts  12.9 us (3%)
  other arithmetic  5.84 us (1%)
    pallas_call x10, Pallas kernels, exchange(): pl.pallas_call(kernel, out_shape=[jax.ShapeDtypeStruct(o[0], o[1]) for op...  343 us
    dot_general x15, matrix products, dot(): lax.dot_general(a, b, ((dims[:1], dims[1:]), ((), ())), preferred_element...  36.5 us
    pallas_call x1, Pallas kernels, assemble(): pl.pallas_call(assemble_kernel, grid=(4,), in_specs=[pl.BlockSpec((1, 4,...  14.1 us
    unnamed x36, local copies, waits for them, and re-layouts  9.87 us
  transfers between devices with their start and end apart: 1, of which 0 were waited for; matrix products, arithmetic and copies ran while one was open for 3% of the time, Pallas kernels for 23%

profile of v2, /device:TPU:1, one launch (start us, length us, event | category | flops | bytes accessed | tf_op | source)
XLA Modules:
  0.0 427.1 jit_solution(9651867804020912379)
XLA Ops:
  7.2 0.0 all-gather.3.cloned.1.call-start
  7.2 0.8 reshape.167
  8.1 0.1 pad.29.clone
  8.1 0.8 maximum_maximum_fusion.refs_2_
  8.9 1.0 copy-done.5
  9.9 1.0 copy-done.7
  11.0 1.2 copy-done.9
  12.2 0.7 copy-done.10
  12.9 20.3 %start.1 = (bf16[64,2048]{1,0:T(8,128)(2,1)S(1)}, bf16[64,2048]{1,0:T(8,128)(2,1)S(1)}, bf16[4,2,16,512]{3,2,1,0:T(8,128)(2,1)S(1)}, s32[4,16,128]{2,1,0:T(8,128...) custom-call(bf16[128,2048]{1,0:T(8,128)(2,1)S(1)} %bitcast.93, ...), custom_call_target="tpu_custom_call" | custom-call | tf_op jit(solution)/shard_map/start/pallas_call | solution.py:132
  33.4 0.2 convert_reduce_fusion.1
  33.6 0.2 fusion.15
  33.9 0.1 reshape.172
  34.1 0.1 reshape.189
  34.2 0.1 bitcast_select_fusion.refs_5_
  34.2 0.4 copy.28.refs_2_.refs_5_
  34.6 0.2 fusion.8.refs_1_
  34.8 23.2 %gather_h1.1 = (bf16[4,192,2048]{2,1,0:T(8,128)(2,1)S(1)}, bf16[512,2048]{1,0:T(8,128)(2,1)S(1)}) custom-call(bf16[4,192,128]{2,1,0:T(8,128)(2,1)S(1)} %get-tuple-element.58.refs_0_, bf16[64,2048]{1,0:T(8,128)(2,1)S(1)} %fusion.8.refs_1_), custom_call_target="tpu_custom_call" | custom-call | tf_op jit(solution)/shard_map/gather_h1/pallas_call | solution.py:132
  58.0 0.0 copy-start.2
  58.0 0.3 multiply_sine_fusion
  58.3 1.8 add_convert_fusion.1.refs_0_
  60.2 0.3 copy-done.11
  60.4 40.6 %attention.1 = (bf16[256,512]{1,0:T(8,128)(2,1)S(1)}, bf16[192,2048]{1,0:T(8,128)(2,1)S(1)}, f32[64,2048]{1,0:T(8,128)S(1)}, f32[1,2048]{1,0:T(1,128)S(1)}, bf16...) custom-call(bf16[768,512]{1,0:T(8,128)(2,1)S(1)} %add_convert_fusion.1.refs_0_, ...), custom_call_target="tpu_custom_call" | custom-call | tf_op jit(solution)/shard_map/attention/pallas_call | solution.py:132
  101.0 0.7 convolution_convert_fusion.4.refs_1_
  101.8 24.3 %sum_out.1 = (bf16[4,176,2048]{2,1,0:T(8,128)(2,1)S(1)}, f32[64,2048]{1,0:T(8,128)S(1)}) custom-call(bf16[4,176,128]{2,1,0:T(8,128)(2,1)S(1)} %get-tuple-element.71.refs_0_, bf16[512,2048]{1,0:T(8,128)(2,1)S(1)} %convolution_convert_fusion.4.refs_1_), custom_call_target="tpu_custom_call" | custom-call | tf_op jit(solution)/shard_map/sum_out/pallas_call | solution.py:132
  126.1 0.2 fusion.17
  126.3 0.2 multiply_reduce_fusion.2
  126.5 4.6 %fusion.20 = f32[704,512]{1,0:T(8,128)} fusion(bf16[704,2048]{1,0:T(8,128)(2,1)} %bitcast.126, bf16[512,2048]{1,0:T(8,128)(2,1)S(1)} %copy-done.14), kind=kOutput, calls=%fused_computation.77 | convolution fusion | flops 1476395008 | bytes 6422528 | tf_op jit(solution)/shard_map/dot_general | solution.py:717
  131.1 0.2 add_convert_fusion.3.refs_1_
  131.3 27.5 %gather_h2.1 = (bf16[4,176,2048]{2,1,0:T(8,128)(2,1)S(1)}, bf16[512,2048]{1,0:T(8,128)(2,1)S(1)}) custom-call(bf16[4,176,128]{2,1,0:T(8,128)(2,1)S(1)} %get-tuple-element.70.refs_0_, bf16[64,2048]{1,0:T(8,128)(2,1)S(1)} %add_convert_fusion.3.refs_1_), custom_call_target="tpu_custom_call" | custom-call | tf_op jit(solution)/shard_map/gather_h2/pallas_call | solution.py:132
  158.8 1.7 fusion.21
  160.5 2.2 multiply_convert_fusion
  162.8 3.2 convolution_convert_fusion.2
  166.0 3.2 convolution_convert_fusion.6.refs_1_
  169.2 3.2 convolution_convert_fusion.3
  172.5 1.9 fusion.22
  174.3 3.2 convolution_convert_fusion.1
  177.6 2.1 add_convert_fusion.refs_0_
  179.7 39.1 %sum_mlp.1 = (f32[64,2048]{1,0:T(8,128)S(1)}, f32[64,2048]{1,0:T(8,128)S(1)}, bf16[96,2048]{1,0:T(8,128)(2,1)S(1)}, bf16[4,80,512]{2,1,0:T(8,128)(2,1)S(1)}, bf1...) custom-call(bf16[512,2048]{1,0:T(8,128)(2,1)S(1)} %add_convert_fusion.refs_0_, ...), custom_call_target="tpu_custom_call" | custom-call | tf_op jit(solution)/shard_map/sum_mlp/pallas_call | solution.py:132
  218.9 0.3 multiply_reduce_fusion
  219.2 0.3 fusion.16
  219.5 30.6 %gather_dz.1 = (bf16[512,2048]{1,0:T(8,128)(2,1)S(1)}, bf16[96,2048]{1,0:T(8,128)(2,1)S(1)}, bf16[4,80,512]{2,1,0:T(8,128)(2,1)S(1)}, bf16[4,176,128]{2,1,0:T(8,128)(2,1)S(1)}) custom-call(bf16[64,2048]{1,0:T(8,128)(2,1)S(1)} %get-tuple-element.115.refs_0_, bf16[4,176,2048]{2,1,0:T(8,128)(2,1)} %bitcast.108, bf16[96,2048]{1,0:T(8,128)(2,1)S(1)} %get-tuple-element.78.refs_2_, ...), custom_call_target="tpu_custom_call" | custom-call | tf_op jit(solution)/shard_map/gather_dz/pallas_call | solution.py:132
  250.1 0.0 copy-start.4
  250.1 0.7 convolution_convert_fusion.8.refs_0_
  250.9 0.6 copy-done.4
  251.4 39.9 %attention_back.1 = (bf16[768,512]{1,0:T(8,128)(2,1)S(1)}, bf16[4,176,128]{2,1,0:T(8,128)(2,1)S(1)}, bf16[4,176,128]{2,1,0:T(8,128)(2,1)S(1)}, bf16[128,2048]{1,0:T(8,128)(2,1)S(1)}) custom-call(bf16[256,512]{1,0:T(8,128)(2,1)S(1)} %convolution_convert_fusion.8.refs_0_, bf16[192,2048]{1,0:T(8,128)(2,1)S(1)} %get-tuple-element.81.refs_1_, ...), custom_call_target="tpu_custom_call" | custom-call | tf_op jit(solution)/shard_map/attention_back/pallas_call | solution.py:132
  291.4 0.8 pad_maximum_fusion
  292.2 0.0 all-gather.3.cloned.1.call-update
  292.3 2.5 convolution_convert_fusion.7
  294.7 0.0 copy-start.3
  294.7 3.5 convolution_convert_fusion
  298.2 1.8 convolution_convert_fusion.5.refs_0_
  300.0 52.1 %sum_dh1.1 = (f32[64,2048]{1,0:T(8,128)S(1)}, bf16[96,2048]{1,0:T(8,128)(2,1)S(1)}, bf16[4,96,512]{2,1,0:T(8,128)(2,1)S(1)}, bf16[32,2048]{1,0:T(8,128)(2,1)S(1)}, bf16[4,32,512]{2,1,0:T(8,128)(2,1)S(1)}) custom-call(bf16[512,2048]{1,0:T(8,128)(2,1)S(1)} %convolution_convert_fusion.5.refs_0_, bf16[4,192,2048]{2,1,0:T(8,128)(2,1)} %bitcast.106, ...), custom_call_target="tpu_custom_call" | custom-call | tf_op jit(solution)/shard_map/sum_dh1/pallas_call | solution.py:132
  352.2 0.2 convert_reduce_fusion
  352.4 0.3 fusion.10
  352.8 0.3 fusion.14.refs_4_
  353.1 45.2 %finish.1 = (bf16[16,4,256,128]{3,2,1,0:T(8,128)(2,1)S(1)}, f32[8,512]{1,0:T(8,128)S(1)}, f32[8,8,128]{2,1,0:T(8,128)S(1)}, bf16[128,2048]{1,0:T(8,128)(2,1)S(1)}) custom-call(bf16[128,2048]{1,0:T(8,128)(2,1)S(1)} %pad_maximum_fusion.1.refs_0_, bf16[4,128,512]{2,1,0:T(8,128)(2,1)S(1)} %pad_maximum_fusion.2.refs_1_, ...), custom_call_target="tpu_custom_call" | custom-call | tf_op jit(solution)/shard_map/finish/pallas_call | solution.py:132
  398.4 2.0 copy-done
  400.4 0.2 reshape.187
  400.7 0.6 copy.30
  401.3 0.6 fusion.19
  401.9 1.1 bitcast_convert_fusion
  403.0 2.2 copy-done.1
  405.2 14.1 %assemble.1 = (f32[512,2,2816]{2,1,0:T(2,128)}, f32[2816,512]{1,0:T(8,128)}, f32[3,512,1024]{2,1,0:T(8,128)}, f32[1024,512]{1,0:T(8,128)}) custom-call(bf16[4,4,4,528,128]{4,3,2,1,0:T(8,128)(2,1)} %bitcast.105, bf16[4,4,4,256,128]{4,3,2,1,0:T(8,128)(2,1)S(1)} %bitcast.87), custom_call_target="tpu_custom_call" | custom-call | tf_op jit(solution)/shard_map/assemble/pallas_call | solution.py:843
  419.2 0.8 copy.35
  (51 shorter events, 0.4 us)
Async XLA Ops:
  7.2 395.8 %all-gather.3.cloned.1.call-start = ((), (), s32[]{:S(2)}) async-start(), calls=%async_computation | async-start | bytes 9191424 | tf_op jit(solution)/shard_map/all_gather | solution.py:1022
  8.9 1.0 copy-start.5
  9.9 1.0 copy-start.7
  11.0 1.2 copy-start.9
  12.2 0.7 copy-start.10
  12.9 20.4 %copy-start.6 = (bf16[1,128,2048]{2,1,0:T(8,128)(2,1)S(1)}, bf16[1,128,2048]{2,1,0:T(8,128)(2,1)}, u32[]{:S(2)}) copy-start(bf16[1,128,2048]{2,1,0:T(8,128)(2,1)} %param.10) | copy-start | bytes 1572868
  12.9 21.3 %copy-start.8 = (bf16[1,128,2048]{2,1,0:T(8,128)(2,1)S(1)}, bf16[1,128,2048]{2,1,0:T(8,128)(2,1)}, u32[]{:S(2)}) copy-start(bf16[1,128,2048]{2,1,0:T(8,128)(2,1)} %param.19) | copy-start | bytes 1572868
  58.0 2.2 copy-start.2
  58.0 2.4 copy-start.11
  101.8 24.7 %copy-start.14 = (bf16[512,2048]{1,0:T(8,128)(2,1)S(1)}, bf16[512,2048]{1,0:T(8,128)(2,1)}, u32[]{:S(2)}) copy-start(bf16[512,2048]{1,0:T(8,128)(2,1)} %get-tuple-element.69) | copy-start | bytes 6291460
  158.8 1.7 copy-start.16
  160.5 2.2 copy-start.15
  162.8 3.3 copy-start.13
  250.1 1.3 copy-start.4
  292.3 2.5 copy-start.12
  294.7 3.5 copy-start.3
  398.4 2.0 copy-start
  403.0 2.2 copy-start.1
Sparse Core Ops, SparseCore 0:
  292.4 83.2 all-gather.2

commit v3 on v2

--- a/solution.py
+++ b/solution.py
@@ -94,6 +94,21 @@
         self.ins, self.outs, self.peers, self.body, self.scratch = ins, outs, peers, body, scratch
 
 
+def greet(peers):
+    barrier = pltpu.get_barrier_semaphore()
+    for peer in peers:
+        pl.semaphore_signal(barrier, 1, device_id=peer(), device_id_type=MESH_ID)
+    pl.semaphore_wait(barrier, len(peers))
+
+
+def semaphores(n_remote, n_local):
+    return [
+        pltpu.SemaphoreType.DMA((n_remote,)),
+        pltpu.SemaphoreType.DMA((n_remote,)),
+        pltpu.SemaphoreType.DMA((n_local,)),
+    ]
+
+
 def exchange(name, number, ops, n_remote, n_local):
     peers = []
     for op in ops:
@@ -113,10 +128,7 @@
         outs = [take(len(op.outs)) for op in ops]
         scratch = [take(len(op.scratch)) for op in ops]
         engine = Engine(*refs)
-        barrier = pltpu.get_barrier_semaphore()
-        for peer in peers:
-            pl.semaphore_signal(barrier, 1, device_id=peer(), device_id_type=MESH_ID)
-        pl.semaphore_wait(barrier, len(peers))
+        greet(peers)
         running = [op.body(engine, *i, *o, *s) for op, i, o, s in zip(ops, ins, outs, scratch)]
         while running:
             left = []
@@ -135,11 +147,7 @@
         in_specs=[spec for _, spec in given],
         out_specs=[o[2] if len(o) > 2 else ANY for op in ops for o in op.outs],
         scratch_shapes=[s for op in ops for s in op.scratch]
-        + [
-            pltpu.SemaphoreType.DMA((n_remote,)),
-            pltpu.SemaphoreType.DMA((n_remote,)),
-            pltpu.SemaphoreType.DMA((n_local,)),
-        ],
+        + semaphores(n_remote, n_local),
         compiler_params=pltpu.CompilerParams(
             collective_id=number, has_side_effects=True, vmem_limit_bytes=48 * 2**20
         ),
@@ -152,129 +160,86 @@
     return split
 
 
-def swap_op(values):
-    def body(engine, src, dst):
-        core = lax.axis_index("core")
-        copy = engine.send(src.at[rows_at(1 - core, OWN)], dst, sibling())
-        yield
-        copy.wait()
-
-    return Op([values], [((OWN, WIDTH), values.dtype)], [sibling], body)
-
-
-def send_pieces(engine, pieces, dst):
+def spread(values):
+    return jnp.concatenate(
+        [values[:, (a * 4 + b) * 128 : (a * 4 + b + 1) * 128] for b in range(4) for a in range(4)], axis=1
+    )
+
+
+def finish(thread):
+    for _ in thread:
+        pass
+
+
+def send_pieces(engine, pieces, slots):
     z = lax.axis_index("z")
-    copies = [engine.local(pieces(z), dst.at[z])]
+    copies = [engine.local(pieces(z), slots(z))]
     for d in (1, 2, 3):
         to = z_peer(d)
-        copies.append(engine.send(pieces(to["z"]), dst.at[z], to))
+        copies.append(engine.send(pieces(to["z"]), slots(z), to))
     return copies
 
 
-def weight_rows_op(weight, n):
-    def body(engine, src, dst):
-        x, yl, core = (lax.axis_index(a) for a in ("x", "yl", "core"))
-
-        def pieces(z):
-            return src.at[rows_at((z * 2 + core) * 2 + yl, n), lanes(x)]
-
-        copies = send_pieces(engine, pieces, dst)
-        yield
-        for copy in copies:
-            copy.wait()
-
-    return Op([weight], [((4, n, 128), weight.dtype)], Z_PEERS, body)
-
-
-def weight_columns_op(weight, n, middle):
-    groups = weight.shape[1] if middle else weight.shape[0]
-    features = weight.shape[2]
-    joined = not middle
-    block = (128, groups, features) if middle else (groups, 128, features)
-
-    def body(engine, src, *refs):
-        dsts = refs[: 1 if joined else groups]
-        held, turned, cut = refs[len(dsts) :]
-        x, yl, core = (lax.axis_index(a) for a in ("x", "yl", "core"))
-        rows = rows_at(x, 128)
-        load = engine.local(src.at[rows] if middle else src.at[:, rows], held)
-        yield
-        load.wait()
-        copies = []
-        for g in range(groups):
-            turned[...] = (held[:, g, :] if middle else held[g]).astype(F32).T
-            for z in range(4):
-                rows = rows_at((z * 2 + core) * 2 + yl, n)
-                cut[g, z] = turned[rows, :].astype(BF16)
-        for g in range(groups):
-            dst = dsts[0].at[:, pl.ds(g * n, n)] if joined else dsts[g]
-            copies += send_pieces(engine, lambda z: cut.at[g, z], dst)
-        yield
-        for copy in copies:
-            copy.wait()
-
-    if joined:
-        outs = [((4, groups * n, 128), BF16)]
-    else:
-        outs = [((4, n, 128), BF16)] * groups
-    scratch = (pltpu.VMEM(block, BF16), pltpu.VMEM((features, 128), F32), pltpu.VMEM((groups, 4, n, 128), BF16))
-    return Op([weight], outs, Z_PEERS, body, scratch)
-
-
-def small_op(packed):
-    def body(engine, src, dst):
-        z, yh = lax.axis_index("z"), lax.axis_index("yh")
-        copies = [engine.local(src, dst.at[z, yh])]
-        for d in range(4):
-            for e in range(2):
-                if d or e:
-                    to = {"z": lax.rem(z + d, 4), "yh": lax.rem(yh + e, 2)}
-                    copies.append(engine.send(src, dst.at[z, yh], to))
-        yield
-        for copy in copies:
-            copy.wait()
-
-    def partner(d, e):
-        return {
-            "z": lax.rem(lax.axis_index("z") + d, 4),
-            "yh": lax.rem(lax.axis_index("yh") + e, 2),
-        }
-
-    peers = [functools.partial(partner, d, e) for d in range(4) for e in range(2) if d or e]
-    return Op([packed], [((4, 2) + packed.shape, packed.dtype)], peers, body)
-
-
-def z_gather_op(block):
-    def body(engine, src, dst):
-        z = lax.axis_index("z")
-        copies = [engine.local(src, dst.at[z])]
-        for d in (1, 2, 3):
-            copies.append(engine.send(src, dst.at[z], z_peer(d)))
-        yield
-        for copy in copies:
-            copy.wait()
-
-    return Op([block], [((4,) + block.shape, block.dtype)], Z_PEERS, body)
+def gather_tokens(engine, src, dst):
+    z, core = lax.axis_index("z"), lax.axis_index("core")
+    mine = dst.at[rows_at(z * 2 + core, OWN)]
+    first = [engine.send(src, mine, z_peer(d)) for d in (1, 2, 3)]
+    rest = [engine.send(src, mine, sibling()), engine.local(src, mine)]
+    yield
+    for d in (1, 2, 3):
+        first[d - 1].wait_recv()
+        here = dst.at[rows_at(lax.rem(z + 4 - d, 4) * 2 + core, OWN)]
+        rest.append(engine.send(here, here, sibling()))
+    yield
+    for copy in first:
+        copy.wait_send()
+    for copy in rest:
+        copy.wait()
+
+
+def gather_weight(engine, src, dst):
+    n = src.shape[0]
+    top = first_part(n)
+    head, tail = pl.ds(0, top), pl.ds(top, n - top)
+    x = lax.axis_index("x")
+    y = lax.axis_index("yh") * 2 + lax.axis_index("yl")
+    left_y, left_x = lax.rem(y + 3, 4), lax.rem(x + 3, 4)
+    right_y, right_x = lax.rem(y + 1, 4), lax.rem(x + 1, 4)
+    mine = lanes(x, 512)
+    local = engine.local(src, dst.at[y, :, mine])
+    along_x = [engine.send(src.at[head], dst.at[y, head, mine], x_peer(d)) for d in (1, 2, 3)]
+    along_y = [engine.send(src.at[tail], dst.at[y, tail, mine], y_peer(d)) for d in (1, 2, 3)]
+    yield
+    local.wait()
+    for copy in along_x:
+        copy.wait_recv()
+    ring_y = [engine.send(dst.at[y, head], dst.at[y, head], y_peer(d)) for d in (1, 3)]
+    for copy in along_y:
+        copy.wait_recv()
+    ring_x = [engine.send(dst.at[:, tail, mine], dst.at[:, tail, mine], x_peer(d)) for d in (1, 3)]
+    yield
+    rest = []
+    half = first_part(top)
+    early, late = pl.ds(0, half), pl.ds(half, top - half)
+    ring_y[0].wait_recv()
+    rest.append(engine.send(dst.at[left_y, early], dst.at[left_y, early], y_peer(1)))
+    ring_y[1].wait_recv()
+    rest.append(engine.send(dst.at[right_y, late], dst.at[right_y, late], y_peer(3)))
+    ring_x[0].wait_recv()
+    block = dst.at[:, tail, lanes(left_x * 2, 256)]
+    rest.append(engine.send(block, block, x_peer(1)))
+    ring_x[1].wait_recv()
+    block = dst.at[:, tail, lanes(right_x * 2 + 1, 256)]
+    rest.append(engine.send(block, block, x_peer(3)))
+    yield
+    for copy in along_x + along_y + ring_y + ring_x:
+        copy.wait_send()
+    for copy in rest:
+        copy.wait()
 
 
 def token_gather_op(block):
-    def body(engine, src, dst):
-        z, core = lax.axis_index("z"), lax.axis_index("core")
-        mine = dst.at[rows_at(z * 2 + core, OWN)]
-        first = [engine.send(src, mine, z_peer(d)) for d in (1, 2, 3)]
-        rest = [engine.send(src, mine, sibling()), engine.local(src, mine)]
-        yield
-        for d in (1, 2, 3):
-            first[d - 1].wait_recv()
-            here = dst.at[rows_at(lax.rem(z + 4 - d, 4) * 2 + core, OWN)]
-            rest.append(engine.send(here, here, sibling()))
-        yield
-        for copy in first:
-            copy.wait_send()
-        for copy in rest:
-            copy.wait()
-
-    return Op([block], [((ROWS, WIDTH), block.dtype)], Z_PEERS + [sibling], body)
+    return Op([block], [((ROWS, WIDTH), block.dtype)], Z_PEERS + [sibling], gather_tokens)
 
 
 def token_scatter_op(partial):
@@ -317,60 +282,6 @@
     return (n // 2 + 15) // 16 * 16
 
 
-def weight_xy_op(piece):
-    n = piece.shape[1]
-    cut = first_part(n)
-    head, tail = pl.ds(0, cut), pl.ds(cut, n - cut)
-
-    def body(engine, src, dst):
-        x = lax.axis_index("x")
-        y = lax.axis_index("yh") * 2 + lax.axis_index("yl")
-        local = [engine.local(src.at[zz], dst.at[y, :, lanes(zz * 4 + x)]) for zz in range(4)]
-        along_x, along_y = [], []
-        for d in (1, 2, 3):
-            for zz in range(4):
-                along_x.append(engine.send(src.at[zz, head], dst.at[y, head, lanes(zz * 4 + x)], x_peer(d)))
-                along_y.append(engine.send(src.at[zz, tail], dst.at[y, tail, lanes(zz * 4 + x)], y_peer(d)))
-        yield
-        for copy in local:
-            copy.wait()
-        for copy in along_x:
-            copy.wait_recv()
-        left_y, left_x = lax.rem(y + 3, 4), lax.rem(x + 3, 4)
-        right_y, right_x = lax.rem(y + 1, 4), lax.rem(x + 1, 4)
-        ring_y = [engine.send(dst.at[y, head], dst.at[y, head], y_peer(d)) for d in (1, 3)]
-        for copy in along_y:
-            copy.wait_recv()
-
-        def column(zz, xx):
-            return dst.at[:, tail, lanes(zz * 4 + xx)]
-
-        ring_x = [[engine.send(column(zz, x), column(zz, x), x_peer(d)) for zz in range(4)] for d in (1, 3)]
-        yield
-        rest = []
-        half = first_part(cut)
-        early, late = pl.ds(0, half), pl.ds(half, cut - half)
-        ring_y[0].wait_recv()
-        rest.append(engine.send(dst.at[left_y, early], dst.at[left_y, early], y_peer(1)))
-        ring_y[1].wait_recv()
-        rest.append(engine.send(dst.at[right_y, late], dst.at[right_y, late], y_peer(3)))
-        for zz in range(2):
-            ring_x[0][zz].wait_recv()
-            rest.append(engine.send(column(zz, left_x), column(zz, left_x), x_peer(1)))
-            ring_x[1][zz + 2].wait_recv()
-            rest.append(engine.send(column(zz + 2, right_x), column(zz + 2, right_x), x_peer(3)))
-        yield
-        for zz in range(2):
-            ring_x[0][zz + 2].wait_recv()
-            ring_x[1][zz].wait_recv()
-        for copy in along_x + along_y + ring_y + ring_x[0] + ring_x[1]:
-            copy.wait_send()
-        for copy in rest:
-            copy.wait()
-
-    return Op([piece], [((4, n, WIDTH), piece.dtype)], X_PEERS + Y_PEERS, body)
-
-
 def send_items(engine, src, dst, n):
     x, yl, yh = (lax.axis_index(a) for a in ("x", "yl", "yh"))
     y = yh * 2 + yl
@@ -394,34 +305,6 @@
     return copies
 
 
-def attention_op(qkv_t, seg_row, seg_col, cosine, sine):
-    def body(engine, src, row, col, cos, sin, dst, kept, wide, lse, item, out):
-        copies = send_items(engine, src, item, 3 * HEAD)
-        yield
-        for copy in copies[:-1]:
-            copy.wait_recv()
-        copies[-1].wait()
-        yield
-        attend(item, row, col, cos, sin, out, wide, lse, kept)
-        for copy in copies[:-1]:
-            copy.wait_send()
-        back = return_items(engine, out, dst, HEAD)
-        yield
-        yield
-        for copy in back:
-            copy.wait()
-
-    outs = [
-        ((4 * HEAD, ROWS), BF16),
-        ((3 * HEAD, SEQ), BF16, VMEM),
-        ((HEAD, SEQ), F32, VMEM),
-        ((1, SEQ), F32, VMEM),
-    ]
-    scratch = (pltpu.VMEM((3 * HEAD, SEQ), BF16), pltpu.VMEM((HEAD, SEQ), BF16))
-    ins = [qkv_t] + [(value, VMEM) for value in (seg_row, seg_col, cosine, sine)]
-    return Op(ins, outs, XY_PEERS, body, scratch)
-
-
 def attention_back_op(d_o, kept, wide, lse, seg_row, seg_col, cosine, sine):
     def body(engine, src, kept, wide, lse, row, col, cos, sin, dst, item, out, dk, dv):
         copies = send_items(engine, src, item, HEAD)
@@ -470,15 +353,12 @@
     def body(engine, src, sum_y, sum_x, by_y, by_x, own_y, own_x):
         x = lax.axis_index("x")
         y = lax.axis_index("yh") * 2 + lax.axis_index("yl")
-        copies, local = [], [engine.local(src.at[y, head], own_y)]
-        for zz in range(4):
-            local.append(engine.local(src.at[:, tail, lanes(zz * 4 + x)], own_x.at[:, :, lanes(zz)]))
+        copies = []
+        local = [engine.local(src.at[y, head], own_y), engine.local(src.at[:, tail, lanes(x, 512)], own_x)]
         for d in (1, 2, 3):
             ty, tx = y_peer(d), x_peer(d)
             copies.append(engine.send(src.at[ty["yh"] * 2 + ty["yl"], head], by_y.at[d - 1], ty))
-            for zz in range(4):
-                block = src.at[:, tail, lanes(zz * 4 + tx["x"])]
-                copies.append(engine.send(block, by_x.at[d - 1, :, :, lanes(zz)], tx))
+            copies.append(engine.send(src.at[:, tail, lanes(tx["x"], 512)], by_x.at[d - 1], tx))
         yield
         for copy in local:
             copy.wait()
@@ -509,14 +389,11 @@
         x, yl, core = (lax.axis_index(a) for a in ("x", "yl", "core"))
         y = lax.axis_index("yh") * 2 + yl
         copies, local = [], [engine.local(tails.at[y], own.at[pl.ds(cut, rest)])]
-        for zz in range(4):
-            local.append(engine.local(heads.at[:, lanes(zz * 4 + x)], own.at[pl.ds(0, cut), lanes(zz)]))
+        local.append(engine.local(heads.at[:, lanes(x, 512)], own.at[pl.ds(0, cut)]))
         for d in (1, 2, 3):
             ty, tx = y_peer(d), x_peer(d)
             copies.append(engine.send(tails.at[ty["yh"] * 2 + ty["yl"]], by_y.at[d - 1], ty))
-            for zz in range(4):
-                block = heads.at[:, lanes(zz * 4 + tx["x"])]
-                copies.append(engine.send(block, by_x.at[d - 1, :, lanes(zz)], tx))
+            copies.append(engine.send(heads.at[:, lanes(tx["x"], 512)], by_x.at[d - 1], tx))
         yield
         for copy in local:
             copy.wait()
@@ -525,7 +402,7 @@
         add_up(total.at[pl.ds(0, cut)], own.at[pl.ds(0, cut)], by_x, (), cut, 512)
         add_up(total.at[pl.ds(cut, rest)], own.at[pl.ds(cut, rest)], by_y, (), rest, 512)
         landing = held[0] if gather else dst
-        moved = send_pieces(engine, lambda z: total.at[:, lanes(z)], landing)
+        moved = send_pieces(engine, lambda z: total.at[:, lanes(z)], lambda z: landing.at[z])
         for copy in copies:
             copy.wait_send()
         yield
@@ -806,6 +683,263 @@
     out_ref[:HEAD] = rope_back(jnp.concatenate(dq_parts, axis=1), cosine, sine).astype(BF16)
     out_ref[HEAD : 2 * HEAD] = rope_back(dk_ref[...].T, cosine, sine).astype(BF16)
     out_ref[2 * HEAD :] = dv_ref[...].T.astype(BF16)
+
+
+def small_peer(dz, dh):
+    return {
+        "z": lax.rem(lax.axis_index("z") + dz, 4),
+        "yh": lax.rem(lax.axis_index("yh") + dh, 2),
+    }
+
+
+SMALL_ALL = [(dz, dh) for dz in range(4) for dh in range(2) if dz or dh]
+FORWARD_PEERS = XY_PEERS + Z_PEERS + [sibling]
+FORWARD_PEERS += [functools.partial(small_peer, dz, 1) for dz in (1, 2, 3)]
+
+FORWARD_OUTS = [
+    ("m_qkv", (4, 192, WIDTH), BF16, VMEM),
+    ("m_out", (4, 64, WIDTH), BF16, VMEM),
+    ("m_down", (4, 176, WIDTH), BF16, ANY),
+    ("m_gate", (4, 176, WIDTH), BF16, ANY),
+    ("m_up", (4, 176, WIDTH), BF16, ANY),
+    ("x_own", (OWN, WIDTH), BF16, VMEM),
+    ("dy_own", (OWN, WIDTH), BF16, VMEM),
+    ("middle", (OWN, WIDTH), F32, VMEM),
+    ("norms", (8, WIDTH), F32, VMEM),
+    ("h1", (ROWS, WIDTH), BF16, VMEM),
+    ("h2", (ROWS, WIDTH), BF16, VMEM),
+    ("dy", (ROWS, WIDTH), BF16, ANY),
+    ("o_t", (4 * HEAD, ROWS), BF16, VMEM),
+    ("kept", (3 * HEAD, SEQ), BF16, VMEM),
+    ("wide", (HEAD, SEQ), F32, VMEM),
+    ("lse", (1, SEQ), F32, VMEM),
+    ("seg_row", (1, SEQ), F32, VMEM),
+    ("seg_col", (SEQ, 1), F32, VMEM),
+]
+FORWARD_SCRATCH = [
+    ("small", (4, 2, 16, 640), BF16),
+    ("near_x", (OWN, WIDTH), BF16),
+    ("near_dy", (OWN, WIDTH), BF16),
+    ("far_x", (OWN, WIDTH), BF16),
+    ("far_dy", (OWN, WIDTH), BF16),
+    ("h1_own", (OWN, WIDTH), BF16),
+    ("h2_own", (OWN, WIDTH), BF16),
+    ("held_qkv", (3, 128, 1024), BF16),
+    ("held_gu", (128, 2, 2816), BF16),
+    ("turned", (2816, 128), F32),
+    ("cut_qkv", (4, 192, 128), BF16),
+    ("cut_gate", (4, 176, 128), BF16),
+    ("cut_up", (4, 176, 128), BF16),
+    ("p_qkv", (192, 512), BF16),
+    ("p_out", (64, 512), BF16),
+    ("p_down", (176, 512), BF16),
+    ("p_gate", (176, 512), BF16),
+    ("p_up", (176, 512), BF16),
+    ("bias", (4, 192, 1), F32),
+    ("qkv_t", (12 * HEAD, ROWS), BF16),
+    ("item", (3 * HEAD, SEQ), BF16),
+    ("out", (HEAD, SEQ), BF16),
+    ("o_rows", (ROWS, 4 * HEAD), BF16),
+    ("give", (4, OWN, WIDTH), BF16),
+    ("other", (4, OWN, WIDTH), BF16),
+    ("own", (4, OWN, WIDTH), F32),
+    ("total", (3, OWN, WIDTH), BF16),
+    ("arrived", (3, OWN, WIDTH), BF16),
+]
+
+
+class Refs:
+    pass
+
+
+def forward_kernel(*refs):
+    r = Refs()
+    names = ["tokens", "cotangent", "packed", "w_qkv", "w_out", "w_down", "w_gate_up", "cos", "sin"]
+    names += [o[0] for o in FORWARD_OUTS] + [o[0] for o in FORWARD_SCRATCH]
+    for name, ref in zip(names, refs):
+        setattr(r, name, ref)
+    engine = Engine(*refs[len(names) :])
+    z, x, yl, core, yh = place()
+    y = yh * 2 + yl
+    greet(FORWARD_PEERS)
+
+    load_qkv = engine.local(r.w_qkv.at[:, rows_at(x, 128)], r.held_qkv)
+    load_x = engine.local(r.tokens.at[rows_at(core, OWN)], r.near_x)
+    load_dy = engine.local(r.cotangent.at[rows_at(core, OWN)], r.near_dy)
+    swap_x = engine.send(r.tokens.at[rows_at(1 - core, OWN)], r.far_x, sibling())
+    smalls = [engine.send(r.packed, r.small.at[z, yh], small_peer(dz, dh)) for dz, dh in SMALL_ALL]
+    small_here = engine.local(r.packed, r.small.at[z, yh])
+    load_gu = engine.local(r.w_gate_up.at[rows_at(x, 128)], r.held_gu)
+    swap_dy = engine.send(r.cotangent.at[rows_at(1 - core, OWN)], r.far_dy, sibling())
+
+    def rows_of(n):
+        return lambda zz: rows_at((zz * 2 + core) * 2 + yl, n)
+
+    def slots_of(piece):
+        return lambda zz: piece.at[:, lanes(zz)]
+
+    load_qkv.wait()
+    for part in range(3):
+        r.turned[:1024, :] = r.held_qkv[part].astype(F32).T
+        for zz in range(4):
+            r.cut_qkv[zz, part * HEAD : (part + 1) * HEAD] = r.turned[rows_of(HEAD)(zz), :].astype(BF16)
+    pieces_qkv = send_pieces(engine, lambda zz: r.cut_qkv.at[zz], slots_of(r.p_qkv))
+
+    stays = core == yh
+    load_x.wait()
+    swap_x.wait_recv()
+    x_rows = spread(jnp.where(stays, r.near_x[...].astype(F32), r.far_x[...].astype(F32)))
+    r.x_own[...] = x_rows.astype(BF16)
+    small_here.wait()
+    for copy in smalls:
+        copy.wait_recv()
+    parts = [r.small[zz, 0].astype(F32) for zz in range(4)]
+    r.norms[...] = jnp.concatenate(
+        [parts[zz][:8, xx * 128 : (xx + 1) * 128] for xx in range(4) for zz in range(4)], axis=1
+    )
+    h1_full, _, _ = layer_norm(x_rows, r.norms[0:1], r.norms[2:3])
+    r.h1_own[...] = h1_full.astype(BF16)
+    tokens_h1 = gather_tokens(engine, r.h1_own, r.h1)
+    next(tokens_h1)
+
+    for copy in pieces_qkv[1:]:
+        copy.wait_recv()
+    pieces_qkv[0].wait()
+    weight_qkv = gather_weight(engine, r.p_qkv, r.m_qkv)
+    next(weight_qkv)
+    pieces_out = send_pieces(engine, lambda zz: r.w_out.at[rows_of(64)(zz), lanes(x)], slots_of(r.p_out))
+
+    lane_at = lax.broadcasted_iota(jnp.int32, (64, 128), 1)
+    for h in range(2):
+        table = jnp.concatenate([r.small[zz, h, :, 512:].astype(F32) for zz in range(4)], axis=0)
+        for j in range(2):
+            for part in range(3):
+                picked = jnp.where(lane_at == (z * 2 + core) * 6 + j * 3 + part, table, 0.0)
+                r.bias[h * 2 + j, part * HEAD : (part + 1) * HEAD] = jnp.sum(picked, axis=1, keepdims=True)
+    marks = r.small[x, 0, :, :512].astype(F32)
+    marks = [marks[4 + i : 5 + i, k * 128 : (k + 1) * 128] for i in range(4) for k in range(4)]
+    r.seg_row[...] = jnp.concatenate(marks, axis=1)
+    marks = jnp.concatenate(marks, axis=0).T
+    r.seg_col[...] = jnp.concatenate([marks[:, k : k + 1] for k in range(16)], axis=0)
+
+    next(weight_qkv)
+    load_gu.wait()
+    r.turned[...] = r.held_gu[:, 0, :].astype(F32).T
+    for zz in range(4):
+        r.cut_gate[zz] = r.turned[rows_of(176)(zz), :].astype(BF16)
+    next(tokens_h1)
+    next(weight_qkv)
+    pieces_gate = send_pieces(engine, lambda zz: r.cut_gate.at[zz], slots_of(r.p_gate))
+    pieces_down = send_pieces(engine, lambda zz: r.w_down.at[rows_of(176)(zz), lanes(x)], slots_of(r.p_down))
+    r.turned[...] = r.held_gu[:, 1, :].astype(F32).T
+    for zz in range(4):
+        r.cut_up[zz] = r.turned[rows_of(176)(zz), :].astype(BF16)
+    pieces_up = send_pieces(engine, lambda zz: r.cut_up.at[zz], slots_of(r.p_up))
+
+    def start_weight(pieces, piece, matrix):
+        pieces[0].wait()
+        for copy in pieces[1:]:
+            copy.wait_recv()
+        thread = gather_weight(engine, piece, matrix)
+        next(thread)
+        return thread
+
+    weight_out = start_weight(pieces_out, r.p_out, r.m_out)
+    load_dy.wait()
+    swap_dy.wait_recv()
+    dy_rows = jnp.where(stays, r.near_dy[...].astype(F32), r.far_dy[...].astype(F32))
+    r.dy_own[...] = spread(dy_rows).astype(BF16)
+    finish(tokens_h1)
+    finish(weight_qkv)
+
+    place_here = lanes(x * 4 + yl * 2 + yh)
+    to_items, stay = [], None
+    for dy in (2, 1, 3, 0):
+        ty = lax.rem(y + dy, 4)
+        rows = rows_at(ty, 3 * HEAD)
+        r.qkv_t[rows, :] = (dot(r.m_qkv[ty], r.h1[...], (1, 1)) + r.bias[ty]).astype(BF16)
+        for dx in (2, 1, 3, 0):
+            block = r.qkv_t.at[rows, lanes(lax.rem(x + dx, 4))]
+            if dx or dy:
+                to_items.append(engine.send(block, r.item.at[:, place_here], xy_peer(dx, dy)))
+            else:
+                stay = engine.local(block, r.item.at[:, place_here])
+    tokens_dy = gather_tokens(engine, r.dy_own, r.dy)
+    next(tokens_dy)
+    next(weight_out)
+    stay.wait()
+    for copy in to_items:
+        copy.wait_recv()
+    next(weight_out)
+    weight_down = start_weight(pieces_down, r.p_down, r.m_down)
+    weight_gate = start_weight(pieces_gate, r.p_gate, r.m_gate)
+    attend(r.item, r.seg_row, r.seg_col, r.cos, r.sin, r.out, r.wide, r.lse, r.kept)
+    back = return_items(engine, r.out, r.o_t, HEAD)
+    next(weight_down)
+    next(tokens_dy)
+    finish(weight_out)
+    back[-1].wait()
+    for copy in back[:-1]:
+        copy.wait_recv()
+
+    r.o_rows[...] = r.o_t[...].astype(F32).T.astype(BF16)
+    matrix = r.m_out[...].reshape(4 * HEAD, WIDTH)
+    to_core = []
+    for i in range(4):
+        base = lax.rem(z + 1 + i, 4) * 2
+        r.give[i] = dot(r.o_rows[rows_at(base + 1 - core, OWN), :], matrix, (1, 0)).astype(BF16)
+        to_core.append(engine.send(r.give.at[i], r.other.at[i], sibling()))
+        r.own[i] = dot(r.o_rows[rows_at(base + core, OWN), :], matrix, (1, 0))
+    to_z = []
+    for i in range(3):
+        to_core[i].wait_recv()
+        r.total[i] = (r.own[i] + r.other[i].astype(F32)).astype(BF16)
+        to_z.append(engine.send(r.total.at[i], r.arrived.at[i], z_peer(i + 1)))
+    next(weight_gate)
+    next(weight_down)
+    weight_up = start_weight(pieces_up, r.p_up, r.m_up)
+    to_core[3].wait_recv()
+    r.middle[...] = x_rows + r.own[3] + r.other[3].astype(F32)
+    for copy, arrived in zip(to_z, range(3)):
+        copy.wait_recv()
+        r.middle[...] += r.arrived[arrived].astype(F32)
+
+    h2_full, _, _ = layer_norm(r.middle[...], r.norms[1:2], r.norms[3:4])
+    r.h2_own[...] = h2_full.astype(BF16)
+    tokens_h2 = gather_tokens(engine, r.h2_own, r.h2)
+    next(tokens_h2)
+    next(weight_up)
+    next(weight_gate)
+    finish(weight_down)
+    next(weight_up)
+    next(tokens_h2)
+    finish(weight_gate)
+    finish(tokens_dy)
+    finish(weight_up)
+    finish(tokens_h2)
+    sent = smalls + to_items + back[:-1] + to_core + to_z + [swap_x, swap_dy]
+    for pieces in (pieces_qkv, pieces_out, pieces_gate, pieces_down, pieces_up):
+        sent += pieces[1:]
+    for copy in sent:
+        copy.wait_send()
+
+
+def forward(tokens, cotangent, packed, w_qkv, w_out, w_down, w_gate_up, cosine, sine):
+    values = pl.pallas_call(
+        forward_kernel,
+        out_shape=[jax.ShapeDtypeStruct(o[1], o[2]) for o in FORWARD_OUTS],
+        in_specs=[ANY] * 7 + [VMEM] * 2,
+        out_specs=[o[3] for o in FORWARD_OUTS],
+        scratch_shapes=[pltpu.VMEM(shape, dtype) for _, shape, dtype in FORWARD_SCRATCH] + semaphores(160, 24),
+        compiler_params=pltpu.CompilerParams(
+            collective_id=1, has_side_effects=True, vmem_limit_bytes=50 * 2**20
+        ),
+        name="forward",
+    )(tokens, cotangent, packed, w_qkv, w_out, w_down, w_gate_up, cosine, sine)
+    result = Refs()
+    for (name, *_), value in zip(FORWARD_OUTS, values):
+        setattr(result, name, value)
+    return result
 
 
 def assemble_kernel(mlp_ref, attn_ref, gu_ref, down_ref, qkv_ref, out_ref, turned):
@@ -893,84 +1027,28 @@
 
 
 def local(tokens, segments, w_qkv, b_qkv, w_out, w_gate_up, w_down, norm_gains, norm_shifts, cotangent):
-    z, x, yl, core, yh = place()
+    z, _, _, core, yh = place()
 
     def pick(values, axis, index):
         return lax.dynamic_index_in_dim(values, index, axis, keepdims=False)
 
-    packed = jnp.concatenate(
-        [
-            norm_gains,
-            norm_shifts,
-            jnp.pad(b_qkv.reshape(-1), (0, 256)).reshape(2, 512),
-            jnp.zeros((10, 512), BF16),
-        ],
-        axis=0,
-    )
-    token_block, grad_block = tokens[0], cotangent[0]
-    got = exchange(
-        "start",
-        1,
-        [
-            swap_op(token_block),
-            swap_op(grad_block),
-            small_op(packed),
-            z_gather_op(segments.reshape(16, 128)),
-            weight_columns_op(w_qkv.transpose(1, 0, 2), HEAD, False),
-            weight_rows_op(w_out, 64),
-            weight_rows_op(w_down, 176),
-            weight_columns_op(w_gate_up, 176, True),
-        ],
-        48,
-        16,
-    )
-    (swapped_x,), (swapped_dy,), (small,), (all_segments,) = got[:4]
-    (z_qkv,), (z_out,), (z_down,), (z_gate, z_up) = got[4:]
-
-    stays = core == yh
-    x_own = jnp.where(stays, lax.dynamic_slice_in_dim(token_block, core * OWN, OWN, 0), swapped_x).astype(F32)
-    dy_own = jnp.where(stays, lax.dynamic_slice_in_dim(grad_block, core * OWN, OWN, 0), swapped_dy)
-    wide = small[:, 0, :4].transpose(1, 0, 2).reshape(4, WIDTH).astype(F32)
-    gains, shifts = wide[:2], wide[2:]
-    bias = small[:, :, 4:6].reshape(4, 2, 1024)[:, :, :768].reshape(4, 2, 3, 4, 2, 2, 16)
-    bias = pick(pick(bias, 3, z), 3, core)
-    bias = bias.transpose(1, 3, 2, 0, 4).reshape(768, 1).astype(F32)
-    item_segments = pick(all_segments, 0, x).reshape(1, SEQ)
-    segment_column = item_segments.reshape(SEQ, 1)
+    rows = jnp.concatenate(
+        [norm_gains, norm_shifts, segments.astype(BF16).reshape(4, 512), jnp.zeros((8, 512), BF16)], axis=0
+    )
+    biases = b_qkv.reshape(3, 4, 2, 2, 16).transpose(4, 1, 2, 3, 0).reshape(16, 48)
+    packed = jnp.concatenate([rows, jnp.pad(biases, ((0, 0), (0, 80)))], axis=1)
     cosine, sine = rotation_tables()
-
-    h1_full, normed_a, rstd_a = layer_norm(x_own, gains[:1], shifts[:1])
-    (m_qkv,), (h1,) = exchange(
-        "gather_h1", 2, [weight_xy_op(z_qkv), token_gather_op(h1_full.astype(BF16))], 64, 8
-    )
-    m_qkv = m_qkv.reshape(768, WIDTH)
-    qkv_t = (dot(m_qkv, h1, (1, 1)) + bias).astype(BF16)
-
-    attention, (dy,), (m_out,), (m_down,) = exchange(
-        "attention",
-        3,
-        [
-            attention_op(qkv_t, item_segments, segment_column, cosine, sine),
-            token_gather_op(dy_own),
-            weight_xy_op(z_out),
-            weight_xy_op(z_down),
-        ],
-        144,
-        16,
-    )
-    o_t, kept, o_wide, lse = attention
-    m_out = m_out.reshape(256, WIDTH)
-    m_down = m_down.reshape(704, WIDTH)
-
-    part = dot(o_t, m_out, (0, 0)).astype(BF16)
-    (m_gate,), (attn_own,) = exchange("sum_out", 4, [weight_xy_op(z_gate), token_scatter_op(part)], 64, 12)
-    middle = x_own + attn_own
-    h2_full, normed_b, rstd_b = layer_norm(middle, gains[1:], shifts[1:])
-    (m_up,), (h2,) = exchange(
-        "gather_h2", 5, [weight_xy_op(z_up), token_gather_op(h2_full.astype(BF16))], 64, 8
-    )
-    m_gate = m_gate.reshape(704, WIDTH)
-    m_up = m_up.reshape(704, WIDTH)
+    f = forward(
+        tokens[0], cotangent[0], packed, w_qkv.transpose(1, 0, 2), w_out, w_down, w_gate_up, cosine, sine
+    )
+    gains, shifts = f.norms[:2], f.norms[2:4]
+    x_own, dy_own, middle = f.x_own.astype(F32), f.dy_own, f.middle
+    h1, h2, dy, o_t, kept, o_wide, lse = f.h1, f.h2, f.dy, f.o_t, f.kept, f.wide, f.lse
+    item_segments, segment_column = f.seg_row, f.seg_col
+    m_qkv, m_out, m_down = f.m_qkv.reshape(768, WIDTH), f.m_out.reshape(256, WIDTH), f.m_down.reshape(704, WIDTH)
+    m_gate, m_up = f.m_gate.reshape(704, WIDTH), f.m_up.reshape(704, WIDTH)
+    _, normed_a, rstd_a = layer_norm(x_own, gains[:1], shifts[:1])
+    _, normed_b, rstd_b = layer_norm(middle, gains[1:], shifts[1:])
 
     gate, up = dot(m_gate, h2, (1, 1)), dot(m_up, h2, (1, 1))
     sigmoid = jax.nn.sigmoid(gate)
@@ -988,18 +1066,18 @@
     g_gate, g_up, g_down = weight_grad(d_gate, h2), weight_grad(d_up, h2), weight_grad(act, dy)
     (dh2_own,), (mlp_own,), first_gate, first_down = exchange(
         "sum_mlp",
-        6,
+        2,
         [token_scatter_op(back_part), token_scatter_op(mlp_part), grad_first_op(g_gate), grad_first_op(g_down)],
         48,
         24,
     )
 
-    out_own = (middle + mlp_own).astype(BF16)
+    out_own = spread((middle + mlp_own).astype(BF16))
     back_b, gain_b, shift_b = norm_back(dh2_own, normed_b, rstd_b, gains[1:])
     d_middle = dy_own.astype(F32) + back_b
     (dz,), first_up, (z_down,) = exchange(
         "gather_dz",
-        7,
+        3,
         [token_gather_op(d_middle.astype(BF16)), grad_first_op(g_up), grad_rest_op(*first_down)],
         48,
         24,
@@ -1008,7 +1086,7 @@
     g_out = weight_grad(o_t, dz)
     (d_qkv,), (z_gate,), (z_up,), (layer_out,) = exchange(
         "attention_back",
-        8,
+        4,
         [
             attention_back_op(d_o, kept, o_wide, lse, item_segments, segment_column, cosine, sine),
             grad_rest_op(*first_gate),
@@ -1025,15 +1103,15 @@
     g_qkv = weight_grad(d_qkv, h1)
     g_bias = jnp.sum(d_qkv.astype(F32), axis=1)
     (dh1_own,), first_qkv, first_out = exchange(
-        "sum_dh1", 9, [token_scatter_op(back_part), grad_first_op(g_qkv), grad_first_op(g_out)], 48, 24
+        "sum_dh1", 5, [token_scatter_op(back_part), grad_first_op(g_qkv), grad_first_op(g_out)], 48, 24
     )
     back_a, gain_a, shift_a = norm_back(dh1_own, normed_a, rstd_a, gains[:1])
-    grad_own = (d_middle + back_a).astype(BF16)
-    norms = jnp.pad(jnp.stack([gain_a, gain_b, shift_a, shift_b]), ((0, 4), (0, 0)))
+    grad_own = spread((d_middle + back_a).astype(BF16))
+    norms = spread(jnp.pad(jnp.stack([gain_a, gain_b, shift_a, shift_b]), ((0, 4), (0, 0))))
     first_attn = [jnp.concatenate([a, b], axis=-2) for a, b in zip(first_qkv, first_out)]
     (attn_all,), (norm_sum, bias_all), (grad_tokens,) = exchange(
         "finish",
-        10,
+        6,
         [
             grad_rest_op(*first_attn, gather=True),
             small_sum_op(norms, jnp.pad(g_bias, (0, 256)).reshape(8, 128)),

time: 431 us -> 408 us (0.947)
  Pallas kernels: 357 us -> 334 us
    pallas_call x10 -> x5, Pallas kernels: 343 us -> 204 us  [exchange(): pl.pallas_call(kernel, out_shape=[jax.ShapeDtypeStruct(o[0], o[1]) for op...]
    pallas_call x0 -> x1, Pallas kernels: none -> 115 us  [forward(): pl.pallas_call(forward_kernel, out_shape=[jax.ShapeDtypeStruct(o[1], o[2]...]
    dot_general x15 -> x13, matrix products: 36.5 us -> 32.5 us  [dot(): lax.dot_general(a, b, ((dims[:1], dims[1:]), ((), ())), preferred_element...]
    unnamed x36 -> x97, local copies, waits for them, and re-layouts: 9.87 us -> 10.8 us
  transfers between devices with their start and end apart: 1 -> 1, of which waited for: 0 -> 0; matrix products, arithmetic and copies ran while one was open for 3% -> 2% of each run, Pallas kernels for 23% -> 24%
where the time goes in v3:
time: 408 us; the launch traced here: 404 us
  Pallas kernels  334 us (82%)
  matrix products  32.5 us (8%)
  between operations  15.1 us (4%)
  local copies, waits for them, and re-layouts  14.6 us (4%)
  other arithmetic  8.36 us (2%)
    pallas_call x5, Pallas kernels, exchange(): pl.pallas_call(kernel, out_shape=[jax.ShapeDtypeStruct(o[0], o[1]) for op...  204 us
    pallas_call x1, Pallas kernels, forward(): pl.pallas_call(forward_kernel, out_shape=[jax.ShapeDtypeStruct(o[1], o[2]...  115 us
    dot_general x13, matrix products, dot(): lax.dot_general(a, b, ((dims[:1], dims[1:]), ((), ())), preferred_element...  32.5 us
    pallas_call x1, Pallas kernels, assemble(): pl.pallas_call(assemble_kernel, grid=(4,), in_specs=[pl.BlockSpec((1, 4,...  14.1 us
    unnamed x97, local copies, waits for them, and re-layouts  10.8 us
  transfers between devices with their start and end apart: 1, of which 0 were waited for; matrix products, arithmetic and copies ran while one was open for 2% of the time, Pallas kernels for 24%

profile of v3, /device:TPU:1, one launch (start us, length us, event | category | flops | bytes accessed | tf_op | source)
XLA Modules:
  0.0 404.4 jit_solution(13627881366969062313)
XLA Ops:
  7.2 0.0 all-gather.3.cloned.1.call-start
  7.2 0.7 copy.31
  8.0 0.1 copy.25
  8.1 0.7 convert_reduce_fusion.2
  8.8 0.3 multiply_sine_fusion
  9.1 0.7 fusion.14.refs_2_
  9.9 0.0 copy-start.5
  9.9 1.0 copy-done.5
  10.9 1.0 copy-done.6
  11.9 115.3 %forward.1 = (bf16[4,192,2048]{2,1,0:T(8,128)(2,1)}, bf16[4,64,2048]{2,1,0:T(8,128)(2,1)}, bf16[4,176,2048]{2,1,0:T(8,128)(2,1)}, bf16[4,176,2048]{2,1,0:T(8,128...) custom-call(bf16[128,2048]{1,0:T(8,128)(2,1)S(1)} %bitcast.71, ...), custom_call_target="tpu_custom_call" | custom-call | tf_op jit(solution)/shard_map/forward/pallas_call | solution.py:928
  127.2 0.0 copy-start.3
  127.3 0.0 copy-start.11
  127.3 4.7 %fusion.19 = f32[704,512]{1,0:T(8,128)S(1)} fusion(bf16[704,2048]{1,0:T(8,128)(2,1)} %bitcast.82, bf16[512,2048]{1,0:T(8,128)(2,1)} %get-tuple-element.59), kind=kOutput, calls=%fused_computation.117 | convolution fusion | flops 1476395008 | bytes 6422528 | tf_op jit(solution)/shard_map/dot_general | solution.py:594
  132.0 1.7 fusion.18
  133.7 0.1 copy-done.19
  133.8 0.6 copy-done.22
  134.5 2.3 multiply_convert_fusion
  136.7 1.8 fusion.20
  138.6 3.2 convolution_convert_fusion.3
  141.8 3.2 convolution_convert_fusion.2
  145.1 3.2 convolution_convert_fusion.5.refs_1_
  148.2 3.4 convolution_convert_fusion.1
  151.7 2.0 add_convert_fusion.refs_0_
  153.7 0.6 reduce_sum.118
  154.3 0.7 broadcast_multiply_fusion.4
  155.0 0.2 multiply_reduce_fusion.2
  155.2 1.5 fusion.16
  156.7 38.5 %sum_mlp.1 = (f32[64,2048]{1,0:T(8,128)S(1)}, f32[64,2048]{1,0:T(8,128)S(1)}, bf16[96,2048]{1,0:T(8,128)(2,1)S(1)}, bf16[4,80,512]{2,1,0:T(8,128)(2,1)S(1)}, bf1...) custom-call(bf16[512,2048]{1,0:T(8,128)(2,1)S(1)} %add_convert_fusion.refs_0_, ...), custom_call_target="tpu_custom_call" | custom-call | tf_op jit(solution)/shard_map/sum_mlp/pallas_call | solution.py:144
  195.2 0.9 multiply_reduce_fusion
  196.4 1.1 fusion.15
  197.5 28.7 %gather_dz.1 = (bf16[512,2048]{1,0:T(8,128)(2,1)S(1)}, bf16[96,2048]{1,0:T(8,128)(2,1)S(1)}, bf16[4,80,512]{2,1,0:T(8,128)(2,1)S(1)}, bf16[4,176,128]{2,1,0:T(8,128)(2,1)S(1)}) custom-call(bf16[64,2048]{1,0:T(8,128)(2,1)S(1)} %get-tuple-element.107.refs_0_, bf16[4,176,2048]{2,1,0:T(8,128)(2,1)} %bitcast.79, bf16[96,2048]{1,0:T(8,128)(2,1)S(1)} %get-tuple-element.64.refs_2_, ...), custom_call_target="tpu_custom_call" | custom-call | tf_op jit(solution)/shard_map/gather_dz/pallas_call | solution.py:144
  226.2 0.0 copy-start.4
  226.2 0.9 convolution_convert_fusion.7.refs_0_
  227.1 0.3 copy-done.2
  227.4 0.2 copy-done.4
  227.6 0.1 copy-done.8
  227.8 40.3 %attention_back.1 = (bf16[768,512]{1,0:T(8,128)(2,1)S(1)}, bf16[4,176,128]{2,1,0:T(8,128)(2,1)S(1)}, bf16[4,176,128]{2,1,0:T(8,128)(2,1)S(1)}, bf16[128,2048]{1,0:T(8,128)(2,1)S(1)}) custom-call(bf16[256,512]{1,0:T(8,128)(2,1)S(1)} %convolution_convert_fusion.7.refs_0_, bf16[192,2048]{1,0:T(8,128)(2,1)S(1)} %copy-done.4, f32[64,2048]{1,0:T(8,128)S(1)} %copy-done.8, ...), custom_call_target="tpu_custom_call" | custom-call | tf_op jit(solution)/shard_map/attention_back/pallas_call | solution.py:144
  268.1 0.8 copy-done.9
  268.9 0.8 pad_maximum_fusion
  269.8 0.0 all-gather.3.cloned.1.call-update
  269.8 0.7 convolution_convert_fusion.6
  270.5 0.9 copy-done.21
  271.4 3.5 convolution_convert_fusion
  274.9 1.9 convolution_convert_fusion.4.refs_0_
  276.8 0.0 copy-start.18
  276.8 52.1 %sum_dh1.1 = (f32[64,2048]{1,0:T(8,128)S(1)}, bf16[96,2048]{1,0:T(8,128)(2,1)S(1)}, bf16[4,96,512]{2,1,0:T(8,128)(2,1)S(1)}, bf16[32,2048]{1,0:T(8,128)(2,1)S(1)}, bf16[4,32,512]{2,1,0:T(8,128)(2,1)S(1)}) custom-call(bf16[512,2048]{1,0:T(8,128)(2,1)S(1)} %convolution_convert_fusion.4.refs_0_, bf16[4,192,2048]{2,1,0:T(8,128)(2,1)} %bitcast.77, ...), custom_call_target="tpu_custom_call" | custom-call | tf_op jit(solution)/shard_map/sum_dh1/pallas_call | solution.py:144
  328.8 0.0 copy-start.15
  328.8 0.0 copy-start.16
  328.9 0.0 copy-start.14
  328.9 0.2 convert_reduce_fusion
  329.1 0.2 fusion.12
  329.4 0.1 copy-done.15
  329.5 0.3 fusion.7
  330.1 0.3 fusion.11
  330.8 44.8 %finish.1 = (bf16[16,4,256,128]{3,2,1,0:T(8,128)(2,1)S(1)}, f32[8,512]{1,0:T(8,128)S(1)}, f32[8,8,128]{2,1,0:T(8,128)S(1)}, bf16[128,2048]{1,0:T(8,128)(2,1)S(1)}) custom-call(bf16[128,2048]{1,0:T(8,128)(2,1)S(1)} %pad_maximum_fusion.1.refs_0_, bf16[4,128,512]{2,1,0:T(8,128)(2,1)S(1)} %pad_maximum_fusion.2.refs_1_, ...), custom_call_target="tpu_custom_call" | custom-call | tf_op jit(solution)/shard_map/finish/pallas_call | solution.py:144
  375.6 0.0 copy-start
  375.6 2.0 copy-done
  377.6 0.2 reshape.145
  377.9 0.6 copy.26
  378.5 0.6 fusion.17
  379.1 1.1 bitcast_convert_fusion
  380.2 2.2 copy-done.1
  382.4 14.1 %assemble.1 = (f32[512,2,2816]{2,1,0:T(2,128)}, f32[2816,512]{1,0:T(8,128)}, f32[3,512,1024]{2,1,0:T(8,128)}, f32[1024,512]{1,0:T(8,128)}) custom-call(bf16[4,4,4,528,128]{4,3,2,1,0:T(8,128)(2,1)} %bitcast.75, bf16[4,4,4,256,128]{4,3,2,1,0:T(8,128)(2,1)S(1)} %bitcast.69), custom_call_target="tpu_custom_call" | custom-call | tf_op jit(solution)/shard_map/assemble/pallas_call | solution.py:977
  396.5 0.8 copy.78
  (97 shorter events, 0.8 us)
Async XLA Ops:
  7.2 373.0 %all-gather.3.cloned.1.call-start = ((), (), s32[]{:S(2)}) async-start(), calls=%async_computation | async-start | bytes 9191424 | tf_op jit(solution)/shard_map/all_gather | solution.py:1100
  9.9 1.0 copy-start.5
  10.9 1.0 copy-start.6
  127.2 4.7 %copy-start.3 = (bf16[192,2048]{1,0:T(8,128)(2,1)}, bf16[192,2048]{1,0:T(8,128)(2,1)S(1)}, u32[]{:S(2)}) copy-start(bf16[192,2048]{1,0:T(8,128)(2,1)S(1)} %get-tuple-element.67.refs_1_) | copy-start | bytes 2359300
  127.2 4.7 %copy-start.7 = (f32[64,2048]{1,0:T(8,128)}, f32[64,2048]{1,0:T(8,128)S(1)}, u32[]{:S(2)}) copy-start(f32[64,2048]{1,0:T(8,128)S(1)} %get-tuple-element.68.refs_2_) | copy-start | bytes 1572868
  127.3 4.7 %copy-start.11 = (f32[8,2048]{1,0:T(8,128)}, f32[8,2048]{1,0:T(8,128)S(1)}, u32[]{:S(2)}) copy-start(f32[8,2048]{1,0:T(8,128)S(1)} %get-tuple-element.62) | copy-start | bytes 196612
  127.3 4.7 %copy-start.20 = (bf16[4,176,2048]{2,1,0:T(8,128)(2,1)S(1)}, bf16[4,176,2048]{2,1,0:T(8,128)(2,1)}, u32[]{:S(2)}) copy-start(bf16[4,176,2048]{2,1,0:T(8,128)(2,1)} %get-tuple-element.56) | copy-start | bytes 8650756
  127.3 4.7 %copy-start.23 = (bf16[512,2048]{1,0:T(8,128)(2,1)S(1)}, bf16[512,2048]{1,0:T(8,128)(2,1)}, u32[]{:S(2)}) copy-start(bf16[512,2048]{1,0:T(8,128)(2,1)} %get-tuple-element.57) | copy-start | bytes 6291460
  132.0 1.8 copy-start.19
  132.0 2.5 copy-start.22
  134.5 2.3 copy-start.13
  197.5 28.7 %copy-start.24 = (bf16[4,64,2048]{2,1,0:T(8,128)(2,1)S(1)}, bf16[4,64,2048]{2,1,0:T(8,128)(2,1)}, u32[]{:S(2)}) copy-start(bf16[4,64,2048]{2,1,0:T(8,128)(2,1)} %get-tuple-element.54) | copy-start | bytes 3145732
  226.2 1.2 copy-start.2
  226.2 1.4 copy-start.4
  226.2 1.6 copy-start.8
  268.1 0.8 copy-start.9
  269.8 1.6 copy-start.21
  271.4 3.5 copy-start.12
  276.8 52.4 %copy-start.18 = (f32[64]{0:T(128)S(1)}, f32[64]{0:T(128)}, u32[]{:S(2)}) copy-start(f32[64]{0:T(128)} %get-tuple-element.119) | copy-start | bytes 772
  328.8 0.7 copy-start.15
  328.8 1.0 copy-start.16
  328.9 1.0 copy-start.17
  328.9 1.2 copy-start.14
  375.6 2.0 copy-start
  380.2 2.2 copy-start.1
  382.4 14.1 %copy-start.10 = (bf16[128,2048]{1,0:T(8,128)(2,1)S(1)}, bf16[128,2048]{1,0:T(8,128)(2,1)}, u32[]{:S(2)}) copy-start(bf16[128,2048]{1,0:T(8,128)(2,1)} %copy-done.9) | copy-start | bytes 1572868
Sparse Core Ops, SparseCore 0:
  269.9 82.6 all-gather.2

commit v4 on v3

--- a/solution.py
+++ b/solution.py
@@ -89,11 +89,6 @@
         return copy
 
 
-class Op:
-    def __init__(self, ins, outs, peers, body, scratch=()):
-        self.ins, self.outs, self.peers, self.body, self.scratch = ins, outs, peers, body, scratch
-
-
 def greet(peers):
     barrier = pltpu.get_barrier_semaphore()
     for peer in peers:
@@ -107,57 +102,6 @@
         pltpu.SemaphoreType.DMA((n_remote,)),
         pltpu.SemaphoreType.DMA((n_local,)),
     ]
-
-
-def exchange(name, number, ops, n_remote, n_local):
-    peers = []
-    for op in ops:
-        for peer in op.peers:
-            if peer not in peers:
-                peers.append(peer)
-
-    def kernel(*refs):
-        refs = list(refs)
-
-        def take(count):
-            taken = refs[:count]
-            del refs[:count]
-            return taken
-
-        ins = [take(len(op.ins)) for op in ops]
-        outs = [take(len(op.outs)) for op in ops]
-        scratch = [take(len(op.scratch)) for op in ops]
-        engine = Engine(*refs)
-        greet(peers)
-        running = [op.body(engine, *i, *o, *s) for op, i, o, s in zip(ops, ins, outs, scratch)]
-        while running:
-            left = []
-            for item in running:
-                try:
-                    next(item)
-                    left.append(item)
-                except StopIteration:
-                    pass
-            running = left
-
-    given = [i if isinstance(i, tuple) else (i, ANY) for op in ops for i in op.ins]
-    results = pl.pallas_call(
-        kernel,
-        out_shape=[jax.ShapeDtypeStruct(o[0], o[1]) for op in ops for o in op.outs],
-        in_specs=[spec for _, spec in given],
-        out_specs=[o[2] if len(o) > 2 else ANY for op in ops for o in op.outs],
-        scratch_shapes=[s for op in ops for s in op.scratch]
-        + semaphores(n_remote, n_local),
-        compiler_params=pltpu.CompilerParams(
-            collective_id=number, has_side_effects=True, vmem_limit_bytes=48 * 2**20
-        ),
-        name=name,
-    )(*[value for value, _ in given])
-    split = []
-    for op in ops:
-        split.append(tuple(results[: len(op.outs)]))
-        results = results[len(op.outs) :]
-    return split
 
 
 def spread(values):
@@ -238,46 +182,6 @@
         copy.wait()
 
 
-def token_gather_op(block):
-    return Op([block], [((ROWS, WIDTH), block.dtype)], Z_PEERS + [sibling], gather_tokens)
-
-
-def token_scatter_op(partial):
-    def body(engine, src, dst, own, other, arrived):
-        z, core = lax.axis_index("z"), lax.axis_index("core")
-        pairs = []
-        for i in range(4):
-            base = lax.rem(z + 1 + i, 4) * 2
-            there = engine.send(src.at[rows_at(base + 1 - core, OWN)], other.at[i], sibling())
-            here = engine.local(src.at[rows_at(base + core, OWN)], own.at[i])
-            pairs.append((there, here))
-        yield
-        sent = []
-        for i in range(3):
-            pairs[i][0].wait_recv()
-            pairs[i][1].wait()
-            own[i] = (own[i].astype(F32) + other[i].astype(F32)).astype(BF16)
-            sent.append(engine.send(own.at[i], arrived.at[i], z_peer(i + 1)))
-        yield
-        pairs[3][0].wait_recv()
-        pairs[3][1].wait()
-        dst[...] = own[3].astype(F32) + other[3].astype(F32)
-        for i in range(3):
-            sent[i].wait_recv()
-            dst[...] += arrived[i].astype(F32)
-        for i in range(3):
-            sent[i].wait_send()
-        for there, _ in pairs:
-            there.wait_send()
-
-    scratch = (
-        pltpu.VMEM((4, OWN, WIDTH), BF16),
-        pltpu.VMEM((4, OWN, WIDTH), BF16),
-        pltpu.VMEM((3, OWN, WIDTH), BF16),
-    )
-    return Op([partial], [((OWN, WIDTH), F32, VMEM)], Z_PEERS + [sibling], body, scratch)
-
-
 def first_part(n):
     return (n // 2 + 15) // 16 * 16
 
@@ -305,33 +209,6 @@
     return copies
 
 
-def attention_back_op(d_o, kept, wide, lse, seg_row, seg_col, cosine, sine):
-    def body(engine, src, kept, wide, lse, row, col, cos, sin, dst, item, out, dk, dv):
-        copies = send_items(engine, src, item, HEAD)
-        yield
-        for copy in copies[:-1]:
-            copy.wait_recv()
-        copies[-1].wait()
-        yield
-        attend_back(kept, item, wide, lse, row, col, cos, sin, out, dk, dv)
-        for copy in copies[:-1]:
-            copy.wait_send()
-        back = return_items(engine, out, dst, 3 * HEAD)
-        yield
-        yield
-        for copy in back:
-            copy.wait()
-
-    scratch = (
-        pltpu.VMEM((HEAD, SEQ), BF16),
-        pltpu.VMEM((3 * HEAD, SEQ), BF16),
-        pltpu.VMEM((SEQ, HEAD), F32),
-        pltpu.VMEM((SEQ, HEAD), F32),
-    )
-    ins = [d_o] + [(value, VMEM) for value in (kept, wide, lse, seg_row, seg_col, cosine, sine)]
-    return Op(ins, [((12 * HEAD, ROWS), BF16)], XY_PEERS, body, scratch)
-
-
 def add_up(total, own, others, index, rows, width):
     def step(i, carry):
         here = (*index, rows_at(i, 16), slice(0, width))
@@ -344,135 +221,158 @@
     lax.fori_loop(0, rows // 16, step, 0)
 
 
-def grad_first_op(grad):
-    n = grad.shape[1]
-    cut = first_part(n)
+def scatter_tokens(engine, src, dst, own, other, arrived):
+    z, core = lax.axis_index("z"), lax.axis_index("core")
+    pairs = []
+    for i in range(4):
+        base = lax.rem(z + 1 + i, 4) * 2
+        there = engine.send(src.at[rows_at(base + 1 - core, OWN)], other.at[i], sibling())
+        here = engine.local(src.at[rows_at(base + core, OWN)], own.at[i])
+        pairs.append((there, here))
+    yield
+    sent = []
+    for i in range(3):
+        pairs[i][0].wait_recv()
+        pairs[i][1].wait()
+        own[i] = (own[i].astype(F32) + other[i].astype(F32)).astype(BF16)
+        sent.append(engine.send(own.at[i], arrived.at[i], z_peer(i + 1)))
+    yield
+    pairs[3][0].wait_recv()
+    pairs[3][1].wait()
+    dst[...] = own[3].astype(F32) + other[3].astype(F32)
+    for i in range(3):
+        sent[i].wait_recv()
+        dst[...] += arrived[i].astype(F32)
+    yield
+    for copy in sent:
+        copy.wait_send()
+    for there, _ in pairs:
+        there.wait_send()
+
+
+def scatter_product(engine, rows, matrix, dst, give, own, other, total, arrived):
+    z, core = lax.axis_index("z"), lax.axis_index("core")
+    to_core = []
+    for i in range(4):
+        base = lax.rem(z + 1 + i, 4) * 2
+        give[i] = dot(rows[rows_at(base + 1 - core, OWN), :], matrix, (1, 0)).astype(BF16)
+        to_core.append(engine.send(give.at[i], other.at[i], sibling()))
+        own[i] = dot(rows[rows_at(base + core, OWN), :], matrix, (1, 0))
+    to_z = []
+    for i in range(3):
+        to_core[i].wait_recv()
+        total[i] = (own[i] + other[i].astype(F32)).astype(BF16)
+        to_z.append(engine.send(total.at[i], arrived.at[i], z_peer(i + 1)))
+    yield
+    to_core[3].wait_recv()
+    dst[...] = own[3] + other[3].astype(F32)
+    for i in range(3):
+        to_z[i].wait_recv()
+        dst[...] += arrived[i].astype(F32)
+    yield
+    for copy in to_core + to_z:
+        copy.wait_send()
+
+
+def sum_first(engine, src, sum_y, sum_x, by_y, by_x, own_y, own_x):
+    n, cut = src.shape[1], sum_y.shape[0]
     rest = n - cut
     head, tail = pl.ds(0, cut), pl.ds(cut, rest)
-
-    def body(engine, src, sum_y, sum_x, by_y, by_x, own_y, own_x):
-        x = lax.axis_index("x")
-        y = lax.axis_index("yh") * 2 + lax.axis_index("yl")
-        copies = []
-        local = [engine.local(src.at[y, head], own_y), engine.local(src.at[:, tail, lanes(x, 512)], own_x)]
-        for d in (1, 2, 3):
-            ty, tx = y_peer(d), x_peer(d)
-            copies.append(engine.send(src.at[ty["yh"] * 2 + ty["yl"], head], by_y.at[d - 1], ty))
-            copies.append(engine.send(src.at[:, tail, lanes(tx["x"], 512)], by_x.at[d - 1], tx))
-        yield
-        for copy in local:
-            copy.wait()
-        yield
-        for copy in copies:
-            copy.wait_recv()
-        add_up(sum_y, own_y, by_y, (), cut, WIDTH)
-        for q in range(4):
-            add_up(sum_x, own_x, by_x, (q,), rest, 512)
-        for copy in copies:
-            copy.wait_send()
-
-    outs = [((cut, WIDTH), BF16, VMEM), ((4, rest, 512), BF16, VMEM)]
-    scratch = (
-        pltpu.VMEM((3, cut, WIDTH), BF16),
-        pltpu.VMEM((3, 4, rest, 512), BF16),
-        pltpu.VMEM((cut, WIDTH), BF16),
-        pltpu.VMEM((4, rest, 512), BF16),
-    )
-    return Op([grad], outs, X_PEERS + Y_PEERS, body, scratch)
-
-
-def grad_rest_op(sum_y, sum_x, gather=False):
-    cut, rest = sum_y.shape[0], sum_x.shape[1]
-    n = cut + rest
-
-    def body(engine, heads, tails, dst, by_x, by_y, own, total, *held):
-        x, yl, core = (lax.axis_index(a) for a in ("x", "yl", "core"))
-        y = lax.axis_index("yh") * 2 + yl
-        copies, local = [], [engine.local(tails.at[y], own.at[pl.ds(cut, rest)])]
-        local.append(engine.local(heads.at[:, lanes(x, 512)], own.at[pl.ds(0, cut)]))
-        for d in (1, 2, 3):
-            ty, tx = y_peer(d), x_peer(d)
-            copies.append(engine.send(tails.at[ty["yh"] * 2 + ty["yl"]], by_y.at[d - 1], ty))
-            copies.append(engine.send(heads.at[:, lanes(tx["x"], 512)], by_x.at[d - 1], tx))
-        yield
-        for copy in local:
-            copy.wait()
-        for copy in copies:
-            copy.wait_recv()
-        add_up(total.at[pl.ds(0, cut)], own.at[pl.ds(0, cut)], by_x, (), cut, 512)
-        add_up(total.at[pl.ds(cut, rest)], own.at[pl.ds(cut, rest)], by_y, (), rest, 512)
-        landing = held[0] if gather else dst
-        moved = send_pieces(engine, lambda z: total.at[:, lanes(z)], lambda z: landing.at[z])
-        for copy in copies:
-            copy.wait_send()
-        yield
-        for copy in moved:
-            copy.wait()
-        if not gather:
-            return
-
-        def slot(xx, ll, cc):
-            return (xx * 2 + ll) * 2 + cc
-
-        first, second = pl.ds(0, 2), pl.ds(2, 2)
-        me = slot(x, yl, core)
-        partner = {"yl": 1 - yl}
-        there = sibling()
-        done = [engine.local(landing, dst.at[me]), engine.send(landing, dst.at[me], there)]
-        to_y = engine.send(landing.at[first], dst.at[me, first], partner)
-        to_x = [engine.send(landing.at[second], dst.at[me, second], x_peer(d)) for d in (1, 2, 3)]
-        yield
-        done[0].wait()
-        final = []
-
-        def pass_on(index, part):
-            block = dst.at[index, part]
-            done.append(engine.send(block, block, there))
-
-        for d in (1, 2, 3):
-            block = dst.at[me, first]
-            final.append((slot(lax.rem(x + 4 - d, 4), yl, core), first, engine.send(block, block, x_peer(d))))
-        block = dst.at[me, second]
-        final.append((slot(x, 1 - yl, core), second, engine.send(block, block, partner)))
-        to_y.wait_recv()
-        other = slot(x, 1 - yl, core)
-        for d in (1, 2, 3):
-            block = dst.at[other, first]
-            final.append((slot(lax.rem(x + 4 - d, 4), 1 - yl, core), first, engine.send(block, block, x_peer(d))))
-        pass_on(other, first)
-        for d in (1, 2, 3):
-            to_x[d - 1].wait_recv()
-            source = lax.rem(x + 4 - d, 4)
-            block = dst.at[slot(source, yl, core), second]
-            final.append((slot(source, 1 - yl, core), second, engine.send(block, block, partner)))
-            pass_on(slot(source, yl, core), second)
-        yield
-        for index, part, copy in final:
-            copy.wait_recv()
-            pass_on(index, part)
-        yield
-        for copy in [to_y] + to_x + [c for _, _, c in final]:
-            copy.wait_send()
-        for copy in done[1:]:
-            copy.wait()
-
-    shape = (4, n, 128)
-    scratch = [
-        pltpu.VMEM((3, cut, 512), BF16),
-        pltpu.VMEM((3, rest, 512), BF16),
-        pltpu.VMEM((n, 512), BF16),
-        pltpu.VMEM((n, 512), BF16),
-    ]
-    peers = X_PEERS + Y_PEERS + Z_PEERS
-    if gather:
-        scratch.append(pltpu.VMEM(shape, BF16))
-        shape = (16,) + shape
-        peers = peers + [sibling, other_yl]
-    return Op([sum_y, sum_x], [(shape, BF16)], peers, body, tuple(scratch))
-
-
-def other_yl():
-    return {"yl": 1 - lax.axis_index("yl")}
+    x = lax.axis_index("x")
+    y = lax.axis_index("yh") * 2 + lax.axis_index("yl")
+    copies = []
+    for d in (2, 1, 3):
+        ty, tx = y_peer(d), x_peer(d)
+        copies.append(engine.send(src.at[ty["yh"] * 2 + ty["yl"], head], by_y.at[d - 1], ty))
+        copies.append(engine.send(src.at[:, tail, lanes(tx["x"], 512)], by_x.at[d - 1], tx))
+    yield
+    own_y, own_x = own_y.at[head], own_x.at[:, pl.ds(0, rest)]
+    local = [engine.local(src.at[y, head], own_y), engine.local(src.at[:, tail, lanes(x, 512)], own_x)]
+    for copy in local:
+        copy.wait()
+    for copy in copies:
+        copy.wait_recv()
+    add_up(sum_y, own_y, by_y, (), cut, WIDTH)
+    for q in range(4):
+        add_up(sum_x, own_x, by_x, (q,), rest, 512)
+    yield
+    for copy in copies:
+        copy.wait_send()
+
+
+def sum_rest(engine, heads, tails, landing, by_x, by_y, own, total):
+    cut, rest = heads.shape[0], tails.shape[1]
+    x = lax.axis_index("x")
+    y = lax.axis_index("yh") * 2 + lax.axis_index("yl")
+    first, second = pl.ds(0, cut), pl.ds(cut, rest)
+    copies = []
+    for d in (2, 1, 3):
+        ty, tx = y_peer(d), x_peer(d)
+        copies.append(engine.send(heads.at[:, lanes(tx["x"], 512)], by_x.at[d - 1], tx))
+        copies.append(engine.send(tails.at[ty["yh"] * 2 + ty["yl"]], by_y.at[d - 1], ty))
+    local = [engine.local(tails.at[y], own.at[second]), engine.local(heads.at[:, lanes(x, 512)], own.at[first])]
+    yield
+    for copy in local:
+        copy.wait()
+    for copy in copies:
+        copy.wait_recv()
+    add_up(total.at[first], own.at[first], by_x, (), cut, 512)
+    add_up(total.at[second], own.at[second], by_y, (), rest, 512)
+    moved = send_pieces(engine, lambda z: total.at[:, lanes(z)], landing)
+    yield
+    moved[0].wait()
+    for copy in moved[1:]:
+        copy.wait_recv()
+    yield
+    for copy in copies + moved[1:]:
+        copy.wait_send()
+
+
+def gather_ctx(engine, landing, dst):
+    x, yl, core = (lax.axis_index(a) for a in ("x", "yl", "core"))
+
+    def slot(xx, ll):
+        return (xx * 2 + ll) * 2 + core
+
+    first, second = pl.ds(0, 2), pl.ds(2, 2)
+    me, other = slot(x, yl), slot(x, 1 - yl)
+    partner, there = {"yl": 1 - yl}, sibling()
+    local = engine.local(landing, dst.at[me])
+    done = [engine.send(landing, dst.at[me], there)]
+    to_y = engine.send(landing.at[first], dst.at[me, first], partner)
+    to_x = [engine.send(landing.at[second], dst.at[me, second], x_peer(d)) for d in (1, 2, 3)]
+    final = []
+    for d in (1, 2, 3):
+        copy = engine.send(landing.at[first], dst.at[me, first], x_peer(d))
+        final.append((slot(lax.rem(x + 4 - d, 4), yl), first, copy))
+    final.append((other, second, engine.send(landing.at[second], dst.at[me, second], partner)))
+    yield
+
+    def pass_on(index, part):
+        block = dst.at[index, part]
+        done.append(engine.send(block, block, there))
+
+    to_y.wait_recv()
+    block = dst.at[other, first]
+    for d in (1, 2, 3):
+        final.append((slot(lax.rem(x + 4 - d, 4), 1 - yl), first, engine.send(block, block, x_peer(d))))
+    pass_on(other, first)
+    for d in (1, 2, 3):
+        to_x[d - 1].wait_recv()
+        source = lax.rem(x + 4 - d, 4)
+        block = dst.at[slot(source, yl), second]
+        final.append((slot(source, 1 - yl), second, engine.send(block, block, partner)))
+        pass_on(slot(source, yl), second)
+    yield
+    for index, part, copy in final:
+        copy.wait_recv()
+        pass_on(index, part)
+    yield
+    local.wait()
+    for copy in [to_y] + to_x + [c for _, _, c in final]:
+        copy.wait_send()
+    for copy in done:
+        copy.wait()
 
 
 def group_peer(dz, dc):
@@ -483,111 +383,93 @@
 
 
 GROUP_ALL = [(dz, dc) for dz in range(4) for dc in range(2) if dz or dc]
-GROUP_PEERS = [functools.partial(group_peer, dz, dc) for dz, dc in GROUP_ALL]
-
-
-def small_sum_op(norms, bias):
-    def body(engine, norms, bias, norm_sum, bias_all, by_group, by_x, by_y):
-        z, x, yl, core, yh = place()
-        y = yh * 2 + yl
-        me = z * 2 + core
-        first = []
-        for dz, dc in GROUP_ALL:
-            to = group_peer(dz, dc)
-            first.append(engine.send(norms.at[:, lanes(to["z"], 512)], by_group.at[me], to))
-        mine = engine.local(norms.at[:, lanes(z, 512)], by_group.at[me])
-        yield
-        mine.wait()
-        for copy in first:
-            copy.wait()
-        by_x[x, :, :512] = sum(by_group[k] for k in range(8))
-        by_x[x, :, 512:] = bias[...]
-        second = [engine.send(by_x.at[x], by_x.at[x], x_peer(d)) for d in (1, 2, 3)]
-        yield
-        for copy in second:
-            copy.wait()
-        by_y[y] = sum(by_x[k] for k in range(4))
-        third = [engine.send(by_y.at[y], by_y.at[y], y_peer(d)) for d in (1, 2, 3)]
-        yield
-        for copy in third:
-            copy.wait()
-        total = sum(by_y[k] for k in range(4))
-        norm_sum[...] = total[:, :512]
-        bias_all[me] = total[:, 512:]
-        last = [engine.send(bias_all.at[me], bias_all.at[me], group_peer(dz, dc)) for dz, dc in GROUP_ALL]
-        yield
-        for copy in last:
-            copy.wait()
-
-    outs = [((8, 512), F32, VMEM), ((8, 8, 128), F32, VMEM)]
-    scratch = (
-        pltpu.VMEM((8, 8, 512), F32),
-        pltpu.VMEM((4, 8, 640), F32),
-        pltpu.VMEM((4, 8, 640), F32),
-    )
-    return Op([(norms, VMEM), (bias, VMEM)], outs, GROUP_PEERS + X_PEERS + Y_PEERS, body, scratch)
-
-
-def hand_back_op(block):
-    def body(engine, src, dst):
-        core, yh = lax.axis_index("core"), lax.axis_index("yh")
-        far = {"core": yh, "yh": 1 - yh}
-        near = {"core": yh}
-        stays = core == yh
-        mine = dst.at[rows_at(core, OWN)]
-        i, j = engine.remote, engine.locals
-        engine.remote += 4
-        engine.locals += 1
-        send_sem, recv_sem, local_sem = engine.sems
-
-        def make(to, slot):
-            return pltpu.make_async_remote_copy(
-                src,
-                mine,
-                send_sem.at[i + slot],
-                recv_sem.at[i + 2 + core],
-                device_id=to,
-                device_id_type=MESH_ID,
-            )
-
-        def arrival(half):
-            part = dst.at[rows_at(half, OWN)]
-            return pltpu.make_async_remote_copy(
-                part, part, send_sem.at[i], recv_sem.at[i + 2 + half], device_id=far, device_id_type=MESH_ID
-            )
-
-        make(far, 0).start()
-
-        @pl.when(stays)
-        def _():
-            pltpu.make_async_copy(src, mine, local_sem.at[j]).start()
-
-        @pl.when(jnp.logical_not(stays))
-        def _():
-            make(near, 1).start()
-
-        yield
-        make(far, 0).wait_send()
-
-        @pl.when(stays)
-        def _():
-            pltpu.make_async_copy(src, mine, local_sem.at[j]).wait()
-            arrival(1 - core).wait_recv()
-
-        @pl.when(jnp.logical_not(stays))
-        def _():
-            make(near, 1).wait_send()
-            arrival(core).wait_recv()
-            arrival(1 - core).wait_recv()
-
-    def partner(dc, dh):
-        return {
-            "core": lax.rem(lax.axis_index("core") + dc, 2),
-            "yh": lax.rem(lax.axis_index("yh") + dh, 2),
-        }
-
-    peers = [functools.partial(partner, dc, dh) for dc, dh in ((0, 1), (1, 0), (1, 1))]
-    return Op([block], [((2 * OWN, WIDTH), block.dtype)], peers, body)
+
+
+def sum_small(engine, norms, bias, norm_sum, bias_all, by_group, by_x, by_y):
+    z, x, yl, core, yh = place()
+    y = yh * 2 + yl
+    me = z * 2 + core
+    first = []
+    for dz, dc in GROUP_ALL:
+        to = group_peer(dz, dc)
+        first.append(engine.send(norms.at[:, lanes(to["z"], 512)], by_group.at[me], to))
+    mine = engine.local(norms.at[:, lanes(z, 512)], by_group.at[me])
+    yield
+    mine.wait()
+    for copy in first:
+        copy.wait_recv()
+    by_x[x, :, :512] = sum(by_group[k] for k in range(8))
+    by_x[x, :, 512:] = bias[...]
+    second = [engine.send(by_x.at[x], by_x.at[x], x_peer(d)) for d in (1, 2, 3)]
+    yield
+    for copy in second:
+        copy.wait_recv()
+    by_y[y] = sum(by_x[k] for k in range(4))
+    third = [engine.send(by_y.at[y], by_y.at[y], y_peer(d)) for d in (1, 2, 3)]
+    yield
+    for copy in third:
+        copy.wait_recv()
+    total = sum(by_y[k] for k in range(4))
+    norm_sum[...] = total[:, :512]
+    bias_all[me] = total[:, 512:]
+    last = [engine.send(bias_all.at[me], bias_all.at[me], group_peer(dz, dc)) for dz, dc in GROUP_ALL]
+    yield
+    for copy in last:
+        copy.wait()
+    for copy in first + second + third:
+        copy.wait_send()
+
+
+def hand_back(engine, src, dst):
+    core, yh = lax.axis_index("core"), lax.axis_index("yh")
+    far = {"core": yh, "yh": 1 - yh}
+    near = {"core": yh}
+    stays = core == yh
+    mine = dst.at[rows_at(core, OWN)]
+    i, j = engine.remote, engine.locals
+    engine.remote += 4
+    engine.locals += 1
+    send_sem, recv_sem, local_sem = engine.sems
+
+    def make(to, slot):
+        return pltpu.make_async_remote_copy(
+            src,
+            mine,
+            send_sem.at[i + slot],
+            recv_sem.at[i + 2 + core],
+            device_id=to,
+            device_id_type=MESH_ID,
+        )
+
+    def arrival(half):
+        part = dst.at[rows_at(half, OWN)]
+        return pltpu.make_async_remote_copy(
+            part, part, send_sem.at[i], recv_sem.at[i + 2 + half], device_id=far, device_id_type=MESH_ID
+        )
+
+    make(far, 0).start()
+
+    @pl.when(stays)
+    def _():
+        pltpu.make_async_copy(src, mine, local_sem.at[j]).start()
+
+    @pl.when(jnp.logical_not(stays))
+    def _():
+        make(near, 1).start()
+
+    yield
+    make(far, 0).wait_send()
+
+    @pl.when(stays)
+    def _():
+        pltpu.make_async_copy(src, mine, local_sem.at[j]).wait()
+        arrival(1 - core).wait_recv()
+
+    @pl.when(jnp.logical_not(stays))
+    def _():
+        make(near, 1).wait_send()
+        arrival(core).wait_recv()
+        arrival(1 - core).wait_recv()
 
 
 def dot(a, b, dims):
@@ -942,6 +824,231 @@
     return result
 
 
+def back_peer(dc, dh):
+    return {
+        "core": lax.rem(lax.axis_index("core") + dc, 2),
+        "yh": lax.rem(lax.axis_index("yh") + dh, 2),
+    }
+
+
+BACKWARD_PEERS = XY_PEERS + Z_PEERS + [sibling, functools.partial(back_peer, 1, 1)]
+BACKWARD_PEERS += [functools.partial(group_peer, dz, 1) for dz in (1, 2, 3)]
+BACKWARD_FAR = ["back_part", "mlp_part", "g_gate", "g_up", "g_down", "h1", "m_qkv"]
+BACKWARD_NEAR = ["middle", "x_own", "dy_own", "norms", "m_out", "o_t", "kept", "wide", "lse"]
+BACKWARD_NEAR += ["seg_row", "seg_col", "cos", "sin"]
+BACKWARD_OUTS = [
+    ("layer_out", (2 * OWN, WIDTH), BF16, ANY),
+    ("grad_tokens", (2 * OWN, WIDTH), BF16, ANY),
+    ("mlp_all", (16, 4, 528, 128), BF16, ANY),
+    ("attn_all", (16, 4, 256, 128), BF16, ANY),
+    ("norm_sum", (8, 512), F32, VMEM),
+    ("bias_all", (8, 8, 768), F32, VMEM),
+]
+BACKWARD_SCRATCH = [
+    ("v_h1", (ROWS, WIDTH), BF16),
+    ("v_qkv", (4, 192, WIDTH), BF16),
+    ("dz_own", (OWN, WIDTH), BF16),
+    ("dz", (ROWS, WIDTH), BF16),
+    ("d_middle", (OWN, WIDTH), F32),
+    ("summed", (OWN, WIDTH), F32),
+    ("out_own", (OWN, WIDTH), BF16),
+    ("grad_own", (OWN, WIDTH), BF16),
+    ("own_dh2", (4, OWN, WIDTH), BF16),
+    ("other_dh2", (4, OWN, WIDTH), BF16),
+    ("arrived_dh2", (3, OWN, WIDTH), BF16),
+    ("own_mlp", (4, OWN, WIDTH), BF16),
+    ("other_mlp", (4, OWN, WIDTH), BF16),
+    ("arrived_mlp", (3, OWN, WIDTH), BF16),
+    ("give", (4, OWN, WIDTH), BF16),
+    ("own_dh1", (4, OWN, WIDTH), F32),
+    ("other_dh1", (4, OWN, WIDTH), BF16),
+    ("total_dh1", (3, OWN, WIDTH), BF16),
+    ("arrived_dh1", (3, OWN, WIDTH), BF16),
+    ("own_y", (128, WIDTH), BF16),
+    ("own_x", (4, 128, 512), BF16),
+    ("d_o", (4 * HEAD, ROWS), BF16),
+    ("item", (HEAD, SEQ), BF16),
+    ("item_out", (3 * HEAD, SEQ), BF16),
+    ("dk", (SEQ, HEAD), F32),
+    ("dv", (SEQ, HEAD), F32),
+    ("d_qkv", (12 * HEAD, ROWS), BF16),
+    ("d_rows", (ROWS, 12 * HEAD), BF16),
+    ("g_attn", (4, 256, WIDTH), BF16),
+    ("landing_mlp", (4, 528, 128), BF16),
+    ("landing_attn", (4, 256, 128), BF16),
+    ("small_norms", (8, WIDTH), F32),
+    ("small_bias", (8, 768), F32),
+    ("by_group", (8, 8, 512), F32),
+    ("small_x", (4, 8, 1280), F32),
+    ("small_y", (4, 8, 1280), F32),
+]
+for _name, _n in (("gate", 176), ("down", 176), ("up", 176), ("attn", 256)):
+    _cut = first_part(_n)
+    BACKWARD_SCRATCH += [
+        ("sum_y_" + _name, (_cut, WIDTH), BF16),
+        ("sum_x_" + _name, (4, _n - _cut, 512), BF16),
+        ("by_y_" + _name, (3, _cut, WIDTH), BF16),
+        ("by_x_" + _name, (3, 4, _n - _cut, 512), BF16),
+        ("rest_x_" + _name, (3, _cut, 512), BF16),
+        ("rest_y_" + _name, (3, _n - _cut, 512), BF16),
+        ("rest_own_" + _name, (_n, 512), BF16),
+        ("rest_total_" + _name, (_n, 512), BF16),
+    ]
+
+
+def backward_kernel(*refs):
+    r = Refs()
+    names = BACKWARD_FAR + BACKWARD_NEAR + [o[0] for o in BACKWARD_OUTS] + [o[0] for o in BACKWARD_SCRATCH]
+    for name, ref in zip(names, refs):
+        setattr(r, name, ref)
+    engine = Engine(*refs[len(names) :])
+    z, x, yl, core, yh = place()
+    y = yh * 2 + yl
+    greet(BACKWARD_PEERS)
+
+    def first_of(name, grad):
+        parts = [getattr(r, part + name) for part in ("sum_y_", "sum_x_", "by_y_", "by_x_")]
+        thread = sum_first(engine, grad, *parts, r.own_y, r.own_x)
+        next(thread)
+        return thread
+
+    def rest_of(name, landing):
+        parts = [getattr(r, part + name) for part in ("rest_x_", "rest_y_", "rest_own_", "rest_total_")]
+        thread = sum_rest(engine, getattr(r, "sum_y_" + name), getattr(r, "sum_x_" + name), landing, *parts)
+        next(thread)
+        return thread
+
+    def mlp_landing(first):
+        return lambda zz: r.landing_mlp.at[zz, pl.ds(first, 176)]
+
+    dh2 = scatter_tokens(engine, r.back_part, r.summed, r.own_dh2, r.other_dh2, r.arrived_dh2)
+    next(dh2)
+    gate = first_of("gate", r.g_gate)
+    down = first_of("down", r.g_down)
+    load_h1 = engine.local(r.h1, r.v_h1)
+    load_qkv = engine.local(r.m_qkv, r.v_qkv)
+    next(dh2)
+    mlp = scatter_tokens(engine, r.mlp_part, r.d_middle, r.own_mlp, r.other_mlp, r.arrived_mlp)
+    next(mlp)
+    _, normed_b, rstd_b = layer_norm(r.middle[...], r.norms[1:2], r.norms[3:4])
+    next(dh2)
+    back_b, gain_b, shift_b = norm_back(r.summed[...], normed_b, rstd_b, r.norms[1:2])
+    d_middle = r.dy_own[...].astype(F32) + back_b
+    r.dz_own[...] = d_middle.astype(BF16)
+    tokens_dz = gather_tokens(engine, r.dz_own, r.dz)
+    next(tokens_dz)
+    r.small_norms[1:2] = gain_b[None]
+    r.small_norms[3:4] = shift_b[None]
+    next(mlp)
+    next(gate)
+    rest_gate = rest_of("gate", mlp_landing(0))
+    next(tokens_dz)
+    finish(tokens_dz)
+
+    place_here = lanes(x * 4 + yl * 2 + yh)
+    to_items, stay = [], None
+    for dy in (2, 1, 3, 0):
+        ty = lax.rem(y + dy, 4)
+        rows = rows_at(ty, HEAD)
+        r.d_o[rows, :] = dot(r.m_out[ty], r.dz[...], (1, 1)).astype(BF16)
+        for dx in (2, 1, 3, 0):
+            block = r.d_o.at[rows, lanes(lax.rem(x + dx, 4))]
+            if dx or dy:
+                to_items.append(engine.send(block, r.item.at[:, place_here], xy_peer(dx, dy)))
+            else:
+                stay = engine.local(block, r.item.at[:, place_here])
+    up = first_of("up", r.g_up)
+    next(mlp)
+    r.out_own[...] = spread(r.middle[...] + r.d_middle[...]).astype(BF16)
+    r.d_middle[...] = d_middle
+    hand_out = hand_back(engine, r.out_own, r.layer_out)
+    next(hand_out)
+    for q in range(4):
+        r.g_attn[q, 192:] = dot(r.o_t[q * HEAD : (q + 1) * HEAD, :], r.dz[...], (1, 0)).astype(BF16)
+    stay.wait()
+    for copy in to_items:
+        copy.wait_recv()
+    next(down)
+    rest_down = rest_of("down", mlp_landing(352))
+    attend_back(
+        r.kept, r.item, r.wide, r.lse, r.seg_row, r.seg_col, r.cos, r.sin, r.item_out, r.dk, r.dv
+    )
+    back = return_items(engine, r.item_out, r.d_qkv, 3 * HEAD)
+    next(rest_gate)
+    next(rest_down)
+    next(up)
+    rest_up = rest_of("up", mlp_landing(176))
+    back[-1].wait()
+    for copy in back[:-1]:
+        copy.wait_recv()
+
+    load_h1.wait()
+    load_qkv.wait()
+    r.d_rows[...] = r.d_qkv[...].astype(F32).T.astype(BF16)
+    matrix = r.v_qkv[...].reshape(12 * HEAD, WIDTH)
+    dh1 = scatter_product(
+        engine, r.d_rows, matrix, r.summed, r.give, r.own_dh1, r.other_dh1, r.total_dh1, r.arrived_dh1
+    )
+    next(dh1)
+    for q in range(4):
+        rows = slice(q * 3 * HEAD, (q + 1) * 3 * HEAD)
+        r.g_attn[q, :192] = dot(r.d_qkv[rows, :], r.v_h1[...], (1, 0)).astype(BF16)
+    attn = first_of("attn", r.g_attn)
+    r.small_bias[...] = dot(jnp.ones((8, ROWS), BF16), r.d_qkv[...], (1, 1))
+    next(rest_up)
+    for thread in (rest_gate, rest_down, rest_up):
+        next(thread)
+    gather_mlp = gather_ctx(engine, r.landing_mlp, r.mlp_all)
+    next(gather_mlp)
+    _, normed_a, rstd_a = layer_norm(r.x_own[...].astype(F32), r.norms[0:1], r.norms[2:3])
+    next(dh1)
+    back_a, gain_a, shift_a = norm_back(r.summed[...], normed_a, rstd_a, r.norms[0:1])
+    r.grad_own[...] = spread(r.d_middle[...] + back_a).astype(BF16)
+    hand_grad = hand_back(engine, r.grad_own, r.grad_tokens)
+    next(hand_grad)
+    r.small_norms[0:1] = gain_a[None]
+    r.small_norms[2:3] = shift_a[None]
+    r.small_norms[4:] = jnp.zeros((4, WIDTH), F32)
+    r.small_norms[...] = spread(r.small_norms[...])
+    small = sum_small(
+        engine, r.small_norms, r.small_bias, r.norm_sum, r.bias_all, r.by_group, r.small_x, r.small_y
+    )
+    next(small)
+    next(attn)
+    rest_attn = rest_of("attn", lambda zz: r.landing_attn.at[zz])
+    next(small)
+    next(rest_attn)
+    next(small)
+    next(rest_attn)
+    gather_attn = gather_ctx(engine, r.landing_attn, r.attn_all)
+    next(gather_attn)
+    next(gather_mlp)
+    next(small)
+    next(gather_attn)
+    next(gather_mlp)
+    next(gather_attn)
+    threads = (dh2, mlp, gate, down, up, attn, rest_gate, rest_down, rest_up, rest_attn)
+    for thread in threads + (hand_out, dh1, hand_grad, small, gather_mlp, gather_attn):
+        finish(thread)
+    for copy in to_items + back[:-1]:
+        copy.wait_send()
+
+
+def backward(values):
+    given = [values[name] for name in BACKWARD_FAR + BACKWARD_NEAR]
+    return pl.pallas_call(
+        backward_kernel,
+        out_shape=[jax.ShapeDtypeStruct(o[1], o[2]) for o in BACKWARD_OUTS],
+        in_specs=[ANY] * len(BACKWARD_FAR) + [VMEM] * len(BACKWARD_NEAR),
+        out_specs=[o[3] for o in BACKWARD_OUTS],
+        scratch_shapes=[pltpu.VMEM(shape, dtype) for _, shape, dtype in BACKWARD_SCRATCH] + semaphores(240, 48),
+        compiler_params=pltpu.CompilerParams(
+            collective_id=2, has_side_effects=True, vmem_limit_bytes=58 * 2**20
+        ),
+        name="backward",
+    )(*given)
+
+
 def assemble_kernel(mlp_ref, attn_ref, gu_ref, down_ref, qkv_ref, out_ref, turned):
     for g in range(2):
         for zz in range(4):
@@ -958,15 +1065,10 @@
                 row = zz * 704 + core * 352 + yl * 176
                 down_ref[row : row + 176, :] = mlp_ref[0, yl * 2 + core, zz, 352:].astype(F32)
                 row = zz * 256 + core * 128 + yl * 64
-                out_ref[row : row + 32, :] = attn_ref[0, yl * 2 + core, zz, 96:128].astype(F32)
-                out_ref[row + 32 : row + 64, :] = attn_ref[0, yl * 2 + core, zz, 224:].astype(F32)
+                out_ref[row : row + 64, :] = attn_ref[0, yl * 2 + core, zz, 192:].astype(F32)
             for part in range(3):
-                pieces = []
-                for yl in range(2):
-                    for row in (part * 64, part * 64 + 32):
-                        row = row if row < 96 else row + 32
-                        pieces.append(attn_ref[0, yl * 2 + core, zz, row : row + 32])
-                block = jnp.concatenate(pieces, axis=0)
+                rows = slice(part * 64, (part + 1) * 64)
+                block = jnp.concatenate([attn_ref[0, core, zz, rows], attn_ref[0, 2 + core, zz, rows]], axis=0)
                 column = zz * 256 + core * 128
                 qkv_ref[part, :, column : column + 128] = block.astype(F32).T
 
@@ -1041,14 +1143,8 @@
     f = forward(
         tokens[0], cotangent[0], packed, w_qkv.transpose(1, 0, 2), w_out, w_down, w_gate_up, cosine, sine
     )
-    gains, shifts = f.norms[:2], f.norms[2:4]
-    x_own, dy_own, middle = f.x_own.astype(F32), f.dy_own, f.middle
-    h1, h2, dy, o_t, kept, o_wide, lse = f.h1, f.h2, f.dy, f.o_t, f.kept, f.wide, f.lse
-    item_segments, segment_column = f.seg_row, f.seg_col
-    m_qkv, m_out, m_down = f.m_qkv.reshape(768, WIDTH), f.m_out.reshape(256, WIDTH), f.m_down.reshape(704, WIDTH)
-    m_gate, m_up = f.m_gate.reshape(704, WIDTH), f.m_up.reshape(704, WIDTH)
-    _, normed_a, rstd_a = layer_norm(x_own, gains[:1], shifts[:1])
-    _, normed_b, rstd_b = layer_norm(middle, gains[1:], shifts[1:])
+    h2, dy = f.h2, f.dy
+    m_down, m_gate, m_up = (m.reshape(704, WIDTH) for m in (f.m_down, f.m_gate, f.m_up))
 
     gate, up = dot(m_gate, h2, (1, 1)), dot(m_up, h2, (1, 1))
     sigmoid = jax.nn.sigmoid(gate)
@@ -1064,64 +1160,11 @@
         return dot(a, b, (1, 0)).astype(BF16).reshape(4, a.shape[0] // 4, WIDTH)
 
     g_gate, g_up, g_down = weight_grad(d_gate, h2), weight_grad(d_up, h2), weight_grad(act, dy)
-    (dh2_own,), (mlp_own,), first_gate, first_down = exchange(
-        "sum_mlp",
-        2,
-        [token_scatter_op(back_part), token_scatter_op(mlp_part), grad_first_op(g_gate), grad_first_op(g_down)],
-        48,
-        24,
-    )
-
-    out_own = spread((middle + mlp_own).astype(BF16))
-    back_b, gain_b, shift_b = norm_back(dh2_own, normed_b, rstd_b, gains[1:])
-    d_middle = dy_own.astype(F32) + back_b
-    (dz,), first_up, (z_down,) = exchange(
-        "gather_dz",
-        3,
-        [token_gather_op(d_middle.astype(BF16)), grad_first_op(g_up), grad_rest_op(*first_down)],
-        48,
-        24,
-    )
-    d_o = dot(m_out, dz, (1, 1)).astype(BF16)
-    g_out = weight_grad(o_t, dz)
-    (d_qkv,), (z_gate,), (z_up,), (layer_out,) = exchange(
-        "attention_back",
-        4,
-        [
-            attention_back_op(d_o, kept, o_wide, lse, item_segments, segment_column, cosine, sine),
-            grad_rest_op(*first_gate),
-            grad_rest_op(*first_up),
-            hand_back_op(out_own),
-        ],
-        96,
-        24,
-    )
-    mlp_z = jnp.concatenate([z_gate, z_up, z_down], axis=1)
-    mlp_all = lax.all_gather(mlp_z, ("x", "yl", "core"), axis=0)
-
-    back_part = dot(d_qkv, m_qkv, (0, 0)).astype(BF16)
-    g_qkv = weight_grad(d_qkv, h1)
-    g_bias = jnp.sum(d_qkv.astype(F32), axis=1)
-    (dh1_own,), first_qkv, first_out = exchange(
-        "sum_dh1", 5, [token_scatter_op(back_part), grad_first_op(g_qkv), grad_first_op(g_out)], 48, 24
-    )
-    back_a, gain_a, shift_a = norm_back(dh1_own, normed_a, rstd_a, gains[:1])
-    grad_own = spread((d_middle + back_a).astype(BF16))
-    norms = spread(jnp.pad(jnp.stack([gain_a, gain_b, shift_a, shift_b]), ((0, 4), (0, 0))))
-    first_attn = [jnp.concatenate([a, b], axis=-2) for a, b in zip(first_qkv, first_out)]
-    (attn_all,), (norm_sum, bias_all), (grad_tokens,) = exchange(
-        "finish",
-        6,
-        [
-            grad_rest_op(*first_attn, gather=True),
-            small_sum_op(norms, jnp.pad(g_bias, (0, 256)).reshape(8, 128)),
-            hand_back_op(grad_own),
-        ],
-        80,
-        24,
-    )
-    attn_all = attn_all.reshape(16, 4, 256, 128)
-    bias_all = bias_all.reshape(8, 1024)[:, :768].reshape(4, 2, 2, 2, 3, 4, 16)
+    values = dict(vars(f), cos=cosine, sin=sine, back_part=back_part, mlp_part=mlp_part)
+    values.update(g_gate=g_gate, g_up=g_up, g_down=g_down)
+    layer_out, grad_tokens, mlp_all, attn_all, norm_sum, bias_all = backward(values)
+
+    bias_all = bias_all[:, 0].reshape(4, 2, 2, 2, 3, 4, 16)
     bias_all = pick(pick(bias_all, 2, yh), 4, z)
     grad_bias = bias_all.transpose(3, 0, 1, 2, 4).reshape(3, 16, 16)
     out_gu, out_down, out_qkv, out_out = assemble(mlp_all, attn_all)

time: 408 us -> 362 us (0.89)
  Pallas kernels: 334 us -> 317 us
  between operations: 15.1 us -> 1.27 us
  other arithmetic: 8.36 us -> 2.85 us
  local copies, waits for them, and re-layouts: 14.6 us -> 9.2 us
  matrix products: 32.5 us -> 27.5 us
    pallas_call x5 -> x1, Pallas kernels: 204 us -> 188 us  [backward(): pl.pallas_call(backward_kernel, out_shape=[jax.ShapeDtypeStruct(o[1], o[2...]
    dot_general x13 -> x9, matrix products: 32.5 us -> 27.5 us  [dot(): lax.dot_general(a, b, ((dims[:1], dims[1:]), ((), ())), preferred_element...]
    unnamed x97 -> x46, local copies, waits for them, and re-layouts: 10.8 us -> 5.89 us
  transfers between devices with their start and end apart: 1 -> 0, of which waited for: 0 -> 0; matrix products, arithmetic and copies ran while one was open for 2% -> 0% of each run, Pallas kernels for 24% -> 0%
where the time goes in v4:
time: 362 us; the launch traced here: 358 us
  Pallas kernels  317 us (88%)
  matrix products  27.5 us (8%)
  local copies, waits for them, and re-layouts  9.2 us (3%)
    pallas_call x1, Pallas kernels, backward(): pl.pallas_call(backward_kernel, out_shape=[jax.ShapeDtypeStruct(o[1], o[2...  188 us
    pallas_call x1, Pallas kernels, forward(): pl.pallas_call(forward_kernel, out_shape=[jax.ShapeDtypeStruct(o[1], o[2]...  115 us
    dot_general x9, matrix products, dot(): lax.dot_general(a, b, ((dims[:1], dims[1:]), ((), ())), preferred_element...  27.5 us
    pallas_call x1, Pallas kernels, assemble(): pl.pallas_call(assemble_kernel, grid=(4,), in_specs=[pl.BlockSpec((1, 4,...  14.1 us

profile of v4, /device:TPU:1, one launch (start us, length us, event | category | flops | bytes accessed | tf_op | source)
XLA Modules:
  0.0 358.2 jit_solution(7006711465129876122)
XLA Ops:
  0.7 0.3 multiply_sine_fusion
  1.0 0.0 copy-start.2
  1.0 0.0 copy-start.3
  1.0 0.8 copy.31
  1.8 0.1 copy.24
  1.9 0.7 convert_reduce_fusion
  2.6 0.7 fusion.2.refs_2_
  3.3 0.0 copy-start.4
  3.4 1.0 copy-done.4
  4.4 0.0 copy-start.5
  4.4 1.0 copy-done.5
  5.4 115.2 %forward.1 = (bf16[4,192,2048]{2,1,0:T(8,128)(2,1)}, bf16[4,64,2048]{2,1,0:T(8,128)(2,1)}, bf16[4,176,2048]{2,1,0:T(8,128)(2,1)}, bf16[4,176,2048]{2,1,0:T(8,128...) custom-call(bf16[128,2048]{1,0:T(8,128)(2,1)S(1)} %bitcast.47, ...), custom_call_target="tpu_custom_call" | custom-call | tf_op jit(solution)/shard_map/forward/pallas_call | solution.py:810
  120.6 0.0 copy-done.2
  120.6 0.0 copy-done.3
  120.7 0.0 copy-start.1
  120.7 0.0 copy-start.6
  120.7 0.0 copy-start.7
  120.7 0.0 copy-start.8
  120.7 0.0 copy-start.9
  120.7 0.0 copy-start.10
  120.7 0.0 copy-start.11
  120.7 0.0 copy-start.12
  120.7 0.0 copy-start.13
  120.8 0.0 copy-start.19
  120.8 0.0 copy-start.21
  120.8 5.1 %fusion.5 = f32[704,512]{1,0:T(8,128)S(1)} fusion(bf16[704,2048]{1,0:T(8,128)(2,1)} %bitcast.54, bf16[512,2048]{1,0:T(8,128)(2,1)} %get-tuple-element.40), kind=kOutput, calls=%fused_computation.25 | convolution fusion | flops 1476395008 | bytes 6422528 | tf_op jit(solution)/shard_map/dot_general | solution.py:476
  125.9 0.0 copy-done.1
  125.9 0.0 copy-done.6
  125.9 0.0 copy-done.7
  125.9 0.0 copy-done.8
  125.9 0.0 copy-done.9
  125.9 0.0 copy-done.10
  125.9 0.0 copy-done.11
  125.9 0.0 copy-done.12
  125.9 0.0 copy-done.13
  125.9 0.0 copy-done.19
  126.0 0.0 copy-done.21
  126.0 0.0 copy-start.18
  126.0 0.0 copy-start.20
  126.0 1.7 fusion.4
  127.7 0.1 copy-done.18
  127.8 0.6 copy-done.20
  128.4 2.3 multiply_convert_fusion
  130.8 3.2 convolution_convert_fusion
  134.0 3.3 convolution_convert_fusion.1
  137.3 3.3 convolution_convert_fusion.2
  140.6 0.0 copy-start.14
  140.6 3.2 convolution_convert_fusion.3.refs_1_
  143.8 0.0 copy-done.14
  143.8 2.1 fusion.6
  145.9 3.3 add_convert_fusion.refs_0_
  149.2 188.0 %backward.1 = (bf16[128,2048]{1,0:T(8,128)(2,1)}, bf16[128,2048]{1,0:T(8,128)(2,1)}, bf16[16,4,528,128]{3,2,1,0:T(8,128)(2,1)}, bf16[16,4,256,128]{3,2,1,0:T(8,1...) custom-call(bf16[512,2048]{1,0:T(8,128)(2,1)} %add_convert_fusion.refs_0_, ...), custom_call_target="tpu_custom_call" | custom-call | tf_op jit(solution)/shard_map/backward/pallas_call | solution.py:1039
  337.2 0.0 copy-start
  337.2 2.2 copy-done
  339.4 14.1 %assemble.1 = (f32[512,2,2816]{2,1,0:T(2,128)}, f32[2816,512]{1,0:T(8,128)}, f32[3,512,1024]{2,1,0:T(8,128)}, f32[1024,512]{1,0:T(8,128)}) custom-call(bf16[4,4,4,528,128]{4,3,2,1,0:T(8,128)(2,1)} %bitcast.49, bf16[4,4,4,256,128]{4,3,2,1,0:T(8,128)(2,1)S(1)} %bitcast.46), custom_call_target="tpu_custom_call" | custom-call | tf_op jit(solution)/shard_map/assemble/pallas_call | solution.py:1079
  353.5 0.0 copy-done.15
  353.5 1.1 bitcast_convert_fusion
  354.6 1.0 slice_reduce_fusion
  355.6 0.2 reshape_squeeze.3
  355.9 0.6 copy.26
  356.5 0.0 copy-done.17
  356.5 0.6 fusion.3
  357.1 0.0 copy-done.16
  357.1 0.8 copy.33
  (10 shorter events, 0.1 us)
Async XLA Ops:
  1.0 119.7 %copy-start.2 = (f32[8,2048]{1,0:T(8,128)}, f32[8,2048]{1,0:T(8,128)S(1)}, u32[]{:S(2)}) copy-start(f32[8,2048]{1,0:T(8,128)S(1)} %get-tuple-element.70.refs_8_.refs_19_) | copy-start | bytes 196612
  1.0 119.7 %copy-start.3 = (f32[8,2048]{1,0:T(8,128)}, f32[8,2048]{1,0:T(8,128)S(1)}, u32[]{:S(2)}) copy-start(f32[8,2048]{1,0:T(8,128)S(1)} %get-tuple-element.71.refs_7_.refs_18_) | copy-start | bytes 196612
  3.3 1.0 copy-start.4
  4.4 1.0 copy-start.5
  120.7 5.2 %copy-start.1 = (bf16[192,2048]{1,0:T(8,128)(2,1)}, bf16[192,2048]{1,0:T(8,128)(2,1)S(1)}, u32[]{:S(2)}) copy-start(bf16[192,2048]{1,0:T(8,128)(2,1)S(1)} %get-tuple-element.50.refs_13_) | copy-start | bytes 2359300
  120.7 5.2 %copy-start.6 = (f32[64,2048]{1,0:T(8,128)}, f32[64,2048]{1,0:T(8,128)S(1)}, u32[]{:S(2)}) copy-start(f32[64,2048]{1,0:T(8,128)S(1)} %get-tuple-element.44.refs_7_) | copy-start | bytes 1572868
  120.7 5.2 %copy-start.7 = (f32[64,2048]{1,0:T(8,128)}, f32[64,2048]{1,0:T(8,128)S(1)}, u32[]{:S(2)}) copy-start(f32[64,2048]{1,0:T(8,128)S(1)} %get-tuple-element.51.refs_14_) | copy-start | bytes 1572868
  120.7 5.2 %copy-start.8 = (bf16[64,2048]{1,0:T(8,128)(2,1)}, bf16[64,2048]{1,0:T(8,128)(2,1)S(1)}, u32[]{:S(2)}) copy-start(bf16[64,2048]{1,0:T(8,128)(2,1)S(1)} %get-tuple-element.45.refs_8_) | copy-start | bytes 786436
  120.7 5.2 %copy-start.9 = (bf16[64,2048]{1,0:T(8,128)(2,1)}, bf16[64,2048]{1,0:T(8,128)(2,1)S(1)}, u32[]{:S(2)}) copy-start(bf16[64,2048]{1,0:T(8,128)(2,1)S(1)} %get-tuple-element.46.refs_9_) | copy-start | bytes 786436
  120.7 5.2 %copy-start.10 = (bf16[256,512]{1,0:T(8,128)(2,1)}, bf16[256,512]{1,0:T(8,128)(2,1)S(1)}, u32[]{:S(2)}) copy-start(bf16[256,512]{1,0:T(8,128)(2,1)S(1)} %get-tuple-element.49.refs_12_) | copy-start | bytes 786436
  120.7 5.2 %copy-start.11 = (f32[8,2048]{1,0:T(8,128)}, f32[8,2048]{1,0:T(8,128)S(1)}, u32[]{:S(2)}) copy-start(f32[8,2048]{1,0:T(8,128)S(1)} %get-tuple-element.47.refs_10_) | copy-start | bytes 196612
  120.7 5.2 %copy-start.12 = (f32[1,2048]{1,0:T(1,128)}, f32[1,2048]{1,0:T(1,128)S(1)}, u32[]{:S(2)}) copy-start(f32[1,2048]{1,0:T(1,128)S(1)} %get-tuple-element.52.refs_15_) | copy-start | bytes 24580
  120.7 5.2 %copy-start.13 = (f32[1,2048]{1,0:T(1,128)}, f32[1,2048]{1,0:T(1,128)S(1)}, u32[]{:S(2)}) copy-start(f32[1,2048]{1,0:T(1,128)S(1)} %get-tuple-element.53.refs_16_) | copy-start | bytes 24580
  120.8 5.2 %copy-start.19 = (bf16[4,176,2048]{2,1,0:T(8,128)(2,1)S(1)}, bf16[4,176,2048]{2,1,0:T(8,128)(2,1)}, u32[]{:S(2)}) copy-start(bf16[4,176,2048]{2,1,0:T(8,128)(2,1)} %get-tuple-element.37) | copy-start | bytes 8650756
  120.8 5.2 %copy-start.21 = (bf16[512,2048]{1,0:T(8,128)(2,1)S(1)}, bf16[512,2048]{1,0:T(8,128)(2,1)}, u32[]{:S(2)}) copy-start(bf16[512,2048]{1,0:T(8,128)(2,1)} %get-tuple-element.38) | copy-start | bytes 6291460
  126.0 1.8 copy-start.18
  126.0 2.5 copy-start.20
  140.6 3.2 copy-start.14
  337.2 2.2 copy-start
  339.4 14.1 %copy-start.15 = (bf16[128,2048]{1,0:T(8,128)(2,1)S(1)}, bf16[128,2048]{1,0:T(8,128)(2,1)}, u32[]{:S(2)}) copy-start(bf16[128,2048]{1,0:T(8,128)(2,1)} %get-tuple-element.56) | copy-start | bytes 1572868
  339.4 17.1 %copy-start.17 = (f32[8,512]{1,0:T(8,128)S(1)}, f32[8,512]{1,0:T(8,128)}, u32[]{:S(2)}) copy-start(f32[8,512]{1,0:T(8,128)} %get-tuple-element.64) | copy-start | bytes 49156
  353.5 3.6 copy-start.16

commit v5 on v4

--- a/solution.py
+++ b/solution.py
@@ -209,12 +209,12 @@
     return copies
 
 
-def add_up(total, own, others, index, rows, width):
+def add_up(total, terms, index, rows, width):
     def step(i, carry):
         here = (*index, rows_at(i, 16), slice(0, width))
-        value = own[here].astype(F32)
-        for k in range(3):
-            value += others[(k, *here)].astype(F32)
+        value = terms[0][here].astype(F32)
+        for term in terms[1:]:
+            value += term[here].astype(F32)
         total[here] = value.astype(total.dtype)
         return carry
 
@@ -250,22 +250,25 @@
         there.wait_send()
 
 
-def scatter_product(engine, rows, matrix, dst, give, own, other, total, arrived):
+def scatter_product(engine, rows, matrix, dst, product, other, arrived):
     z, core = lax.axis_index("z"), lax.axis_index("core")
+    for k in range(4):
+        columns = slice(k * 512, (k + 1) * 512)
+        product[:, columns] = dot(rows[...], matrix[:, columns], (1, 0)).astype(BF16)
     to_core = []
     for i in range(4):
-        base = lax.rem(z + 1 + i, 4) * 2
-        give[i] = dot(rows[rows_at(base + 1 - core, OWN), :], matrix, (1, 0)).astype(BF16)
-        to_core.append(engine.send(give.at[i], other.at[i], sibling()))
-        own[i] = dot(rows[rows_at(base + core, OWN), :], matrix, (1, 0))
+        give = product.at[rows_at(lax.rem(z + 1 + i, 4) * 2 + 1 - core, OWN)]
+        to_core.append(engine.send(give, other.at[i], sibling()))
+    yield
     to_z = []
     for i in range(3):
+        own = rows_at(lax.rem(z + 1 + i, 4) * 2 + core, OWN)
         to_core[i].wait_recv()
-        total[i] = (own[i] + other[i].astype(F32)).astype(BF16)
-        to_z.append(engine.send(total.at[i], arrived.at[i], z_peer(i + 1)))
+        product[own, :] = (product[own, :].astype(F32) + other[i].astype(F32)).astype(BF16)
+        to_z.append(engine.send(product.at[own], arrived.at[i], z_peer(i + 1)))
     yield
     to_core[3].wait_recv()
-    dst[...] = own[3] + other[3].astype(F32)
+    dst[...] = product[rows_at(z * 2 + core, OWN), :].astype(F32) + other[3].astype(F32)
     for i in range(3):
         to_z[i].wait_recv()
         dst[...] += arrived[i].astype(F32)
@@ -274,29 +277,67 @@
         copy.wait_send()
 
 
-def sum_first(engine, src, sum_y, sum_x, by_y, by_x, own_y, own_x):
+def sum_first(engine, src, sum_y, sum_x, by_y, by_x, relay_y, relay_x, own_y, own_x):
     n, cut = src.shape[1], sum_y.shape[0]
-    rest = n - cut
-    head, tail = pl.ds(0, cut), pl.ds(cut, rest)
+    rest, half = n - cut, first_part(cut)
+    tail = pl.ds(cut, rest)
+    early, late = pl.ds(0, half), pl.ds(half, cut - half)
+    low, high = pl.ds(0, 2), pl.ds(2, 2)
     x = lax.axis_index("x")
     y = lax.axis_index("yh") * 2 + lax.axis_index("yl")
-    copies = []
-    for d in (2, 1, 3):
-        ty, tx = y_peer(d), x_peer(d)
-        copies.append(engine.send(src.at[ty["yh"] * 2 + ty["yl"], head], by_y.at[d - 1], ty))
-        copies.append(engine.send(src.at[:, tail, lanes(tx["x"], 512)], by_x.at[d - 1], tx))
-    yield
-    own_y, own_x = own_y.at[head], own_x.at[:, pl.ds(0, rest)]
-    local = [engine.local(src.at[y, head], own_y), engine.local(src.at[:, tail, lanes(x, 512)], own_x)]
+    up_y, down_y = lax.rem(y + 1, 4), lax.rem(y + 3, 4)
+    up_x, down_x = lanes(lax.rem(x + 1, 4), 512), lanes(lax.rem(x + 3, 4), 512)
+    far_y, far_x = lax.rem(y + 2, 4), lanes(lax.rem(x + 2, 4), 512)
+    relays = [
+        engine.send(src.at[far_y, early], relay_y.at[early], y_peer(1)),
+        engine.send(src.at[low, tail, far_x], relay_x.at[low], x_peer(1)),
+        engine.send(src.at[far_y, late], relay_y.at[late], y_peer(3)),
+        engine.send(src.at[high, tail, far_x], relay_x.at[high], x_peer(3)),
+    ]
+    copies = [
+        engine.send(src.at[up_y, late], by_y.at[0, late], y_peer(1)),
+        engine.send(src.at[high, tail, up_x], by_x.at[0, high], x_peer(1)),
+        engine.send(src.at[down_y, early], by_y.at[1, early], y_peer(3)),
+        engine.send(src.at[low, tail, down_x], by_x.at[1, low], x_peer(3)),
+    ]
+    yield
+    own_y, own_x = own_y.at[pl.ds(0, cut)], own_x.at[:, pl.ds(0, rest)]
+    local = [
+        engine.local(src.at[up_y, early], own_y.at[early]),
+        engine.local(src.at[down_y, late], own_y.at[late]),
+        engine.local(src.at[low, tail, up_x], own_x.at[low]),
+        engine.local(src.at[high, tail, down_x], own_x.at[high]),
+    ]
+    for copy in local:
+        copy.wait()
+    relays[0].wait_recv()
+    add_up(relay_y.at[early], [relay_y.at[early], own_y.at[early]], (), half, WIDTH)
+    copies.append(engine.send(relay_y.at[early], by_y.at[0, early], y_peer(1)))
+    relays[1].wait_recv()
+    for q in range(2):
+        add_up(relay_x, [relay_x, own_x], (q,), rest, 512)
+    copies.append(engine.send(relay_x.at[low], by_x.at[0, low], x_peer(1)))
+    relays[2].wait_recv()
+    add_up(relay_y.at[late], [relay_y.at[late], own_y.at[late]], (), cut - half, WIDTH)
+    copies.append(engine.send(relay_y.at[late], by_y.at[1, late], y_peer(3)))
+    relays[3].wait_recv()
+    for q in range(2, 4):
+        add_up(relay_x, [relay_x, own_x], (q,), rest, 512)
+    copies.append(engine.send(relay_x.at[high], by_x.at[1, high], x_peer(3)))
+    yield
+    local = [
+        engine.local(src.at[y, pl.ds(0, cut)], own_y),
+        engine.local(src.at[:, tail, lanes(x, 512)], own_x),
+    ]
     for copy in local:
         copy.wait()
     for copy in copies:
         copy.wait_recv()
-    add_up(sum_y, own_y, by_y, (), cut, WIDTH)
+    add_up(sum_y, [own_y, by_y.at[0], by_y.at[1]], (), cut, WIDTH)
     for q in range(4):
-        add_up(sum_x, own_x, by_x, (q,), rest, 512)
-    yield
-    for copy in copies:
+        add_up(sum_x, [own_x, by_x.at[0], by_x.at[1]], (q,), rest, 512)
+    yield
+    for copy in relays + copies:
         copy.wait_send()
 
 
@@ -316,8 +357,8 @@
         copy.wait()
     for copy in copies:
         copy.wait_recv()
-    add_up(total.at[first], own.at[first], by_x, (), cut, 512)
-    add_up(total.at[second], own.at[second], by_y, (), rest, 512)
+    add_up(total.at[first], [own.at[first]] + [by_x.at[k] for k in range(3)], (), cut, 512)
+    add_up(total.at[second], [own.at[second]] + [by_y.at[k] for k in range(3)], (), rest, 512)
     moved = send_pieces(engine, lambda z: total.at[:, lanes(z)], landing)
     yield
     moved[0].wait()
@@ -331,48 +372,74 @@
 def gather_ctx(engine, landing, dst):
     x, yl, core = (lax.axis_index(a) for a in ("x", "yl", "core"))
 
-    def slot(xx, ll):
-        return (xx * 2 + ll) * 2 + core
-
+    def slot(dx, ll):
+        return (lax.rem(x + dx, 4) * 2 + ll) * 2 + core
+
+    other = 1 - yl
     first, second = pl.ds(0, 2), pl.ds(2, 2)
-    me, other = slot(x, yl), slot(x, 1 - yl)
-    partner, there = {"yl": 1 - yl}, sibling()
+    even, odd = (pl.ds(0, 1), pl.ds(1, 1)), (pl.ds(2, 1), pl.ds(3, 1))
+    partner, there = {"yl": other}, sibling()
+    sent = []
+
+    def send(source, target, part, device):
+        copy = engine.send(source, dst.at[target, part], device)
+        sent.append(copy)
+        return copy
+
+    def hand(index, part):
+        block = dst.at[index, part]
+        return send(block, index, part, there)
+
+    def on(index, part, device):
+        return send(dst.at[index, part], index, part, device)
+
+    me = slot(0, yl)
     local = engine.local(landing, dst.at[me])
-    done = [engine.send(landing, dst.at[me], there)]
-    to_y = engine.send(landing.at[first], dst.at[me, first], partner)
-    to_x = [engine.send(landing.at[second], dst.at[me, second], x_peer(d)) for d in (1, 2, 3)]
-    final = []
-    for d in (1, 2, 3):
-        copy = engine.send(landing.at[first], dst.at[me, first], x_peer(d))
-        final.append((slot(lax.rem(x + 4 - d, 4), yl), first, copy))
-    final.append((other, second, engine.send(landing.at[second], dst.at[me, second], partner)))
-    yield
-
-    def pass_on(index, part):
-        block = dst.at[index, part]
-        done.append(engine.send(block, block, there))
-
+    siblings = [engine.send(landing, dst.at[me], there)]
+    to_y = send(landing.at[first], me, first, partner)
+    round_b = [send(landing.at[second], me, second, x_peer(d)) for d in (1, 3)]
+    round_a = [send(landing.at[first], me, first, x_peer(d)) for d in (1, 3)]
+    over = [send(landing.at[second], me, second, partner)]
+    yield
     to_y.wait_recv()
-    block = dst.at[other, first]
-    for d in (1, 2, 3):
-        final.append((slot(lax.rem(x + 4 - d, 4), 1 - yl), first, engine.send(block, block, x_peer(d))))
-    pass_on(other, first)
-    for d in (1, 2, 3):
-        to_x[d - 1].wait_recv()
-        source = lax.rem(x + 4 - d, 4)
-        block = dst.at[slot(source, yl), second]
-        final.append((slot(source, 1 - yl), second, engine.send(block, block, partner)))
-        pass_on(slot(source, yl), second)
-    yield
-    for index, part, copy in final:
-        copy.wait_recv()
-        pass_on(index, part)
+    round_c = [on(slot(0, other), first, x_peer(d)) for d in (1, 3)]
+    siblings.append(hand(slot(0, other), first))
+    onward = []
+    for k, (d, to) in enumerate(((3, 1), (1, 3))):
+        round_b[k].wait_recv()
+        onward.append(on(slot(d, yl), odd[k], x_peer(to)))
+        over.append(on(slot(d, yl), second, partner))
+        siblings.append(hand(slot(d, yl), second))
+    for k, (d, to) in enumerate(((3, 1), (1, 3))):
+        round_a[k].wait_recv()
+        onward.append(on(slot(d, yl), even[k], x_peer(to)))
+        siblings.append(hand(slot(d, yl), first))
+    yield
+    for k in range(2):
+        onward[k].wait_recv()
+    over.append(on(slot(2, yl), second, partner))
+    siblings.append(hand(slot(2, yl), second))
+    for k, (d, to) in enumerate(((3, 1), (1, 3))):
+        round_c[k].wait_recv()
+        onward.append(on(slot(d, other), even[k], x_peer(to)))
+        siblings.append(hand(slot(d, other), first))
+    yield
+    for k in (2, 3):
+        onward[k].wait_recv()
+    siblings.append(hand(slot(2, yl), first))
+    for k, d in enumerate((0, 3, 1, 2)):
+        over[k].wait_recv()
+        siblings.append(hand(slot(d, other), second))
+    for k in (4, 5):
+        onward[k].wait_recv()
+    siblings.append(hand(slot(2, other), first))
     yield
     local.wait()
-    for copy in [to_y] + to_x + [c for _, _, c in final]:
+    for copy in siblings:
+        copy.wait_recv()
+    siblings[0].wait_send()
+    for copy in sent:
         copy.wait_send()
-    for copy in done:
-        copy.wait()
 
 
 def group_peer(dz, dc):
@@ -539,7 +606,7 @@
         lse_ref[:, start:stop] = top + jnp.log(total)
 
 
-def attend_back(kept_ref, do_ref, wide_ref, lse_ref, row_ref, col_ref, cos_ref, sin_ref, out_ref, dk_ref, dv_ref):
+def attend_back(kept_ref, do_ref, wide_ref, lse_ref, row_ref, col_ref, cos_ref, sin_ref, out_ref, sum_ref):
     cosine, sine = cos_ref[...], sin_ref[...]
     q_t, k_t, do_t = kept_ref[:HEAD], kept_ref[HEAD : 2 * HEAD], do_ref[...]
     queries = q_t.astype(F32).T.astype(BF16)
@@ -549,8 +616,7 @@
     centre = jnp.sum(do_t.astype(F32) * wide_ref[...], axis=0, keepdims=True)
     lse = lse_ref[...]
     seg_row, seg_col = row_ref[...], col_ref[...]
-    dk_ref[...] = jnp.zeros_like(dk_ref)
-    dv_ref[...] = jnp.zeros_like(dv_ref)
+    sum_ref[...] = jnp.zeros_like(sum_ref)
     dq_parts = []
     for start in range(0, SEQ, QB):
         stop = start + QB
@@ -559,12 +625,14 @@
         probs = jnp.exp(scores - lse[:, start:stop])
         d_probs = dot(values[:stop], do_t[:, start:stop], (1, 0))
         d_scores = (probs * (d_probs - centre[:, start:stop])).astype(BF16)
-        dv_ref[:stop] += dot(probs.astype(BF16), grads[start:stop], (1, 0))
-        dk_ref[:stop] += dot(d_scores, queries[start:stop], (1, 0))
+        d_keys = dot(d_scores, queries[start:stop], (1, 0))
+        d_values = dot(probs.astype(BF16), grads[start:stop], (1, 0))
+        sum_ref[:stop] += jnp.concatenate([d_keys, d_values], axis=1)
         dq_parts.append(dot(k_t[:, :stop], d_scores, (1, 0)) * 0.125)
     out_ref[:HEAD] = rope_back(jnp.concatenate(dq_parts, axis=1), cosine, sine).astype(BF16)
-    out_ref[HEAD : 2 * HEAD] = rope_back(dk_ref[...].T, cosine, sine).astype(BF16)
-    out_ref[2 * HEAD :] = dv_ref[...].T.astype(BF16)
+    turned = sum_ref[...].T
+    out_ref[HEAD : 2 * HEAD] = rope_back(turned[:HEAD], cosine, sine).astype(BF16)
+    out_ref[2 * HEAD :] = turned[HEAD:].astype(BF16)
 
 
 def small_peer(dz, dh):
@@ -622,12 +690,13 @@
     ("item", (3 * HEAD, SEQ), BF16),
     ("out", (HEAD, SEQ), BF16),
     ("o_rows", (ROWS, 4 * HEAD), BF16),
-    ("give", (4, OWN, WIDTH), BF16),
     ("other", (4, OWN, WIDTH), BF16),
-    ("own", (4, OWN, WIDTH), F32),
-    ("total", (3, OWN, WIDTH), BF16),
+    ("product", (ROWS, WIDTH), BF16),
     ("arrived", (3, OWN, WIDTH), BF16),
 ]
+
+
+FIRST_PARTS = ("sum_y_", "sum_x_", "by_y_", "by_x_", "relay_y_", "relay_x_")
 
 
 class Refs:
@@ -643,16 +712,12 @@
     engine = Engine(*refs[len(names) :])
     z, x, yl, core, yh = place()
     y = yh * 2 + yl
-    greet(FORWARD_PEERS)
 
     load_qkv = engine.local(r.w_qkv.at[:, rows_at(x, 128)], r.held_qkv)
+    load_gu = engine.local(r.w_gate_up.at[rows_at(x, 128)], r.held_gu)
     load_x = engine.local(r.tokens.at[rows_at(core, OWN)], r.near_x)
     load_dy = engine.local(r.cotangent.at[rows_at(core, OWN)], r.near_dy)
-    swap_x = engine.send(r.tokens.at[rows_at(1 - core, OWN)], r.far_x, sibling())
-    smalls = [engine.send(r.packed, r.small.at[z, yh], small_peer(dz, dh)) for dz, dh in SMALL_ALL]
     small_here = engine.local(r.packed, r.small.at[z, yh])
-    load_gu = engine.local(r.w_gate_up.at[rows_at(x, 128)], r.held_gu)
-    swap_dy = engine.send(r.cotangent.at[rows_at(1 - core, OWN)], r.far_dy, sibling())
 
     def rows_of(n):
         return lambda zz: rows_at((zz * 2 + core) * 2 + yl, n)
@@ -665,7 +730,17 @@
         r.turned[:1024, :] = r.held_qkv[part].astype(F32).T
         for zz in range(4):
             r.cut_qkv[zz, part * HEAD : (part + 1) * HEAD] = r.turned[rows_of(HEAD)(zz), :].astype(BF16)
+    greet(FORWARD_PEERS)
     pieces_qkv = send_pieces(engine, lambda zz: r.cut_qkv.at[zz], slots_of(r.p_qkv))
+    swap_x = engine.send(r.tokens.at[rows_at(1 - core, OWN)], r.far_x, sibling())
+    smalls = [engine.send(r.packed, r.small.at[z, yh], small_peer(dz, dh)) for dz, dh in SMALL_ALL]
+    pieces_out = send_pieces(engine, lambda zz: r.w_out.at[rows_of(64)(zz), lanes(x)], slots_of(r.p_out))
+    swap_dy = engine.send(r.cotangent.at[rows_at(1 - core, OWN)], r.far_dy, sibling())
+    load_gu.wait()
+    for g, cut in ((0, r.cut_gate), (1, r.cut_up)):
+        r.turned[...] = r.held_gu[:, g, :].astype(F32).T
+        for zz in range(4):
+            cut[zz] = r.turned[rows_of(176)(zz), :].astype(BF16)
 
     stays = core == yh
     load_x.wait()
@@ -689,7 +764,6 @@
     pieces_qkv[0].wait()
     weight_qkv = gather_weight(engine, r.p_qkv, r.m_qkv)
     next(weight_qkv)
-    pieces_out = send_pieces(engine, lambda zz: r.w_out.at[rows_of(64)(zz), lanes(x)], slots_of(r.p_out))
 
     lane_at = lax.broadcasted_iota(jnp.int32, (64, 128), 1)
     for h in range(2):
@@ -705,18 +779,11 @@
     r.seg_col[...] = jnp.concatenate([marks[:, k : k + 1] for k in range(16)], axis=0)
 
     next(weight_qkv)
-    load_gu.wait()
-    r.turned[...] = r.held_gu[:, 0, :].astype(F32).T
-    for zz in range(4):
-        r.cut_gate[zz] = r.turned[rows_of(176)(zz), :].astype(BF16)
     next(tokens_h1)
+    pieces_down = send_pieces(engine, lambda zz: r.w_down.at[rows_of(176)(zz), lanes(x)], slots_of(r.p_down))
+    pieces_gate = send_pieces(engine, lambda zz: r.cut_gate.at[zz], slots_of(r.p_gate))
+    pieces_up = send_pieces(engine, lambda zz: r.cut_up.at[zz], slots_of(r.p_up))
     next(weight_qkv)
-    pieces_gate = send_pieces(engine, lambda zz: r.cut_gate.at[zz], slots_of(r.p_gate))
-    pieces_down = send_pieces(engine, lambda zz: r.w_down.at[rows_of(176)(zz), lanes(x)], slots_of(r.p_down))
-    r.turned[...] = r.held_gu[:, 1, :].astype(F32).T
-    for zz in range(4):
-        r.cut_up[zz] = r.turned[rows_of(176)(zz), :].astype(BF16)
-    pieces_up = send_pieces(engine, lambda zz: r.cut_up.at[zz], slots_of(r.p_up))
 
     def start_weight(pieces, piece, matrix):
         pieces[0].wait()
@@ -732,29 +799,22 @@
     dy_rows = jnp.where(stays, r.near_dy[...].astype(F32), r.far_dy[...].astype(F32))
     r.dy_own[...] = spread(dy_rows).astype(BF16)
     finish(tokens_h1)
+    next(weight_out)
     finish(weight_qkv)
 
-    place_here = lanes(x * 4 + yl * 2 + yh)
-    to_items, stay = [], None
-    for dy in (2, 1, 3, 0):
-        ty = lax.rem(y + dy, 4)
-        rows = rows_at(ty, 3 * HEAD)
-        r.qkv_t[rows, :] = (dot(r.m_qkv[ty], r.h1[...], (1, 1)) + r.bias[ty]).astype(BF16)
-        for dx in (2, 1, 3, 0):
-            block = r.qkv_t.at[rows, lanes(lax.rem(x + dx, 4))]
-            if dx or dy:
-                to_items.append(engine.send(block, r.item.at[:, place_here], xy_peer(dx, dy)))
-            else:
-                stay = engine.local(block, r.item.at[:, place_here])
+    r.qkv_t[...] = (
+        dot(r.m_qkv[...].reshape(12 * HEAD, WIDTH), r.h1[...], (1, 1)) + r.bias[...].reshape(12 * HEAD, 1)
+    ).astype(BF16)
+    to_items = send_items(engine, r.qkv_t, r.item, 3 * HEAD)
     tokens_dy = gather_tokens(engine, r.dy_own, r.dy)
     next(tokens_dy)
-    next(weight_out)
-    stay.wait()
-    for copy in to_items:
-        copy.wait_recv()
-    next(weight_out)
     weight_down = start_weight(pieces_down, r.p_down, r.m_down)
     weight_gate = start_weight(pieces_gate, r.p_gate, r.m_gate)
+    weight_up = start_weight(pieces_up, r.p_up, r.m_up)
+    to_items[-1].wait()
+    for copy in to_items[:-1]:
+        copy.wait_recv()
+    next(weight_out)
     attend(r.item, r.seg_row, r.seg_col, r.cos, r.sin, r.out, r.wide, r.lse, r.kept)
     back = return_items(engine, r.out, r.o_t, HEAD)
     next(weight_down)
@@ -766,40 +826,29 @@
 
     r.o_rows[...] = r.o_t[...].astype(F32).T.astype(BF16)
     matrix = r.m_out[...].reshape(4 * HEAD, WIDTH)
-    to_core = []
-    for i in range(4):
-        base = lax.rem(z + 1 + i, 4) * 2
-        r.give[i] = dot(r.o_rows[rows_at(base + 1 - core, OWN), :], matrix, (1, 0)).astype(BF16)
-        to_core.append(engine.send(r.give.at[i], r.other.at[i], sibling()))
-        r.own[i] = dot(r.o_rows[rows_at(base + core, OWN), :], matrix, (1, 0))
-    to_z = []
-    for i in range(3):
-        to_core[i].wait_recv()
-        r.total[i] = (r.own[i] + r.other[i].astype(F32)).astype(BF16)
-        to_z.append(engine.send(r.total.at[i], r.arrived.at[i], z_peer(i + 1)))
+    out = scatter_product(engine, r.o_rows, matrix, r.middle, r.product, r.other, r.arrived)
+    next(out)
+    next(out)
     next(weight_gate)
+    next(weight_up)
     next(weight_down)
-    weight_up = start_weight(pieces_up, r.p_up, r.m_up)
-    to_core[3].wait_recv()
-    r.middle[...] = x_rows + r.own[3] + r.other[3].astype(F32)
-    for copy, arrived in zip(to_z, range(3)):
-        copy.wait_recv()
-        r.middle[...] += r.arrived[arrived].astype(F32)
+    next(weight_gate)
+    next(out)
+    r.middle[...] += x_rows
 
     h2_full, _, _ = layer_norm(r.middle[...], r.norms[1:2], r.norms[3:4])
     r.h2_own[...] = h2_full.astype(BF16)
     tokens_h2 = gather_tokens(engine, r.h2_own, r.h2)
     next(tokens_h2)
     next(weight_up)
-    next(weight_gate)
+    next(tokens_h2)
     finish(weight_down)
-    next(weight_up)
-    next(tokens_h2)
     finish(weight_gate)
     finish(tokens_dy)
     finish(weight_up)
     finish(tokens_h2)
-    sent = smalls + to_items + back[:-1] + to_core + to_z + [swap_x, swap_dy]
+    finish(out)
+    sent = smalls + to_items[:-1] + back[:-1] + [swap_x, swap_dy]
     for pieces in (pieces_qkv, pieces_out, pieces_gate, pieces_down, pieces_up):
         sent += pieces[1:]
     for copy in sent:
@@ -839,7 +888,8 @@
 BACKWARD_OUTS = [
     ("layer_out", (2 * OWN, WIDTH), BF16, ANY),
     ("grad_tokens", (2 * OWN, WIDTH), BF16, ANY),
-    ("mlp_all", (16, 4, 528, 128), BF16, ANY),
+    ("gd_all", (16, 4, 352, 128), BF16, ANY),
+    ("up_all", (16, 4, 176, 128), BF16, ANY),
     ("attn_all", (16, 4, 256, 128), BF16, ANY),
     ("norm_sum", (8, 512), F32, VMEM),
     ("bias_all", (8, 8, 768), F32, VMEM),
@@ -859,22 +909,20 @@
     ("own_mlp", (4, OWN, WIDTH), BF16),
     ("other_mlp", (4, OWN, WIDTH), BF16),
     ("arrived_mlp", (3, OWN, WIDTH), BF16),
-    ("give", (4, OWN, WIDTH), BF16),
-    ("own_dh1", (4, OWN, WIDTH), F32),
+    ("product", (ROWS, WIDTH), BF16),
     ("other_dh1", (4, OWN, WIDTH), BF16),
-    ("total_dh1", (3, OWN, WIDTH), BF16),
     ("arrived_dh1", (3, OWN, WIDTH), BF16),
     ("own_y", (128, WIDTH), BF16),
     ("own_x", (4, 128, 512), BF16),
     ("d_o", (4 * HEAD, ROWS), BF16),
     ("item", (HEAD, SEQ), BF16),
     ("item_out", (3 * HEAD, SEQ), BF16),
-    ("dk", (SEQ, HEAD), F32),
-    ("dv", (SEQ, HEAD), F32),
+    ("d_kv", (SEQ, 2 * HEAD), F32),
     ("d_qkv", (12 * HEAD, ROWS), BF16),
     ("d_rows", (ROWS, 12 * HEAD), BF16),
     ("g_attn", (4, 256, WIDTH), BF16),
-    ("landing_mlp", (4, 528, 128), BF16),
+    ("landing_gd", (4, 352, 128), BF16),
+    ("landing_up", (4, 176, 128), BF16),
     ("landing_attn", (4, 256, 128), BF16),
     ("small_norms", (8, WIDTH), F32),
     ("small_bias", (8, 768), F32),
@@ -887,8 +935,10 @@
     BACKWARD_SCRATCH += [
         ("sum_y_" + _name, (_cut, WIDTH), BF16),
         ("sum_x_" + _name, (4, _n - _cut, 512), BF16),
-        ("by_y_" + _name, (3, _cut, WIDTH), BF16),
-        ("by_x_" + _name, (3, 4, _n - _cut, 512), BF16),
+        ("by_y_" + _name, (2, _cut, WIDTH), BF16),
+        ("by_x_" + _name, (2, 4, _n - _cut, 512), BF16),
+        ("relay_y_" + _name, (_cut, WIDTH), BF16),
+        ("relay_x_" + _name, (4, _n - _cut, 512), BF16),
         ("rest_x_" + _name, (3, _cut, 512), BF16),
         ("rest_y_" + _name, (3, _n - _cut, 512), BF16),
         ("rest_own_" + _name, (_n, 512), BF16),
@@ -904,10 +954,12 @@
     engine = Engine(*refs[len(names) :])
     z, x, yl, core, yh = place()
     y = yh * 2 + yl
+    load_h1 = engine.local(r.h1, r.v_h1)
+    load_qkv = engine.local(r.m_qkv, r.v_qkv)
     greet(BACKWARD_PEERS)
 
     def first_of(name, grad):
-        parts = [getattr(r, part + name) for part in ("sum_y_", "sum_x_", "by_y_", "by_x_")]
+        parts = [getattr(r, part + name) for part in FIRST_PARTS]
         thread = sum_first(engine, grad, *parts, r.own_y, r.own_x)
         next(thread)
         return thread
@@ -918,19 +970,19 @@
         next(thread)
         return thread
 
-    def mlp_landing(first):
-        return lambda zz: r.landing_mlp.at[zz, pl.ds(first, 176)]
+    def part_of(landing, first):
+        return lambda zz: landing.at[zz, pl.ds(first, 176)]
 
     dh2 = scatter_tokens(engine, r.back_part, r.summed, r.own_dh2, r.other_dh2, r.arrived_dh2)
     next(dh2)
     gate = first_of("gate", r.g_gate)
     down = first_of("down", r.g_down)
-    load_h1 = engine.local(r.h1, r.v_h1)
-    load_qkv = engine.local(r.m_qkv, r.v_qkv)
     next(dh2)
     mlp = scatter_tokens(engine, r.mlp_part, r.d_middle, r.own_mlp, r.other_mlp, r.arrived_mlp)
     next(mlp)
     _, normed_b, rstd_b = layer_norm(r.middle[...], r.norms[1:2], r.norms[3:4])
+    next(gate)
+    next(down)
     next(dh2)
     back_b, gain_b, shift_b = norm_back(r.summed[...], normed_b, rstd_b, r.norms[1:2])
     d_middle = r.dy_own[...].astype(F32) + back_b
@@ -939,68 +991,60 @@
     next(tokens_dz)
     r.small_norms[1:2] = gain_b[None]
     r.small_norms[3:4] = shift_b[None]
-    next(mlp)
     next(gate)
-    rest_gate = rest_of("gate", mlp_landing(0))
+    rest_gate = rest_of("gate", part_of(r.landing_gd, 0))
+    next(down)
+    rest_down = rest_of("down", part_of(r.landing_gd, 176))
     next(tokens_dz)
     finish(tokens_dz)
-
-    place_here = lanes(x * 4 + yl * 2 + yh)
-    to_items, stay = [], None
-    for dy in (2, 1, 3, 0):
-        ty = lax.rem(y + dy, 4)
-        rows = rows_at(ty, HEAD)
-        r.d_o[rows, :] = dot(r.m_out[ty], r.dz[...], (1, 1)).astype(BF16)
-        for dx in (2, 1, 3, 0):
-            block = r.d_o.at[rows, lanes(lax.rem(x + dx, 4))]
-            if dx or dy:
-                to_items.append(engine.send(block, r.item.at[:, place_here], xy_peer(dx, dy)))
-            else:
-                stay = engine.local(block, r.item.at[:, place_here])
+    next(mlp)
+
+    r.d_o[...] = dot(r.m_out[...].reshape(4 * HEAD, WIDTH), r.dz[...], (1, 1)).astype(BF16)
+    to_items = send_items(engine, r.d_o, r.item, HEAD)
     up = first_of("up", r.g_up)
+    g_out = dot(r.o_t[...], r.dz[...], (1, 0)).astype(BF16)
+    for q in range(4):
+        r.g_attn[q, 192:] = g_out[q * HEAD : (q + 1) * HEAD]
+    next(rest_gate)
+    next(rest_down)
+    to_items[-1].wait()
+    for copy in to_items[:-1]:
+        copy.wait_recv()
+    attend_back(
+        r.kept, r.item, r.wide, r.lse, r.seg_row, r.seg_col, r.cos, r.sin, r.item_out, r.d_kv
+    )
+    back = return_items(engine, r.item_out, r.d_qkv, 3 * HEAD)
+    next(up)
+    next(rest_gate)
+    next(rest_down)
+    gather_gd = gather_ctx(engine, r.landing_gd, r.gd_all)
+    next(gather_gd)
     next(mlp)
     r.out_own[...] = spread(r.middle[...] + r.d_middle[...]).astype(BF16)
     r.d_middle[...] = d_middle
     hand_out = hand_back(engine, r.out_own, r.layer_out)
     next(hand_out)
-    for q in range(4):
-        r.g_attn[q, 192:] = dot(r.o_t[q * HEAD : (q + 1) * HEAD, :], r.dz[...], (1, 0)).astype(BF16)
-    stay.wait()
-    for copy in to_items:
-        copy.wait_recv()
-    next(down)
-    rest_down = rest_of("down", mlp_landing(352))
-    attend_back(
-        r.kept, r.item, r.wide, r.lse, r.seg_row, r.seg_col, r.cos, r.sin, r.item_out, r.dk, r.dv
-    )
-    back = return_items(engine, r.item_out, r.d_qkv, 3 * HEAD)
-    next(rest_gate)
-    next(rest_down)
-    next(up)
-    rest_up = rest_of("up", mlp_landing(176))
+    load_h1.wait()
+    load_qkv.wait()
     back[-1].wait()
     for copy in back[:-1]:
         copy.wait_recv()
 
-    load_h1.wait()
-    load_qkv.wait()
     r.d_rows[...] = r.d_qkv[...].astype(F32).T.astype(BF16)
     matrix = r.v_qkv[...].reshape(12 * HEAD, WIDTH)
-    dh1 = scatter_product(
-        engine, r.d_rows, matrix, r.summed, r.give, r.own_dh1, r.other_dh1, r.total_dh1, r.arrived_dh1
-    )
+    dh1 = scatter_product(engine, r.d_rows, matrix, r.summed, r.product, r.other_dh1, r.arrived_dh1)
     next(dh1)
+    g_qkv = dot(r.d_qkv[...], r.v_h1[...], (1, 0)).astype(BF16)
     for q in range(4):
-        rows = slice(q * 3 * HEAD, (q + 1) * 3 * HEAD)
-        r.g_attn[q, :192] = dot(r.d_qkv[rows, :], r.v_h1[...], (1, 0)).astype(BF16)
+        r.g_attn[q, :192] = g_qkv[q * 3 * HEAD : (q + 1) * 3 * HEAD]
     attn = first_of("attn", r.g_attn)
+    next(dh1)
     r.small_bias[...] = dot(jnp.ones((8, ROWS), BF16), r.d_qkv[...], (1, 1))
-    next(rest_up)
-    for thread in (rest_gate, rest_down, rest_up):
-        next(thread)
-    gather_mlp = gather_ctx(engine, r.landing_mlp, r.mlp_all)
-    next(gather_mlp)
     _, normed_a, rstd_a = layer_norm(r.x_own[...].astype(F32), r.norms[0:1], r.norms[2:3])
+    next(up)
+    rest_up = rest_of("up", part_of(r.landing_up, 0))
+    next(gather_gd)
+    next(attn)
     next(dh1)
     back_a, gain_a, shift_a = norm_back(r.summed[...], normed_a, rstd_a, r.norms[0:1])
     r.grad_own[...] = spread(r.d_middle[...] + back_a).astype(BF16)
@@ -1014,23 +1058,31 @@
         engine, r.small_norms, r.small_bias, r.norm_sum, r.bias_all, r.by_group, r.small_x, r.small_y
     )
     next(small)
+    next(rest_up)
     next(attn)
     rest_attn = rest_of("attn", lambda zz: r.landing_attn.at[zz])
+    next(rest_up)
+    gather_up = gather_ctx(engine, r.landing_up, r.up_all)
+    next(gather_up)
     next(small)
+    next(gather_gd)
     next(rest_attn)
     next(small)
     next(rest_attn)
     gather_attn = gather_ctx(engine, r.landing_attn, r.attn_all)
     next(gather_attn)
-    next(gather_mlp)
+    next(gather_up)
     next(small)
+    next(gather_gd)
     next(gather_attn)
-    next(gather_mlp)
+    next(gather_up)
+    next(gather_attn)
+    next(gather_up)
     next(gather_attn)
     threads = (dh2, mlp, gate, down, up, attn, rest_gate, rest_down, rest_up, rest_attn)
-    for thread in threads + (hand_out, dh1, hand_grad, small, gather_mlp, gather_attn):
+    for thread in threads + (hand_out, dh1, hand_grad, small, gather_gd, gather_up, gather_attn):
         finish(thread)
-    for copy in to_items + back[:-1]:
+    for copy in to_items[:-1] + back[:-1]:
         copy.wait_send()
 
 
@@ -1041,7 +1093,7 @@
         out_shape=[jax.ShapeDtypeStruct(o[1], o[2]) for o in BACKWARD_OUTS],
         in_specs=[ANY] * len(BACKWARD_FAR) + [VMEM] * len(BACKWARD_NEAR),
         out_specs=[o[3] for o in BACKWARD_OUTS],
-        scratch_shapes=[pltpu.VMEM(shape, dtype) for _, shape, dtype in BACKWARD_SCRATCH] + semaphores(240, 48),
+        scratch_shapes=[pltpu.VMEM(shape, dtype) for _, shape, dtype in BACKWARD_SCRATCH] + semaphores(320, 64),
         compiler_params=pltpu.CompilerParams(
             collective_id=2, has_side_effects=True, vmem_limit_bytes=58 * 2**20
         ),
@@ -1049,13 +1101,13 @@
     )(*given)
 
 
-def assemble_kernel(mlp_ref, attn_ref, gu_ref, down_ref, qkv_ref, out_ref, turned):
+def assemble_kernel(gd_ref, up_ref, attn_ref, gu_ref, down_ref, qkv_ref, out_ref, turned):
     for g in range(2):
         for zz in range(4):
             for core in range(2):
                 for yl in range(2):
                     row = zz * 704 + core * 352 + yl * 176
-                    block = mlp_ref[0, yl * 2 + core, zz, g * 176 : (g + 1) * 176]
+                    block = up_ref[0, yl * 2 + core, zz] if g else gd_ref[0, yl * 2 + core, zz, :176]
                     turned[row : row + 176, :] = block.astype(F32)
         for t in range(22):
             gu_ref[:, g, t * 128 : (t + 1) * 128] = turned[t * 128 : (t + 1) * 128, :].T
@@ -1063,7 +1115,7 @@
         for core in range(2):
             for yl in range(2):
                 row = zz * 704 + core * 352 + yl * 176
-                down_ref[row : row + 176, :] = mlp_ref[0, yl * 2 + core, zz, 352:].astype(F32)
+                down_ref[row : row + 176, :] = gd_ref[0, yl * 2 + core, zz, 176:].astype(F32)
                 row = zz * 256 + core * 128 + yl * 64
                 out_ref[row : row + 64, :] = attn_ref[0, yl * 2 + core, zz, 192:].astype(F32)
             for part in range(3):
@@ -1073,14 +1125,16 @@
                 qkv_ref[part, :, column : column + 128] = block.astype(F32).T
 
 
-def assemble(mlp_all, attn_all):
-    mlp_all = mlp_all.reshape(4, 4, 4, 528, 128)
+def assemble(gd_all, up_all, attn_all):
+    gd_all = gd_all.reshape(4, 4, 4, 352, 128)
+    up_all = up_all.reshape(4, 4, 4, 176, 128)
     attn_all = attn_all.reshape(4, 4, 4, 256, 128)
     return pl.pallas_call(
         assemble_kernel,
         grid=(4,),
         in_specs=[
-            pl.BlockSpec((1, 4, 4, 528, 128), lambda i: (i, 0, 0, 0, 0)),
+            pl.BlockSpec((1, 4, 4, 352, 128), lambda i: (i, 0, 0, 0, 0)),
+            pl.BlockSpec((1, 4, 4, 176, 128), lambda i: (i, 0, 0, 0, 0)),
             pl.BlockSpec((1, 4, 4, 256, 128), lambda i: (i, 0, 0, 0, 0)),
         ],
         out_specs=[
@@ -1098,7 +1152,7 @@
         scratch_shapes=[pltpu.VMEM((2816, 128), F32)],
         compiler_params=pltpu.CompilerParams(vmem_limit_bytes=48 * 2**20),
         name="assemble",
-    )(mlp_all, attn_all)
+    )(gd_all, up_all, attn_all)
 
 
 def rotation_tables():
@@ -1162,12 +1216,12 @@
     g_gate, g_up, g_down = weight_grad(d_gate, h2), weight_grad(d_up, h2), weight_grad(act, dy)
     values = dict(vars(f), cos=cosine, sin=sine, back_part=back_part, mlp_part=mlp_part)
     values.update(g_gate=g_gate, g_up=g_up, g_down=g_down)
-    layer_out, grad_tokens, mlp_all, attn_all, norm_sum, bias_all = backward(values)
+    layer_out, grad_tokens, gd_all, up_all, attn_all, norm_sum, bias_all = backward(values)
 
     bias_all = bias_all[:, 0].reshape(4, 2, 2, 2, 3, 4, 16)
     bias_all = pick(pick(bias_all, 2, yh), 4, z)
     grad_bias = bias_all.transpose(3, 0, 1, 2, 4).reshape(3, 16, 16)
-    out_gu, out_down, out_qkv, out_out = assemble(mlp_all, attn_all)
+    out_gu, out_down, out_qkv, out_out = assemble(gd_all, up_all, attn_all)
     return (
         layer_out[None],
         grad_tokens.astype(F32)[None],

time: 362 us -> 340 us (0.939)
  Pallas kernels: 317 us -> 285 us
  matrix products: 27.5 us -> 39.6 us
    pallas_call x1, Pallas kernels: 188 us -> 157 us  [backward(): pl.pallas_call(backward_kernel, out_shape=[jax.ShapeDtypeStruct(o[1], o[2...]
    dot_general x9, matrix products: 27.5 us -> 39.6 us  [dot(): lax.dot_general(a, b, ((dims[:1], dims[1:]), ((), ())), preferred_element...]
where the time goes in v5:
time: 340 us; the launch traced here: 337 us
  Pallas kernels  285 us (84%)
  matrix products  39.6 us (12%)
  local copies, waits for them, and re-layouts  8.82 us (3%)
    pallas_call x1, Pallas kernels, backward(): pl.pallas_call(backward_kernel, out_shape=[jax.ShapeDtypeStruct(o[1], o[2...  157 us
    pallas_call x1, Pallas kernels, forward(): pl.pallas_call(forward_kernel, out_shape=[jax.ShapeDtypeStruct(o[1], o[2]...  114 us
    dot_general x9, matrix products, dot(): lax.dot_general(a, b, ((dims[:1], dims[1:]), ((), ())), preferred_element...  39.6 us
    pallas_call x1, Pallas kernels, assemble(): pl.pallas_call(assemble_kernel, grid=(4,), in_specs=[pl.BlockSpec((1, 4,...  14.3 us

profile of v5, /device:TPU:1, one launch (start us, length us, event | category | flops | bytes accessed | tf_op | source)
XLA Modules:
  0.0 337.4 jit_solution(2684790523115925873)
XLA Ops:
  0.7 0.3 multiply_sine_fusion
  1.0 0.0 copy-start.2
  1.0 0.0 copy-start.3
  1.0 0.8 copy.31
  1.8 0.1 copy.24
  1.9 0.7 convert_reduce_fusion
  2.6 0.7 fusion.2.refs_2_
  3.3 0.0 copy-start.4
  3.4 1.0 copy-done.4
  4.4 0.0 copy-start.5
  4.4 1.0 copy-done.5
  5.4 113.5 %forward.1 = (bf16[4,192,2048]{2,1,0:T(8,128)(2,1)}, bf16[4,64,2048]{2,1,0:T(8,128)(2,1)}, bf16[4,176,2048]{2,1,0:T(8,128)(2,1)}, bf16[4,176,2048]{2,1,0:T(8,128...) custom-call(bf16[128,2048]{1,0:T(8,128)(2,1)S(1)} %bitcast.48, ...), custom_call_target="tpu_custom_call" | custom-call | tf_op jit(solution)/shard_map/forward/pallas_call | solution.py:859
  119.0 0.0 copy-done.2
  119.0 0.0 copy-done.3
  119.0 0.0 copy-start.1
  119.0 0.0 copy-start.6
  119.0 0.0 copy-start.7
  119.0 0.0 copy-start.8
  119.0 0.0 copy-start.9
  119.0 0.0 copy-start.10
  119.0 0.0 copy-start.11
  119.1 0.0 copy-start.12
  119.1 0.0 copy-start.13
  119.1 0.0 copy-start.19
  119.1 0.0 copy-start.21
  119.1 5.1 %fusion.5 = f32[704,512]{1,0:T(8,128)S(1)} fusion(bf16[704,2048]{1,0:T(8,128)(2,1)} %bitcast.56, bf16[512,2048]{1,0:T(8,128)(2,1)} %get-tuple-element.41), kind=kOutput, calls=%fused_computation.25 | convolution fusion | flops 1476395008 | bytes 6422528 | tf_op jit(solution)/shard_map/dot_general | solution.py:543
  124.2 0.0 copy-done.1
  124.2 0.0 copy-done.6
  124.2 0.0 copy-done.7
  124.2 0.0 copy-done.8
  124.2 0.0 copy-done.9
  124.2 0.0 copy-done.10
  124.2 0.0 copy-done.11
  124.2 0.0 copy-done.12
  124.2 0.0 copy-done.13
  124.3 0.0 copy-done.19
  124.3 0.0 copy-done.21
  124.3 0.0 copy-start.18
  124.3 0.0 copy-start.20
  124.3 1.7 fusion.4
  126.0 0.1 copy-done.18
  126.1 0.6 copy-done.20
  126.7 2.3 multiply_convert_fusion
  129.1 3.2 convolution_convert_fusion
  132.3 3.3 convolution_convert_fusion.1
  135.6 3.3 convolution_convert_fusion.2
  138.9 0.0 copy-start.14
  138.9 3.2 convolution_convert_fusion.3.refs_1_
  142.1 0.0 copy-done.14
  142.1 14.2 %fusion.6 = f32[512,2048]{1,0:T(8,128)S(1)} fusion(bf16[704,512]{1,0:T(8,128)(2,1)S(1)} %get-tuple-element.68, bf16[704,2048]{1,0:T(8,128)(2,1)S(1)} %bitcast.57), kind=kOutput, calls=%fused_computation.26 | convolution fusion | flops 1476395008 | bytes 7798784 | tf_op jit(solution)/shard_map/dot_general | solution.py:543
  156.3 3.3 add_convert_fusion.refs_0_
  159.6 157.1 %backward.1 = (bf16[128,2048]{1,0:T(8,128)(2,1)}, bf16[128,2048]{1,0:T(8,128)(2,1)}, bf16[16,4,352,128]{3,2,1,0:T(8,128)(2,1)}, bf16[16,4,176,128]{3,2,1,0:T(8,1...) custom-call(bf16[512,2048]{1,0:T(8,128)(2,1)} %add_convert_fusion.refs_0_, ...), custom_call_target="tpu_custom_call" | custom-call | tf_op jit(solution)/shard_map/backward/pallas_call | solution.py:1091
  316.7 0.0 copy-start
  316.7 1.8 copy-done
  318.5 14.3 %assemble.1 = (f32[512,2,2816]{2,1,0:T(2,128)}, f32[2816,512]{1,0:T(8,128)}, f32[3,512,1024]{2,1,0:T(8,128)}, f32[1024,512]{1,0:T(8,128)}) custom-call(bf16[4,4,4,352,128]{4,3,2,1,0:T(8,128)(2,1)} %bitcast.50, bf16[4,4,4,176,128]{4,3,2,1,0:T(8,128)(2,1)S(1)} %bitcast.47, bf16[4,4,4,256,128]{4,3,2,1,0:T(8,128)(2,1)} %bitcast.51), custom_call_target="tpu_custom_call" | custom-call | tf_op jit(solution)/shard_map/assemble/pallas_call | solution.py:1132
  332.8 0.0 copy-done.15
  332.8 1.1 bitcast_convert_fusion
  333.9 1.0 slice_reduce_fusion
  334.9 0.2 reshape_squeeze.3
  335.2 0.6 copy.26
  335.8 0.0 copy-done.17
  335.8 0.6 fusion.3
  336.4 0.0 copy-done.16
  336.4 0.8 copy.33
  (10 shorter events, 0.1 us)
Async XLA Ops:
  1.0 118.0 %copy-start.2 = (f32[8,2048]{1,0:T(8,128)}, f32[8,2048]{1,0:T(8,128)S(1)}, u32[]{:S(2)}) copy-start(f32[8,2048]{1,0:T(8,128)S(1)} %get-tuple-element.72.refs_8_.refs_19_) | copy-start | bytes 196612
  1.0 118.0 %copy-start.3 = (f32[8,2048]{1,0:T(8,128)}, f32[8,2048]{1,0:T(8,128)S(1)}, u32[]{:S(2)}) copy-start(f32[8,2048]{1,0:T(8,128)S(1)} %get-tuple-element.73.refs_7_.refs_18_) | copy-start | bytes 196612
  3.3 1.0 copy-start.4
  4.4 1.0 copy-start.5
  119.0 5.2 %copy-start.1 = (bf16[192,2048]{1,0:T(8,128)(2,1)}, bf16[192,2048]{1,0:T(8,128)(2,1)S(1)}, u32[]{:S(2)}) copy-start(bf16[192,2048]{1,0:T(8,128)(2,1)S(1)} %get-tuple-element.51.refs_13_) | copy-start | bytes 2359300
  119.0 5.2 %copy-start.6 = (f32[64,2048]{1,0:T(8,128)}, f32[64,2048]{1,0:T(8,128)S(1)}, u32[]{:S(2)}) copy-start(f32[64,2048]{1,0:T(8,128)S(1)} %get-tuple-element.45.refs_7_) | copy-start | bytes 1572868
  119.0 5.2 %copy-start.7 = (f32[64,2048]{1,0:T(8,128)}, f32[64,2048]{1,0:T(8,128)S(1)}, u32[]{:S(2)}) copy-start(f32[64,2048]{1,0:T(8,128)S(1)} %get-tuple-element.52.refs_14_) | copy-start | bytes 1572868
  119.0 5.2 %copy-start.8 = (bf16[64,2048]{1,0:T(8,128)(2,1)}, bf16[64,2048]{1,0:T(8,128)(2,1)S(1)}, u32[]{:S(2)}) copy-start(bf16[64,2048]{1,0:T(8,128)(2,1)S(1)} %get-tuple-element.46.refs_8_) | copy-start | bytes 786436
  119.0 5.2 %copy-start.9 = (bf16[64,2048]{1,0:T(8,128)(2,1)}, bf16[64,2048]{1,0:T(8,128)(2,1)S(1)}, u32[]{:S(2)}) copy-start(bf16[64,2048]{1,0:T(8,128)(2,1)S(1)} %get-tuple-element.47.refs_9_) | copy-start | bytes 786436
  119.0 5.2 %copy-start.10 = (bf16[256,512]{1,0:T(8,128)(2,1)}, bf16[256,512]{1,0:T(8,128)(2,1)S(1)}, u32[]{:S(2)}) copy-start(bf16[256,512]{1,0:T(8,128)(2,1)S(1)} %get-tuple-element.50.refs_12_) | copy-start | bytes 786436
  119.0 5.2 %copy-start.11 = (f32[8,2048]{1,0:T(8,128)}, f32[8,2048]{1,0:T(8,128)S(1)}, u32[]{:S(2)}) copy-start(f32[8,2048]{1,0:T(8,128)S(1)} %get-tuple-element.48.refs_10_) | copy-start | bytes 196612
  119.1 5.2 %copy-start.12 = (f32[1,2048]{1,0:T(1,128)}, f32[1,2048]{1,0:T(1,128)S(1)}, u32[]{:S(2)}) copy-start(f32[1,2048]{1,0:T(1,128)S(1)} %get-tuple-element.53.refs_15_) | copy-start | bytes 24580
  119.1 5.2 %copy-start.13 = (f32[1,2048]{1,0:T(1,128)}, f32[1,2048]{1,0:T(1,128)S(1)}, u32[]{:S(2)}) copy-start(f32[1,2048]{1,0:T(1,128)S(1)} %get-tuple-element.54.refs_16_) | copy-start | bytes 24580
  119.1 5.2 %copy-start.19 = (bf16[4,176,2048]{2,1,0:T(8,128)(2,1)S(1)}, bf16[4,176,2048]{2,1,0:T(8,128)(2,1)}, u32[]{:S(2)}) copy-start(bf16[4,176,2048]{2,1,0:T(8,128)(2,1)} %get-tuple-element.38) | copy-start | bytes 8650756
  119.1 5.2 %copy-start.21 = (bf16[512,2048]{1,0:T(8,128)(2,1)S(1)}, bf16[512,2048]{1,0:T(8,128)(2,1)}, u32[]{:S(2)}) copy-start(bf16[512,2048]{1,0:T(8,128)(2,1)} %get-tuple-element.39) | copy-start | bytes 6291460
  124.3 1.8 copy-start.18
  124.3 2.5 copy-start.20
  138.9 3.2 copy-start.14
  316.7 1.8 copy-start
  318.5 14.3 %copy-start.15 = (bf16[128,2048]{1,0:T(8,128)(2,1)S(1)}, bf16[128,2048]{1,0:T(8,128)(2,1)}, u32[]{:S(2)}) copy-start(bf16[128,2048]{1,0:T(8,128)(2,1)} %get-tuple-element.57) | copy-start | bytes 1572868
  318.5 17.3 %copy-start.17 = (f32[8,512]{1,0:T(8,128)S(1)}, f32[8,512]{1,0:T(8,128)}, u32[]{:S(2)}) copy-start(f32[8,512]{1,0:T(8,128)} %get-tuple-element.66) | copy-start | bytes 49156
  332.8 3.6 %copy-start.16 = (bf16[128,2048]{1,0:T(8,128)(2,1)S(1)}, bf16[128,2048]{1,0:T(8,128)(2,1)}, u32[]{:S(2)}) copy-start(bf16[128,2048]{1,0:T(8,128)(2,1)} %get-tuple-element.56) | copy-start | bytes 1572868

commit v6 on v5

--- a/solution.py
+++ b/solution.py
@@ -2,6 +2,7 @@
 
 import jax
 import jax.numpy as jnp
+import numpy as np
 from jax import lax
 from jax.experimental import pallas as pl
 from jax.experimental.pallas import tpu as pltpu
@@ -17,10 +18,11 @@
 OWN = 64
 ROWS = 512
 QB = 256
+VMEM_BYTES = 63 * 2**20
 F32 = jnp.float32
 BF16 = jnp.bfloat16
 MESH_ID = pl.DeviceIdType.MESH
-ANY = pl.BlockSpec(memory_space=pl.ANY)
+HBM = pl.BlockSpec(memory_space=pltpu.HBM)
 VMEM = pl.BlockSpec(memory_space=pltpu.VMEM)
 
 
@@ -66,27 +68,51 @@
 XY_PEERS = [functools.partial(xy_peer, dx, dy) for dx, dy in XY_ALL]
 
 
+class Remote:
+    def __init__(self, engine, index, copy):
+        self.engine, self.index, self.copy = engine, index, copy
+
+    def wait_recv(self):
+        self.copy.wait_recv()
+
+    def wait_send(self):
+        self.copy.wait_send()
+        self.engine.free_send.append(self.index)
+
+    def wait(self):
+        self.wait_recv()
+        self.wait_send()
+
+
+class Local:
+    def __init__(self, engine, index, copy):
+        self.engine, self.index, self.copy = engine, index, copy
+
+    def wait(self):
+        self.copy.wait()
+        self.engine.free_local.append(self.index)
+
+
 class Engine:
     def __init__(self, send_sem, recv_sem, local_sem):
-        self.sems = (send_sem, recv_sem, local_sem)
-        self.remote = 0
-        self.locals = 0
+        self.send_sem, self.recv_sem, self.local_sem = send_sem, recv_sem, local_sem
+        self.free_send = list(range(send_sem.shape[0]))[::-1]
+        self.free_recv = list(range(recv_sem.shape[0]))[::-1]
+        self.free_local = list(range(local_sem.shape[0]))[::-1]
 
     def send(self, src, dst, device):
-        i = self.remote
-        self.remote += 1
+        i, k = self.free_send.pop(), self.free_recv.pop()
         copy = pltpu.make_async_remote_copy(
-            src, dst, self.sems[0].at[i], self.sems[1].at[i], device_id=device, device_id_type=MESH_ID
+            src, dst, self.send_sem.at[i], self.recv_sem.at[k], device_id=device, device_id_type=MESH_ID
         )
         copy.start()
-        return copy
+        return Remote(self, i, copy)
 
     def local(self, src, dst):
-        i = self.locals
-        self.locals += 1
-        copy = pltpu.make_async_copy(src, dst, self.sems[2].at[i])
+        i = self.free_local.pop()
+        copy = pltpu.make_async_copy(src, dst, self.local_sem.at[i])
         copy.start()
-        return copy
+        return Local(self, i, copy)
 
 
 def greet(peers):
@@ -96,12 +122,8 @@
     pl.semaphore_wait(barrier, len(peers))
 
 
-def semaphores(n_remote, n_local):
-    return [
-        pltpu.SemaphoreType.DMA((n_remote,)),
-        pltpu.SemaphoreType.DMA((n_remote,)),
-        pltpu.SemaphoreType.DMA((n_local,)),
-    ]
+def semaphores(n_send, n_recv, n_local):
+    return [pltpu.SemaphoreType.DMA((n,)) for n in (n_send, n_recv, n_local)]
 
 
 def spread(values):
@@ -221,40 +243,19 @@
     lax.fori_loop(0, rows // 16, step, 0)
 
 
-def scatter_tokens(engine, src, dst, own, other, arrived):
-    z, core = lax.axis_index("z"), lax.axis_index("core")
-    pairs = []
-    for i in range(4):
-        base = lax.rem(z + 1 + i, 4) * 2
-        there = engine.send(src.at[rows_at(base + 1 - core, OWN)], other.at[i], sibling())
-        here = engine.local(src.at[rows_at(base + core, OWN)], own.at[i])
-        pairs.append((there, here))
-    yield
-    sent = []
-    for i in range(3):
-        pairs[i][0].wait_recv()
-        pairs[i][1].wait()
-        own[i] = (own[i].astype(F32) + other[i].astype(F32)).astype(BF16)
-        sent.append(engine.send(own.at[i], arrived.at[i], z_peer(i + 1)))
-    yield
-    pairs[3][0].wait_recv()
-    pairs[3][1].wait()
-    dst[...] = own[3].astype(F32) + other[3].astype(F32)
-    for i in range(3):
-        sent[i].wait_recv()
-        dst[...] += arrived[i].astype(F32)
-    yield
-    for copy in sent:
-        copy.wait_send()
-    for there, _ in pairs:
-        there.wait_send()
-
-
-def scatter_product(engine, rows, matrix, dst, product, other, arrived):
-    z, core = lax.axis_index("z"), lax.axis_index("core")
+def exact_dot(a, b):
+    return jnp.dot(a, b, precision=lax.Precision.HIGHEST, preferred_element_type=F32)
+
+
+def by_columns(dst, value_of):
     for k in range(4):
         columns = slice(k * 512, (k + 1) * 512)
-        product[:, columns] = dot(rows[...], matrix[:, columns], (1, 0)).astype(BF16)
+        value = value_of(columns).astype(dst.dtype)
+        dst[..., columns] = value.reshape(dst.shape[:-1] + (512,))
+
+
+def scatter_tokens(engine, product, dst, other, arrived):
+    z, core = lax.axis_index("z"), lax.axis_index("core")
     to_core = []
     for i in range(4):
         give = product.at[rows_at(lax.rem(z + 1 + i, 4) * 2 + 1 - core, OWN)]
@@ -310,20 +311,21 @@
     ]
     for copy in local:
         copy.wait()
+    passed = []
     relays[0].wait_recv()
     add_up(relay_y.at[early], [relay_y.at[early], own_y.at[early]], (), half, WIDTH)
-    copies.append(engine.send(relay_y.at[early], by_y.at[0, early], y_peer(1)))
+    passed.append(engine.send(relay_y.at[early], by_y.at[0, early], y_peer(1)))
     relays[1].wait_recv()
     for q in range(2):
         add_up(relay_x, [relay_x, own_x], (q,), rest, 512)
-    copies.append(engine.send(relay_x.at[low], by_x.at[0, low], x_peer(1)))
+    passed.append(engine.send(relay_x.at[low], by_x.at[0, low], x_peer(1)))
     relays[2].wait_recv()
     add_up(relay_y.at[late], [relay_y.at[late], own_y.at[late]], (), cut - half, WIDTH)
-    copies.append(engine.send(relay_y.at[late], by_y.at[1, late], y_peer(3)))
+    passed.append(engine.send(relay_y.at[late], by_y.at[1, late], y_peer(3)))
     relays[3].wait_recv()
     for q in range(2, 4):
         add_up(relay_x, [relay_x, own_x], (q,), rest, 512)
-    copies.append(engine.send(relay_x.at[high], by_x.at[1, high], x_peer(3)))
+    passed.append(engine.send(relay_x.at[high], by_x.at[1, high], x_peer(3)))
     yield
     local = [
         engine.local(src.at[y, pl.ds(0, cut)], own_y),
@@ -331,11 +333,13 @@
     ]
     for copy in local:
         copy.wait()
-    for copy in copies:
+    for copy in copies + passed:
         copy.wait_recv()
     add_up(sum_y, [own_y, by_y.at[0], by_y.at[1]], (), cut, WIDTH)
     for q in range(4):
         add_up(sum_x, [own_x, by_x.at[0], by_x.at[1]], (q,), rest, 512)
+    for copy in passed:
+        copy.wait_send()
     yield
     for copy in relays + copies:
         copy.wait_send()
@@ -375,31 +379,32 @@
     def slot(dx, ll):
         return (lax.rem(x + dx, 4) * 2 + ll) * 2 + core
 
-    other = 1 - yl
-    first, second = pl.ds(0, 2), pl.ds(2, 2)
-    even, odd = (pl.ds(0, 1), pl.ds(1, 1)), (pl.ds(2, 1), pl.ds(3, 1))
+    other, n = 1 - yl, landing.shape[1]
+    half = first_part(n)
+    first, second = (pl.ds(0, 3),), (pl.ds(3, 1),)
+    even, even_other = ((pl.ds(0, 2),), (pl.ds(2, 1),)), ((pl.ds(0, 1),), (pl.ds(1, 2),))
+    odd = ((pl.ds(3, 1), pl.ds(0, half)), (pl.ds(3, 1), pl.ds(half, n - half)))
     partner, there = {"yl": other}, sibling()
     sent = []
 
     def send(source, target, part, device):
-        copy = engine.send(source, dst.at[target, part], device)
+        copy = engine.send(source, dst.at[(target, *part)], device)
         sent.append(copy)
         return copy
 
     def hand(index, part):
-        block = dst.at[index, part]
-        return send(block, index, part, there)
+        return send(dst.at[(index, *part)], index, part, there)
 
     def on(index, part, device):
-        return send(dst.at[index, part], index, part, device)
+        return send(dst.at[(index, *part)], index, part, device)
 
     me = slot(0, yl)
     local = engine.local(landing, dst.at[me])
     siblings = [engine.send(landing, dst.at[me], there)]
-    to_y = send(landing.at[first], me, first, partner)
-    round_b = [send(landing.at[second], me, second, x_peer(d)) for d in (1, 3)]
-    round_a = [send(landing.at[first], me, first, x_peer(d)) for d in (1, 3)]
-    over = [send(landing.at[second], me, second, partner)]
+    to_y = send(landing.at[*first], me, first, partner)
+    round_b = [send(landing.at[*second], me, second, x_peer(d)) for d in (1, 3)]
+    round_a = [send(landing.at[*first], me, first, x_peer(d)) for d in (1, 3)]
+    over = [send(landing.at[*second], me, second, partner)]
     yield
     to_y.wait_recv()
     round_c = [on(slot(0, other), first, x_peer(d)) for d in (1, 3)]
@@ -421,7 +426,7 @@
     siblings.append(hand(slot(2, yl), second))
     for k, (d, to) in enumerate(((3, 1), (1, 3))):
         round_c[k].wait_recv()
-        onward.append(on(slot(d, other), even[k], x_peer(to)))
+        onward.append(on(slot(d, other), even_other[k], x_peer(to)))
         siblings.append(hand(slot(d, other), first))
     yield
     for k in (2, 3):
@@ -493,17 +498,17 @@
     near = {"core": yh}
     stays = core == yh
     mine = dst.at[rows_at(core, OWN)]
-    i, j = engine.remote, engine.locals
-    engine.remote += 4
-    engine.locals += 1
-    send_sem, recv_sem, local_sem = engine.sems
+    sends = [engine.free_send.pop() for _ in range(2)]
+    arrivals = [engine.free_recv.pop() for _ in range(2)]
+    j = engine.free_local.pop()
+    send_sem, recv_sem, local_sem = engine.send_sem, engine.recv_sem, engine.local_sem
 
     def make(to, slot):
         return pltpu.make_async_remote_copy(
             src,
             mine,
-            send_sem.at[i + slot],
-            recv_sem.at[i + 2 + core],
+            send_sem.at[sends[slot]],
+            recv_sem.at[arrivals[0] + (arrivals[1] - arrivals[0]) * core],
             device_id=to,
             device_id_type=MESH_ID,
         )
@@ -511,7 +516,7 @@
     def arrival(half):
         part = dst.at[rows_at(half, OWN)]
         return pltpu.make_async_remote_copy(
-            part, part, send_sem.at[i], recv_sem.at[i + 2 + half], device_id=far, device_id_type=MESH_ID
+            part, part, send_sem.at[sends[0]], recv_sem.at[arrivals[0] + (arrivals[1] - arrivals[0]) * half], device_id=far, device_id_type=MESH_ID
         )
 
     make(far, 0).start()
@@ -537,6 +542,9 @@
         make(near, 1).wait_send()
         arrival(core).wait_recv()
         arrival(1 - core).wait_recv()
+
+    engine.free_send.extend(sends)
+    engine.free_local.append(j)
 
 
 def dot(a, b, dims):
@@ -646,27 +654,31 @@
 FORWARD_PEERS = XY_PEERS + Z_PEERS + [sibling]
 FORWARD_PEERS += [functools.partial(small_peer, dz, 1) for dz in (1, 2, 3)]
 
+FORWARD_KEPT = [
+    ("m_qkv", (4, 192, WIDTH), BF16),
+    ("m_out", (4, 64, WIDTH), BF16),
+    ("x_own", (OWN, WIDTH), BF16),
+    ("dy_own", (OWN, WIDTH), BF16),
+    ("middle", (OWN, WIDTH), F32),
+    ("norms", (8, WIDTH), F32),
+    ("h1", (ROWS, WIDTH), BF16),
+    ("o_t", (4 * HEAD, ROWS), BF16),
+    ("kept", (3 * HEAD, SEQ), BF16),
+    ("wide", (HEAD, SEQ), F32),
+    ("lse", (1, SEQ), F32),
+    ("seg_row", (1, SEQ), F32),
+]
 FORWARD_OUTS = [
-    ("m_qkv", (4, 192, WIDTH), BF16, VMEM),
-    ("m_out", (4, 64, WIDTH), BF16, VMEM),
-    ("m_down", (4, 176, WIDTH), BF16, ANY),
-    ("m_gate", (4, 176, WIDTH), BF16, ANY),
-    ("m_up", (4, 176, WIDTH), BF16, ANY),
-    ("x_own", (OWN, WIDTH), BF16, VMEM),
-    ("dy_own", (OWN, WIDTH), BF16, VMEM),
-    ("middle", (OWN, WIDTH), F32, VMEM),
-    ("norms", (8, WIDTH), F32, VMEM),
-    ("h1", (ROWS, WIDTH), BF16, VMEM),
-    ("h2", (ROWS, WIDTH), BF16, VMEM),
-    ("dy", (ROWS, WIDTH), BF16, ANY),
-    ("o_t", (4 * HEAD, ROWS), BF16, VMEM),
-    ("kept", (3 * HEAD, SEQ), BF16, VMEM),
-    ("wide", (HEAD, SEQ), F32, VMEM),
-    ("lse", (1, SEQ), F32, VMEM),
-    ("seg_row", (1, SEQ), F32, VMEM),
-    ("seg_col", (SEQ, 1), F32, VMEM),
+    ("m_down", (4, 176, WIDTH), BF16),
+    ("m_gate", (4, 176, WIDTH), BF16),
+    ("m_up", (4, 176, WIDTH), BF16),
+    ("h2", (ROWS, WIDTH), BF16),
+    ("dy", (ROWS, WIDTH), BF16),
 ]
-FORWARD_SCRATCH = [
+FORWARD_OUTS += [("to_" + name, shape, dtype) for name, shape, dtype in FORWARD_KEPT]
+FORWARD_SCRATCH = FORWARD_KEPT + [
+    ("seg_col", (SEQ, 1), F32),
+    ("packed", (16, 640), BF16),
     ("small", (4, 2, 16, 640), BF16),
     ("near_x", (OWN, WIDTH), BF16),
     ("near_dy", (OWN, WIDTH), BF16),
@@ -696,16 +708,19 @@
 ]
 
 
-FIRST_PARTS = ("sum_y_", "sum_x_", "by_y_", "by_x_", "relay_y_", "relay_x_")
-
-
 class Refs:
     pass
 
 
+def column_of(row):
+    blocks = jnp.concatenate([row[:, k * 128 : (k + 1) * 128] for k in range(16)], axis=0).T
+    return jnp.concatenate([blocks[:, k : k + 1] for k in range(16)], axis=0)
+
+
 def forward_kernel(*refs):
     r = Refs()
-    names = ["tokens", "cotangent", "packed", "w_qkv", "w_out", "w_down", "w_gate_up", "cos", "sin"]
+    names = ["tokens", "cotangent", "gains", "shifts", "biases", "segments"]
+    names += ["w_qkv", "w_out", "w_down", "w_gate_up", "cos", "sin"]
     names += [o[0] for o in FORWARD_OUTS] + [o[0] for o in FORWARD_SCRATCH]
     for name, ref in zip(names, refs):
         setattr(r, name, ref)
@@ -717,6 +732,15 @@
     load_gu = engine.local(r.w_gate_up.at[rows_at(x, 128)], r.held_gu)
     load_x = engine.local(r.tokens.at[rows_at(core, OWN)], r.near_x)
     load_dy = engine.local(r.cotangent.at[rows_at(core, OWN)], r.near_dy)
+    marks = r.segments[...].astype(F32)
+    rows = [r.gains[...].astype(F32), r.shifts[...].astype(F32)]
+    rows += [marks[:, k * 512 : (k + 1) * 512] for k in range(4)] + [jnp.zeros((8, 512), F32)]
+    r.packed[:, :512] = jnp.concatenate(rows, axis=0).astype(BF16)
+    unit = (
+        lax.broadcasted_iota(jnp.int32, (16, 16), 0) == lax.broadcasted_iota(jnp.int32, (16, 16), 1)
+    ).astype(BF16)
+    columns = [dot(r.biases[part], unit, (0, 0)) for part in range(3)] + [jnp.zeros((16, 80), F32)]
+    r.packed[:, 512:] = jnp.concatenate(columns, axis=1).astype(BF16)
     small_here = engine.local(r.packed, r.small.at[z, yh])
 
     def rows_of(n):
@@ -731,6 +755,12 @@
         for zz in range(4):
             r.cut_qkv[zz, part * HEAD : (part + 1) * HEAD] = r.turned[rows_of(HEAD)(zz), :].astype(BF16)
     greet(FORWARD_PEERS)
+    stores = []
+
+    def store(*names):
+        for name in names:
+            stores.append(engine.local(getattr(r, name), getattr(r, "to_" + name)))
+
     pieces_qkv = send_pieces(engine, lambda zz: r.cut_qkv.at[zz], slots_of(r.p_qkv))
     swap_x = engine.send(r.tokens.at[rows_at(1 - core, OWN)], r.far_x, sibling())
     smalls = [engine.send(r.packed, r.small.at[z, yh], small_peer(dz, dh)) for dz, dh in SMALL_ALL]
@@ -770,13 +800,11 @@
         table = jnp.concatenate([r.small[zz, h, :, 512:].astype(F32) for zz in range(4)], axis=0)
         for j in range(2):
             for part in range(3):
-                picked = jnp.where(lane_at == (z * 2 + core) * 6 + j * 3 + part, table, 0.0)
+                picked = jnp.where(lane_at == part * 16 + (z * 2 + core) * 2 + j, table, 0.0)
                 r.bias[h * 2 + j, part * HEAD : (part + 1) * HEAD] = jnp.sum(picked, axis=1, keepdims=True)
     marks = r.small[x, 0, :, :512].astype(F32)
-    marks = [marks[4 + i : 5 + i, k * 128 : (k + 1) * 128] for i in range(4) for k in range(4)]
-    r.seg_row[...] = jnp.concatenate(marks, axis=1)
-    marks = jnp.concatenate(marks, axis=0).T
-    r.seg_col[...] = jnp.concatenate([marks[:, k : k + 1] for k in range(16)], axis=0)
+    r.seg_row[...] = jnp.concatenate([marks[4 + i : 5 + i] for i in range(4)], axis=1)
+    r.seg_col[...] = column_of(r.seg_row[...])
 
     next(weight_qkv)
     next(tokens_h1)
@@ -793,13 +821,11 @@
         next(thread)
         return thread
 
-    weight_out = start_weight(pieces_out, r.p_out, r.m_out)
     load_dy.wait()
     swap_dy.wait_recv()
     dy_rows = jnp.where(stays, r.near_dy[...].astype(F32), r.far_dy[...].astype(F32))
     r.dy_own[...] = spread(dy_rows).astype(BF16)
     finish(tokens_h1)
-    next(weight_out)
     finish(weight_qkv)
 
     r.qkv_t[...] = (
@@ -807,17 +833,20 @@
     ).astype(BF16)
     to_items = send_items(engine, r.qkv_t, r.item, 3 * HEAD)
     tokens_dy = gather_tokens(engine, r.dy_own, r.dy)
+    weight_out = start_weight(pieces_out, r.p_out, r.m_out)
     next(tokens_dy)
     weight_down = start_weight(pieces_down, r.p_down, r.m_down)
-    weight_gate = start_weight(pieces_gate, r.p_gate, r.m_gate)
-    weight_up = start_weight(pieces_up, r.p_up, r.m_up)
     to_items[-1].wait()
     for copy in to_items[:-1]:
         copy.wait_recv()
     next(weight_out)
+    weight_gate = start_weight(pieces_gate, r.p_gate, r.m_gate)
+    store("m_qkv", "h1", "x_own", "dy_own", "norms", "seg_row")
     attend(r.item, r.seg_row, r.seg_col, r.cos, r.sin, r.out, r.wide, r.lse, r.kept)
+    next(weight_out)
     back = return_items(engine, r.out, r.o_t, HEAD)
     next(weight_down)
+    weight_up = start_weight(pieces_up, r.p_up, r.m_up)
     next(tokens_dy)
     finish(weight_out)
     back[-1].wait()
@@ -826,7 +855,8 @@
 
     r.o_rows[...] = r.o_t[...].astype(F32).T.astype(BF16)
     matrix = r.m_out[...].reshape(4 * HEAD, WIDTH)
-    out = scatter_product(engine, r.o_rows, matrix, r.middle, r.product, r.other, r.arrived)
+    by_columns(r.product, lambda columns: dot(r.o_rows[...], matrix[:, columns], (1, 0)))
+    out = scatter_tokens(engine, r.product, r.middle, r.other, r.arrived)
     next(out)
     next(out)
     next(weight_gate)
@@ -836,10 +866,13 @@
     next(out)
     r.middle[...] += x_rows
 
+    store("kept", "wide", "lse", "o_t", "m_out")
+
     h2_full, _, _ = layer_norm(r.middle[...], r.norms[1:2], r.norms[3:4])
     r.h2_own[...] = h2_full.astype(BF16)
     tokens_h2 = gather_tokens(engine, r.h2_own, r.h2)
     next(tokens_h2)
+    store("middle")
     next(weight_up)
     next(tokens_h2)
     finish(weight_down)
@@ -848,6 +881,8 @@
     finish(weight_up)
     finish(tokens_h2)
     finish(out)
+    for copy in stores:
+        copy.wait()
     sent = smalls + to_items[:-1] + back[:-1] + [swap_x, swap_dy]
     for pieces in (pieces_qkv, pieces_out, pieces_gate, pieces_down, pieces_up):
         sent += pieces[1:]
@@ -855,21 +890,21 @@
         copy.wait_send()
 
 
-def forward(tokens, cotangent, packed, w_qkv, w_out, w_down, w_gate_up, cosine, sine):
+def forward(tokens, cotangent, gains, shifts, biases, segments, w_qkv, w_out, w_down, w_gate_up, cosine, sine):
     values = pl.pallas_call(
         forward_kernel,
         out_shape=[jax.ShapeDtypeStruct(o[1], o[2]) for o in FORWARD_OUTS],
-        in_specs=[ANY] * 7 + [VMEM] * 2,
-        out_specs=[o[3] for o in FORWARD_OUTS],
-        scratch_shapes=[pltpu.VMEM(shape, dtype) for _, shape, dtype in FORWARD_SCRATCH] + semaphores(160, 24),
+        in_specs=[HBM] * 2 + [VMEM] * 4 + [HBM] * 4 + [VMEM] * 2,
+        out_specs=[HBM] * len(FORWARD_OUTS),
+        scratch_shapes=[pltpu.VMEM(shape, dtype) for _, shape, dtype in FORWARD_SCRATCH] + semaphores(117, 152, 20),
         compiler_params=pltpu.CompilerParams(
-            collective_id=1, has_side_effects=True, vmem_limit_bytes=50 * 2**20
+            collective_id=1, has_side_effects=True, vmem_limit_bytes=VMEM_BYTES
         ),
         name="forward",
-    )(tokens, cotangent, packed, w_qkv, w_out, w_down, w_gate_up, cosine, sine)
+    )(tokens, cotangent, gains, shifts, biases, segments, w_qkv, w_out, w_down, w_gate_up, cosine, sine)
     result = Refs()
     for (name, *_), value in zip(FORWARD_OUTS, values):
-        setattr(result, name, value)
+        setattr(result, name.removeprefix("to_"), value)
     return result
 
 
@@ -882,34 +917,52 @@
 
 BACKWARD_PEERS = XY_PEERS + Z_PEERS + [sibling, functools.partial(back_peer, 1, 1)]
 BACKWARD_PEERS += [functools.partial(group_peer, dz, 1) for dz in (1, 2, 3)]
-BACKWARD_FAR = ["back_part", "mlp_part", "g_gate", "g_up", "g_down", "h1", "m_qkv"]
-BACKWARD_NEAR = ["middle", "x_own", "dy_own", "norms", "m_out", "o_t", "kept", "wide", "lse"]
-BACKWARD_NEAR += ["seg_row", "seg_col", "cos", "sin"]
+BACKWARD_FAR = ["m_gate", "m_up", "m_down", "h2", "dy", "h1", "m_qkv"]
+BACKWARD_NEAR = [
+    ("middle", (OWN, WIDTH), F32),
+    ("norms", (8, WIDTH), F32),
+    ("dy_own", (OWN, WIDTH), BF16),
+    ("m_out", (4, 64, WIDTH), BF16),
+    ("kept", (3 * HEAD, SEQ), BF16),
+    ("wide", (HEAD, SEQ), F32),
+    ("lse", (1, SEQ), F32),
+    ("seg_row", (1, SEQ), F32),
+    ("cos", (8, SEQ), F32),
+    ("sin", (8, SEQ), F32),
+    ("o_t", (4 * HEAD, ROWS), BF16),
+    ("x_own", (OWN, WIDTH), BF16),
+]
 BACKWARD_OUTS = [
-    ("layer_out", (2 * OWN, WIDTH), BF16, ANY),
-    ("grad_tokens", (2 * OWN, WIDTH), BF16, ANY),
-    ("gd_all", (16, 4, 352, 128), BF16, ANY),
-    ("up_all", (16, 4, 176, 128), BF16, ANY),
-    ("attn_all", (16, 4, 256, 128), BF16, ANY),
+    ("layer_out", (2 * OWN, WIDTH), BF16, HBM),
+    ("grad_tokens", (2 * OWN, WIDTH), BF16, HBM),
+    ("gd_all", (16, 4, 352, 128), BF16, HBM),
+    ("up_all", (16, 4, 176, 128), BF16, HBM),
+    ("attn_all", (16, 4, 256, 128), BF16, HBM),
     ("norm_sum", (8, 512), F32, VMEM),
-    ("bias_all", (8, 8, 768), F32, VMEM),
+    ("grad_bias", (3, 16, 16), F32, VMEM),
 ]
-BACKWARD_SCRATCH = [
-    ("v_h1", (ROWS, WIDTH), BF16),
-    ("v_qkv", (4, 192, WIDTH), BF16),
+BACKWARD_SCRATCH = BACKWARD_NEAR + [
+    ("seg_col", (SEQ, 1), F32),
+    ("gate_qkv", (4, 192, WIDTH), BF16),
+    ("up_attn", (4, 256, WIDTH), BF16),
+    ("down", (4, 176, WIDTH), BF16),
+    ("normed", (ROWS, WIDTH), BF16),
+    ("dy_all", (ROWS, WIDTH), BF16),
+    ("product", (ROWS, WIDTH), BF16),
+    ("product_mlp", (ROWS, WIDTH), BF16),
+    ("act", (704, ROWS), BF16),
+    ("d_gate", (704, ROWS), BF16),
+    ("d_up", (704, ROWS), BF16),
     ("dz_own", (OWN, WIDTH), BF16),
     ("dz", (ROWS, WIDTH), BF16),
     ("d_middle", (OWN, WIDTH), F32),
     ("summed", (OWN, WIDTH), F32),
     ("out_own", (OWN, WIDTH), BF16),
     ("grad_own", (OWN, WIDTH), BF16),
-    ("own_dh2", (4, OWN, WIDTH), BF16),
     ("other_dh2", (4, OWN, WIDTH), BF16),
     ("arrived_dh2", (3, OWN, WIDTH), BF16),
-    ("own_mlp", (4, OWN, WIDTH), BF16),
     ("other_mlp", (4, OWN, WIDTH), BF16),
     ("arrived_mlp", (3, OWN, WIDTH), BF16),
-    ("product", (ROWS, WIDTH), BF16),
     ("other_dh1", (4, OWN, WIDTH), BF16),
     ("arrived_dh1", (3, OWN, WIDTH), BF16),
     ("own_y", (128, WIDTH), BF16),
@@ -920,12 +973,12 @@
     ("d_kv", (SEQ, 2 * HEAD), F32),
     ("d_qkv", (12 * HEAD, ROWS), BF16),
     ("d_rows", (ROWS, 12 * HEAD), BF16),
-    ("g_attn", (4, 256, WIDTH), BF16),
     ("landing_gd", (4, 352, 128), BF16),
     ("landing_up", (4, 176, 128), BF16),
     ("landing_attn", (4, 256, 128), BF16),
     ("small_norms", (8, WIDTH), F32),
     ("small_bias", (8, 768), F32),
+    ("bias_all", (8, 8, 768), F32),
     ("by_group", (8, 8, 512), F32),
     ("small_x", (4, 8, 1280), F32),
     ("small_y", (4, 8, 1280), F32),
@@ -935,32 +988,57 @@
     BACKWARD_SCRATCH += [
         ("sum_y_" + _name, (_cut, WIDTH), BF16),
         ("sum_x_" + _name, (4, _n - _cut, 512), BF16),
-        ("by_y_" + _name, (2, _cut, WIDTH), BF16),
-        ("by_x_" + _name, (2, 4, _n - _cut, 512), BF16),
-        ("relay_y_" + _name, (_cut, WIDTH), BF16),
-        ("relay_x_" + _name, (4, _n - _cut, 512), BF16),
         ("rest_x_" + _name, (3, _cut, 512), BF16),
         ("rest_y_" + _name, (3, _n - _cut, 512), BF16),
         ("rest_own_" + _name, (_n, 512), BF16),
         ("rest_total_" + _name, (_n, 512), BF16),
     ]
+for _name, _cut, _rest in (("a", 96, 80), ("b", 128, 128)):
+    BACKWARD_SCRATCH += [
+        ("by_y_" + _name, (2, _cut, WIDTH), BF16),
+        ("by_x_" + _name, (2, 4, _rest, 512), BF16),
+        ("relay_y_" + _name, (_cut, WIDTH), BF16),
+        ("relay_x_" + _name, (4, _rest, 512), BF16),
+    ]
 
 
 def backward_kernel(*refs):
     r = Refs()
-    names = BACKWARD_FAR + BACKWARD_NEAR + [o[0] for o in BACKWARD_OUTS] + [o[0] for o in BACKWARD_SCRATCH]
+    names = BACKWARD_FAR + ["in_" + n[0] for n in BACKWARD_NEAR] + [o[0] for o in BACKWARD_OUTS] + [o[0] for o in BACKWARD_SCRATCH]
     for name, ref in zip(names, refs):
         setattr(r, name, ref)
     engine = Engine(*refs[len(names) :])
     z, x, yl, core, yh = place()
     y = yh * 2 + yl
-    load_h1 = engine.local(r.h1, r.v_h1)
-    load_qkv = engine.local(r.m_qkv, r.v_qkv)
+    m_gate, m_up = r.gate_qkv.at[:, pl.ds(0, 176)], r.up_attn.at[:, pl.ds(0, 176)]
+    loads = [
+        engine.local(source, target)
+        for source, target in (
+            (r.m_gate, m_gate),
+            (r.h2, r.normed),
+            (r.m_up, m_up),
+            (r.m_down, r.down),
+            (r.dy, r.dy_all),
+        )
+    ]
+    near = [engine.local(getattr(r, "in_" + n[0]), getattr(r, n[0])) for n in BACKWARD_NEAR]
     greet(BACKWARD_PEERS)
 
-    def first_of(name, grad):
-        parts = [getattr(r, part + name) for part in FIRST_PARTS]
-        thread = sum_first(engine, grad, *parts, r.own_y, r.own_x)
+    def first_of(name, grad, places):
+        cut, rest = getattr(r, "sum_y_" + name).shape[0], getattr(r, "sum_x_" + name).shape[1]
+        head, tail = pl.ds(0, cut), pl.ds(0, rest)
+        thread = sum_first(
+            engine,
+            grad,
+            getattr(r, "sum_y_" + name),
+            getattr(r, "sum_x_" + name),
+            getattr(r, "by_y_" + places).at[:, head],
+            getattr(r, "by_x_" + places).at[:, :, tail],
+            getattr(r, "relay_y_" + places).at[head],
+            getattr(r, "relay_x_" + places).at[:, tail],
+            r.own_y,
+            r.own_x,
+        )
         next(thread)
         return thread
 
@@ -973,13 +1051,47 @@
     def part_of(landing, first):
         return lambda zz: landing.at[zz, pl.ds(first, 176)]
 
-    dh2 = scatter_tokens(engine, r.back_part, r.summed, r.own_dh2, r.other_dh2, r.arrived_dh2)
+    for load in loads:
+        load.wait()
+    for half in range(2):
+        two, rows = slice(2 * half, 2 * half + 2), slice(352 * half, 352 * half + 352)
+        gate = dot(r.gate_qkv[two, :176].reshape(352, WIDTH), r.normed[...], (1, 1))
+        up = dot(r.up_attn[two, :176].reshape(352, WIDTH), r.normed[...], (1, 1))
+        d_act = dot(r.down[two].reshape(352, WIDTH), r.dy_all[...], (1, 1))
+        sigmoid = jax.nn.sigmoid(gate)
+        silu = gate * sigmoid
+        r.act[rows] = (silu * up).astype(BF16)
+        r.d_gate[rows] = (d_act * up * sigmoid * (1.0 + gate * (1.0 - sigmoid))).astype(BF16)
+        r.d_up[rows] = (d_act * silu).astype(BF16)
+
+    def turned(ref):
+        return ref[...].astype(F32).T.astype(BF16)
+
+    def columns_of(ref, columns):
+        return ref[:, :176, columns].reshape(704, 512)
+
+    gate_rows, up_rows = turned(r.d_gate), turned(r.d_up)
+    by_columns(
+        r.product,
+        lambda columns: dot(gate_rows, columns_of(r.gate_qkv, columns), (1, 0))
+        + dot(up_rows, columns_of(r.up_attn, columns), (1, 0)),
+    )
+    dh2 = scatter_tokens(engine, r.product, r.summed, r.other_dh2, r.arrived_dh2)
     next(dh2)
-    gate = first_of("gate", r.g_gate)
-    down = first_of("down", r.g_down)
+    by_columns(m_gate, lambda columns: dot(r.d_gate[...], r.normed[:, columns], (1, 0)))
+    gate = first_of("gate", m_gate, "a")
     next(dh2)
-    mlp = scatter_tokens(engine, r.mlp_part, r.d_middle, r.own_mlp, r.other_mlp, r.arrived_mlp)
+    act_rows = turned(r.act)
+    by_columns(r.product_mlp, lambda columns: dot(act_rows, columns_of(r.down, columns), (1, 0)))
+    by_columns(r.down, lambda columns: dot(r.act[...], r.dy_all[:, columns], (1, 0)))
+    down = first_of("down", r.down, "b")
+    by_columns(m_up, lambda columns: dot(r.d_up[...], r.normed[:, columns], (1, 0)))
+    load_h1 = engine.local(r.h1, r.normed)
+    mlp = scatter_tokens(engine, r.product_mlp, r.d_middle, r.other_mlp, r.arrived_mlp)
     next(mlp)
+    for load in near:
+        load.wait()
+    r.seg_col[...] = column_of(r.seg_row[...])
     _, normed_b, rstd_b = layer_norm(r.middle[...], r.norms[1:2], r.norms[3:4])
     next(gate)
     next(down)
@@ -997,27 +1109,32 @@
     rest_down = rest_of("down", part_of(r.landing_gd, 176))
     next(tokens_dz)
     finish(tokens_dz)
-    next(mlp)
 
     r.d_o[...] = dot(r.m_out[...].reshape(4 * HEAD, WIDTH), r.dz[...], (1, 1)).astype(BF16)
     to_items = send_items(engine, r.d_o, r.item, HEAD)
-    up = first_of("up", r.g_up)
-    g_out = dot(r.o_t[...], r.dz[...], (1, 0)).astype(BF16)
-    for q in range(4):
-        r.g_attn[q, 192:] = g_out[q * HEAD : (q + 1) * HEAD]
     next(rest_gate)
+    up = first_of("up", m_up, "a")
     next(rest_down)
+    next(mlp)
+    finish(gate)
+    load_qkv = engine.local(r.m_qkv, r.gate_qkv)
     to_items[-1].wait()
     for copy in to_items[:-1]:
         copy.wait_recv()
+    next(rest_gate)
+    next(rest_down)
+    gather_gd = gather_ctx(engine, r.landing_gd, r.gd_all)
+    next(gather_gd)
+    finish(down)
+    finish(rest_gate)
+    finish(rest_down)
     attend_back(
         r.kept, r.item, r.wide, r.lse, r.seg_row, r.seg_col, r.cos, r.sin, r.item_out, r.d_kv
     )
     back = return_items(engine, r.item_out, r.d_qkv, 3 * HEAD)
+    for copy in to_items[:-1]:
+        copy.wait_send()
     next(up)
-    next(rest_gate)
-    next(rest_down)
-    gather_gd = gather_ctx(engine, r.landing_gd, r.gd_all)
     next(gather_gd)
     next(mlp)
     r.out_own[...] = spread(r.middle[...] + r.d_middle[...]).astype(BF16)
@@ -1029,22 +1146,28 @@
     back[-1].wait()
     for copy in back[:-1]:
         copy.wait_recv()
+    finish(mlp)
 
     r.d_rows[...] = r.d_qkv[...].astype(F32).T.astype(BF16)
-    matrix = r.v_qkv[...].reshape(12 * HEAD, WIDTH)
-    dh1 = scatter_product(engine, r.d_rows, matrix, r.summed, r.product, r.other_dh1, r.arrived_dh1)
+    matrix = r.gate_qkv[...].reshape(12 * HEAD, WIDTH)
+    finish(dh2)
+    by_columns(r.product, lambda columns: dot(r.d_rows[...], matrix[:, columns], (1, 0)))
+    dh1 = scatter_tokens(engine, r.product, r.summed, r.other_dh1, r.arrived_dh1)
     next(dh1)
-    g_qkv = dot(r.d_qkv[...], r.v_h1[...], (1, 0)).astype(BF16)
-    for q in range(4):
-        r.g_attn[q, :192] = g_qkv[q * 3 * HEAD : (q + 1) * 3 * HEAD]
-    attn = first_of("attn", r.g_attn)
+    next(up)
+    rest_up = rest_of("up", part_of(r.landing_up, 0))
+    finish(up)
+    by_columns(
+        r.up_attn.at[:, pl.ds(0, 192)], lambda columns: dot(r.d_qkv[...], r.normed[:, columns], (1, 0))
+    )
+    by_columns(r.up_attn.at[:, pl.ds(192, 64)], lambda columns: dot(r.o_t[...], r.dz[:, columns], (1, 0)))
+    attn = first_of("attn", r.up_attn, "b")
     next(dh1)
     r.small_bias[...] = dot(jnp.ones((8, ROWS), BF16), r.d_qkv[...], (1, 1))
     _, normed_a, rstd_a = layer_norm(r.x_own[...].astype(F32), r.norms[0:1], r.norms[2:3])
-    next(up)
-    rest_up = rest_of("up", part_of(r.landing_up, 0))
     next(gather_gd)
     next(attn)
+    next(rest_up)
     next(dh1)
     back_a, gain_a, shift_a = norm_back(r.summed[...], normed_a, rstd_a, r.norms[0:1])
     r.grad_own[...] = spread(r.d_middle[...] + back_a).astype(BF16)
@@ -1059,49 +1182,83 @@
     )
     next(small)
     next(rest_up)
+    finish(rest_up)
+    gather_up = gather_ctx(engine, r.landing_up, r.up_all)
+    next(gather_up)
+    next(gather_gd)
+    next(small)
     next(attn)
     rest_attn = rest_of("attn", lambda zz: r.landing_attn.at[zz])
-    next(rest_up)
-    gather_up = gather_ctx(engine, r.landing_up, r.up_all)
     next(gather_up)
     next(small)
-    next(gather_gd)
     next(rest_attn)
-    next(small)
+    next(gather_up)
     next(rest_attn)
     gather_attn = gather_ctx(engine, r.landing_attn, r.attn_all)
     next(gather_attn)
-    next(gather_up)
     next(small)
-    next(gather_gd)
-    next(gather_attn)
     next(gather_up)
     next(gather_attn)
-    next(gather_up)
+    finish(small)
+    table = jnp.concatenate([r.bias_all[k, 0:1] for k in range(8)], axis=0)
+    from_at = lax.broadcasted_iota(jnp.int32, (768, 16), 0)
+    to_at = lax.broadcasted_iota(jnp.int32, (768, 16), 1)
+    row_at = lax.broadcasted_iota(jnp.int32, (16, 8), 0)
+    group_at = lax.broadcasted_iota(jnp.int32, (16, 8), 1)
+    for part in range(3):
+        total = jnp.zeros((16, 16), F32)
+        for j in range(2):
+            chosen = (from_at == to_at + ((yh * 2 + j) * 3 + part) * HEAD + z * 16).astype(F32)
+            spread_rows = (row_at == group_at * 2 + j).astype(F32)
+            total += exact_dot(spread_rows, exact_dot(table, chosen))
+        r.grad_bias[part] = total
+    next(gather_attn)
+    finish(gather_gd)
+    finish(gather_up)
     next(gather_attn)
     threads = (dh2, mlp, gate, down, up, attn, rest_gate, rest_down, rest_up, rest_attn)
     for thread in threads + (hand_out, dh1, hand_grad, small, gather_gd, gather_up, gather_attn):
         finish(thread)
-    for copy in to_items[:-1] + back[:-1]:
+    for copy in back[:-1]:
         copy.wait_send()
 
 
 def backward(values):
-    given = [values[name] for name in BACKWARD_FAR + BACKWARD_NEAR]
+    given = [values[name] for name in BACKWARD_FAR + [n[0] for n in BACKWARD_NEAR]]
     return pl.pallas_call(
         backward_kernel,
         out_shape=[jax.ShapeDtypeStruct(o[1], o[2]) for o in BACKWARD_OUTS],
-        in_specs=[ANY] * len(BACKWARD_FAR) + [VMEM] * len(BACKWARD_NEAR),
+        in_specs=[HBM] * len(given),
         out_specs=[o[3] for o in BACKWARD_OUTS],
-        scratch_shapes=[pltpu.VMEM(shape, dtype) for _, shape, dtype in BACKWARD_SCRATCH] + semaphores(320, 64),
+        scratch_shapes=[pltpu.VMEM(shape, dtype) for _, shape, dtype in BACKWARD_SCRATCH] + semaphores(157, 262, 20),
         compiler_params=pltpu.CompilerParams(
-            collective_id=2, has_side_effects=True, vmem_limit_bytes=58 * 2**20
+            collective_id=2, has_side_effects=True, vmem_limit_bytes=VMEM_BYTES
         ),
         name="backward",
     )(*given)
 
 
-def assemble_kernel(gd_ref, up_ref, attn_ref, gu_ref, down_ref, qkv_ref, out_ref, turned):
+def assemble_kernel(
+    gd_ref,
+    up_ref,
+    attn_ref,
+    layer_ref,
+    tokens_ref,
+    norms_ref,
+    gu_ref,
+    down_ref,
+    qkv_ref,
+    out_ref,
+    layer_out_ref,
+    tokens_out_ref,
+    gains_ref,
+    shifts_ref,
+    turned,
+):
+    layer_out_ref[...] = layer_ref[...]
+    tokens_out_ref[...] = tokens_ref[...].astype(F32)
+    gains_ref[...] = norms_ref[0:2]
+    shifts_ref[...] = norms_ref[2:4]
     for g in range(2):
         for zz in range(4):
             for core in range(2):
@@ -1125,7 +1282,7 @@
                 qkv_ref[part, :, column : column + 128] = block.astype(F32).T
 
 
-def assemble(gd_all, up_all, attn_all):
+def assemble(gd_all, up_all, attn_all, layer_out, grad_tokens, norm_sum):
     gd_all = gd_all.reshape(4, 4, 4, 352, 128)
     up_all = up_all.reshape(4, 4, 4, 176, 128)
     attn_all = attn_all.reshape(4, 4, 4, 256, 128)
@@ -1136,31 +1293,42 @@
             pl.BlockSpec((1, 4, 4, 352, 128), lambda i: (i, 0, 0, 0, 0)),
             pl.BlockSpec((1, 4, 4, 176, 128), lambda i: (i, 0, 0, 0, 0)),
             pl.BlockSpec((1, 4, 4, 256, 128), lambda i: (i, 0, 0, 0, 0)),
+            pl.BlockSpec((32, WIDTH), lambda i: (i, 0)),
+            pl.BlockSpec((32, WIDTH), lambda i: (i, 0)),
+            pl.BlockSpec((8, 512), lambda i: (0, 0)),
         ],
         out_specs=[
             pl.BlockSpec((128, 2, 2816), lambda i: (i, 0, 0)),
             pl.BlockSpec((2816, 128), lambda i: (0, i)),
             pl.BlockSpec((3, 128, 1024), lambda i: (0, i, 0)),
             pl.BlockSpec((1024, 128), lambda i: (0, i)),
+            pl.BlockSpec((32, WIDTH), lambda i: (i, 0)),
+            pl.BlockSpec((32, WIDTH), lambda i: (i, 0)),
+            pl.BlockSpec((2, 512), lambda i: (0, 0)),
+            pl.BlockSpec((2, 512), lambda i: (0, 0)),
         ],
         out_shape=[
             jax.ShapeDtypeStruct((512, 2, 2816), F32),
             jax.ShapeDtypeStruct((2816, 512), F32),
             jax.ShapeDtypeStruct((3, 512, 1024), F32),
             jax.ShapeDtypeStruct((1024, 512), F32),
+            jax.ShapeDtypeStruct((2 * OWN, WIDTH), BF16),
+            jax.ShapeDtypeStruct((2 * OWN, WIDTH), F32),
+            jax.ShapeDtypeStruct((2, 512), F32),
+            jax.ShapeDtypeStruct((2, 512), F32),
         ],
         scratch_shapes=[pltpu.VMEM((2816, 128), F32)],
-        compiler_params=pltpu.CompilerParams(vmem_limit_bytes=48 * 2**20),
+        compiler_params=pltpu.CompilerParams(vmem_limit_bytes=VMEM_BYTES),
         name="assemble",
-    )(gd_all, up_all, attn_all)
+    )(gd_all, up_all, attn_all, layer_out, grad_tokens, norm_sum)
 
 
 def rotation_tables():
     half = ROT // 2
-    positions = jnp.arange(SEQ).astype(F32)
-    inverse = 10000.0 ** (-(jnp.arange(half).astype(F32) * 2.0 / ROT))
-    angles = inverse[:, None] * positions[None, :]
-    return jnp.cos(angles), jnp.sin(angles)
+    positions = np.arange(SEQ, dtype=np.float32)
+    inverse = (10000.0 ** (-(np.arange(half) * 2.0 / ROT))).astype(np.float32)
+    angles = (inverse[:, None] * positions[None, :]).astype(np.float64)
+    return jnp.asarray(np.cos(angles).astype(np.float32)), jnp.asarray(np.sin(angles).astype(np.float32))
 
 
 def layer_norm(values, gain_row, shift_row):
@@ -1183,55 +1351,25 @@
 
 
 def local(tokens, segments, w_qkv, b_qkv, w_out, w_gate_up, w_down, norm_gains, norm_shifts, cotangent):
-    z, _, _, core, yh = place()
-
-    def pick(values, axis, index):
-        return lax.dynamic_index_in_dim(values, index, axis, keepdims=False)
-
-    rows = jnp.concatenate(
-        [norm_gains, norm_shifts, segments.astype(BF16).reshape(4, 512), jnp.zeros((8, 512), BF16)], axis=0
-    )
-    biases = b_qkv.reshape(3, 4, 2, 2, 16).transpose(4, 1, 2, 3, 0).reshape(16, 48)
-    packed = jnp.concatenate([rows, jnp.pad(biases, ((0, 0), (0, 80)))], axis=1)
     cosine, sine = rotation_tables()
     f = forward(
-        tokens[0], cotangent[0], packed, w_qkv.transpose(1, 0, 2), w_out, w_down, w_gate_up, cosine, sine
+        tokens[0], cotangent[0], norm_gains, norm_shifts, b_qkv, segments, w_qkv.transpose(1, 0, 2), w_out, w_down, w_gate_up, cosine, sine
     )
-    h2, dy = f.h2, f.dy
-    m_down, m_gate, m_up = (m.reshape(704, WIDTH) for m in (f.m_down, f.m_gate, f.m_up))
-
-    gate, up = dot(m_gate, h2, (1, 1)), dot(m_up, h2, (1, 1))
-    sigmoid = jax.nn.sigmoid(gate)
-    silu = gate * sigmoid
-    act = (silu * up).astype(BF16)
-    d_act = dot(m_down, dy, (1, 1))
-    d_gate = (d_act * up * sigmoid * (1.0 + gate * (1.0 - sigmoid))).astype(BF16)
-    d_up = (d_act * silu).astype(BF16)
-    mlp_part = dot(act, m_down, (0, 0)).astype(BF16)
-    back_part = (dot(d_gate, m_gate, (0, 0)) + dot(d_up, m_up, (0, 0))).astype(BF16)
-
-    def weight_grad(a, b):
-        return dot(a, b, (1, 0)).astype(BF16).reshape(4, a.shape[0] // 4, WIDTH)
-
-    g_gate, g_up, g_down = weight_grad(d_gate, h2), weight_grad(d_up, h2), weight_grad(act, dy)
-    values = dict(vars(f), cos=cosine, sin=sine, back_part=back_part, mlp_part=mlp_part)
-    values.update(g_gate=g_gate, g_up=g_up, g_down=g_down)
-    layer_out, grad_tokens, gd_all, up_all, attn_all, norm_sum, bias_all = backward(values)
-
-    bias_all = bias_all[:, 0].reshape(4, 2, 2, 2, 3, 4, 16)
-    bias_all = pick(pick(bias_all, 2, yh), 4, z)
-    grad_bias = bias_all.transpose(3, 0, 1, 2, 4).reshape(3, 16, 16)
-    out_gu, out_down, out_qkv, out_out = assemble(gd_all, up_all, attn_all)
+    values = dict(vars(f), cos=cosine, sin=sine)
+    layer_out, grad_tokens, gd_all, up_all, attn_all, norm_sum, grad_bias = backward(values)
+    out_gu, out_down, out_qkv, out_out, layer_out, grad_tokens, gains, shifts = assemble(
+        gd_all, up_all, attn_all, layer_out, grad_tokens, norm_sum
+    )
     return (
         layer_out[None],
-        grad_tokens.astype(F32)[None],
+        grad_tokens[None],
         out_qkv.transpose(1, 0, 2),
         grad_bias,
         out_out,
         out_gu,
         out_down,
-        norm_sum[:2],
-        norm_sum[2:4],
+        gains,
+        shifts,
     )
 
 

time: 340 us -> 290 us (0.85)
  matrix products: 39.6 us -> 0 us
  local copies, waits for them, and re-layouts: 8.82 us -> 0.61 us
    dot_general x9 -> x0, matrix products: 39.6 us -> none  [dot(): lax.dot_general(a, b, ((dims[:1], dims[1:]), ((), ())), preferred_element...]
    unnamed x46 -> x3, local copies, waits for them, and re-layouts: 5.52 us -> 0.61 us
    pallas_call x1, Pallas kernels: 114 us -> 109 us  [forward(): pl.pallas_call(forward_kernel, out_shape=[jax.ShapeDtypeStruct(o[1], o[2]...]
where the time goes in v6:
time: 290 us; the launch traced here: 286 us
  Pallas kernels  285 us (98%)
    pallas_call x1, Pallas kernels, backward(): pl.pallas_call(backward_kernel, out_shape=[jax.ShapeDtypeStruct(o[1], o[2...  159 us
    pallas_call x1, Pallas kernels, forward(): pl.pallas_call(forward_kernel, out_shape=[jax.ShapeDtypeStruct(o[1], o[2]...  109 us
    pallas_call x1, Pallas kernels, assemble(): pl.pallas_call(assemble_kernel, grid=(4,), in_specs=[pl.BlockSpec((1, 4,...  16.7 us

profile of v6, /device:TPU:1, one launch (start us, length us, event | category | flops | bytes accessed | tf_op | source)
XLA Modules:
  0.0 286.3 jit_solution(7519004963071241055)
XLA Ops:
  0.6 108.7 %forward.1 = (bf16[4,176,2048]{2,1,0:T(8,128)(2,1)}, bf16[4,176,2048]{2,1,0:T(8,128)(2,1)}, bf16[4,176,2048]{2,1,0:T(8,128)(2,1)}, bf16[512,2048]{1,0:T(8,128)(2...) custom-call(bf16[128,2048]{1,0:T(8,128)(2,1)} %bitcast.13, ...), custom_call_target="tpu_custom_call" | custom-call | tf_op jit(solution)/shard_map/forward/pallas_call | solution.py:894
  109.3 159.4 %backward.1 = (bf16[128,2048]{1,0:T(8,128)(2,1)}, bf16[128,2048]{1,0:T(8,128)(2,1)}, bf16[16,4,352,128]{3,2,1,0:T(8,128)(2,1)}, bf16[16,4,176,128]{3,2,1,0:T(8,1...) custom-call(bf16[4,176,2048]{2,1,0:T(8,128)(2,1)} %get-tuple-element.41.refs_0_, ...), custom_call_target="tpu_custom_call" | custom-call | tf_op jit(solution)/shard_map/backward/pallas_call | solution.py:1228
  268.7 0.0 copy-start
  268.7 16.7 %assemble.1 = (f32[512,2,2816]{2,1,0:T(2,128)}, f32[2816,512]{1,0:T(8,128)}, f32[3,512,1024]{2,1,0:T(8,128)}, f32[1024,512]{1,0:T(8,128)}, bf16[128,2048]{1,0:T(...) custom-call(bf16[4,4,4,352,128]{4,3,2,1,0:T(8,128)(2,1)} %bitcast.9, ...), custom_call_target="tpu_custom_call" | custom-call | tf_op jit(solution)/shard_map/assemble/pallas_call | solution.py:1289
  285.5 0.0 copy-done
  285.5 0.6 copy.22
Async XLA Ops:
  268.7 16.7 %copy-start = (f32[3,16,16]{2,1,0:T(8,128)S(1)}, f32[3,16,16]{2,1,0:T(8,128)}, u32[]{:S(2)}) copy-start(f32[3,16,16]{2,1,0:T(8,128)} %get-tuple-element.85) | copy-start | bytes 9220
